TPU v7x, 256 devices: a whole 4x4x8 slice. The times are simulated.
256 devices in a mesh: ctx: 64 (over y, x, z_lo, core), head: 4 (over z_hi).
Axes of the slice: x: 4, y: 4, z: 8 (z_hi: 4, z_lo: 2; z = z_hi * 2 + z_lo), core: 2. Of those that a mesh axis runs over, the one named last changes fastest.
Arguments:
- query_states: bfloat16 [32768, 2048], P('ctx', 'head'), may hold values from -8 to 8
- key_states: bfloat16 [32768, 2048], P('ctx', 'head'), may hold values from -8 to 8
- value_states: bfloat16 [32768, 2048], P('ctx', 'head'), may hold values from -6 to 6
- offsets: int32 [6, 16], replicated, may hold values from 0 to 31, as said below
- out_weight: bfloat16 [2048, 2048], P('head'), may hold values from -0.125 to 0.125
Outputs:
- layer_out: bfloat16 [32768, 2048], P('ctx', 'head')
Inputs may be any that keep to these rules, and one draw needn't show every extreme that they name: offsets[l, h] lies in 0 to 2**l - 1; at level 5 some head takes 2**5 - 1.
All inputs are finite; a program needn't handle non-finite values.
Results may differ from a plain program's by a relative error of at most 0.0053.
Values may be sent and summed in bfloat16 or wider, within the bound.
No kernel may reach another device: no remote copies, remote signals or barrier semaphores. Data moves between devices by JAX's collectives and lax.ppermute only.
A program may use at most 128 MiB of HBM per device.

v0:
```python
from functools import reduce
import math

import jax
import jax.numpy as jnp
from jax import lax
from jax.sharding import PartitionSpec as P

HD = 128


def from_behind(block, axis, distance):
    devices = range(lax.axis_size(axis))
    route = [(i - distance, i) for i in devices if i - distance in devices]
    return lax.ppermute(block, axis, route)


def select_rows(series, chosen, dilation, head_count):
    rows_kept = series.shape[0] // dilation
    hit_table = jnp.arange(dilation, dtype=jnp.int32)[:, None] == chosen[None, :]
    grouped = series.reshape(rows_kept, dilation, head_count, series.shape[1] // head_count)
    masked = jnp.where(hit_table[None, :, :, None], grouped, jnp.zeros((), series.dtype))
    return jnp.sum(masked, axis=1, dtype=series.dtype).reshape(rows_kept, series.shape[1])


def spread_rows(level_mixed, level_lse, chosen, dilation, head_count):
    rows_kept, feature_cols = level_mixed.shape
    hit_table = jnp.arange(dilation, dtype=jnp.int32)[:, None] == chosen[None, :]
    grouped = level_mixed.reshape(rows_kept, 1, head_count, feature_cols // head_count)
    full_mixed = jnp.where(hit_table[None, :, :, None], grouped, 0.0).reshape(
        rows_kept * dilation, head_count, feature_cols // head_count
    )
    full_lse = jnp.where(hit_table[None], level_lse[:, None, :], -jnp.inf).reshape(
        rows_kept * dilation, head_count
    )
    return (full_mixed, full_lse)


def store_block(buffer_rows, block_rows, target, usable):
    current = lax.dynamic_index_in_dim(buffer_rows, target, 0, False)
    return lax.dynamic_update_index_in_dim(
        buffer_rows, jnp.where(usable, block_rows, current), target, 0
    )


def cycle_collect(key_part, value_part, rank_in_group, group_span):
    rows_kept, feature_cols = key_part.shape
    blank_buffer = jnp.zeros((group_span, rows_kept, feature_cols), key_part.dtype)
    key_buffer = lax.dynamic_update_index_in_dim(blank_buffer, key_part, rank_in_group, 0)
    value_buffer = lax.dynamic_update_index_in_dim(blank_buffer, value_part, rank_in_group, 0)

    def advance(turn_index, state_tuple):
        moving_keys, moving_values, key_rows, value_rows = state_tuple
        moving_keys, moving_values = from_behind((moving_keys, moving_values), "ctx", 1)
        target = rank_in_group - turn_index
        usable = target >= 0
        target = jnp.maximum(target, 0)
        key_rows = store_block(key_rows, moving_keys, target, usable)
        value_rows = store_block(value_rows, moving_values, target, usable)
        return (moving_keys, moving_values, key_rows, value_rows)

    finished = lax.fori_loop(
        1, group_span, advance, (key_part, value_part, key_buffer, value_buffer)
    )
    return (
        finished[2].reshape(group_span * rows_kept, feature_cols),
        finished[3].reshape(group_span * rows_kept, feature_cols),
    )


def attend_level(query_rows, key_rows, value_rows, rank_in_group, head_count):
    rows_kept, feature_cols = query_rows.shape
    head_width = feature_cols // head_count
    key_count = key_rows.shape[0]
    block_rows = min(rows_kept, 512)
    block_count = rows_kept // block_rows
    scale_factor = 1.0 / math.sqrt(head_width)
    query_blocks = query_rows.reshape(block_count, block_rows, head_count, head_width)
    key_head_states = key_rows.reshape(key_count, head_count, head_width)
    value_head_states = value_rows.reshape(key_count, head_count, head_width)
    key_index = jnp.arange(key_count, dtype=jnp.int32)

    def one_block(packed):
        query_tile_rows, block_index = packed
        query_index = (
            rank_in_group * rows_kept
            + block_index * block_rows
            + jnp.arange(block_rows, dtype=jnp.int32)
        )
        allowed = key_index[None, :] <= query_index[:, None]
        scores = (
            jnp.einsum(
                "poa,zoa->poz", query_tile_rows, key_head_states, preferred_element_type=jnp.float32
            )
            * scale_factor
        )
        scores = jnp.where(allowed[:, None, :], scores, -jnp.inf)
        peak = jnp.max(scores, axis=-1, keepdims=True)
        expo = jnp.exp(scores - peak)
        total = jnp.sum(expo, axis=-1, keepdims=True)
        weight_matrix = expo.astype(jnp.bfloat16)
        level_mixed = (
            jnp.einsum(
                "vzp,pzl->vzl", weight_matrix, value_head_states, preferred_element_type=jnp.float32
            )
            / total
        )
        return (
            level_mixed.reshape(block_rows, feature_cols),
            peak[..., 0] + jnp.log(total[..., 0]),
        )

    mixed_blocks, lse_blocks = lax.map(
        one_block, (query_blocks, jnp.arange(block_count, dtype=jnp.int32))
    )
    return (
        mixed_blocks.reshape(rows_kept, feature_cols),
        lse_blocks.reshape(rows_kept, head_count),
    )


def local(query_states, key_states, value_states, offsets, out_weight):
    tok_rows, feature_cols = query_states.shape
    head_count = feature_cols // HD
    level_count = offsets.shape[0]
    head_group = lax.axis_index("head")
    position = lax.axis_index("ctx")
    local_offset_list = lax.dynamic_slice_in_dim(offsets, head_group * head_count, head_count, 1)
    picked = []
    for level_index in range(level_count):
        dilation = 2**level_index
        chosen = local_offset_list[level_index]
        picked.append(
            tuple(
                (
                    select_rows(series, chosen, dilation, head_count)
                    for series in (query_states, key_states, value_states)
                )
            )
        )
    gathered = []
    for level_index in range(level_count):
        dilation = 2**level_index
        if dilation > 1:
            gathered.append(
                cycle_collect(
                    picked[level_index][1], picked[level_index][2], position % dilation, dilation
                )
            )
        else:
            gathered.append((picked[level_index][1], picked[level_index][2]))
    mixed_parts = []
    lse_parts = []
    for level_index in range(level_count):
        dilation = 2**level_index
        level_mixed, level_lse = attend_level(
            picked[level_index][0],
            gathered[level_index][0],
            gathered[level_index][1],
            position % dilation,
            head_count,
        )
        full_mixed, full_lse = spread_rows(
            level_mixed, level_lse, local_offset_list[level_index], dilation, head_count
        )
        mixed_parts.append(full_mixed)
        lse_parts.append(full_lse)
    top_lse = reduce(jnp.maximum, lse_parts)
    numer = jnp.zeros((tok_rows, head_count, feature_cols // head_count), jnp.float32)
    denom = jnp.zeros((tok_rows, head_count), jnp.float32)
    for level_index in range(level_count):
        share = jnp.exp(lse_parts[level_index] - top_lse)
        numer = numer + share[:, :, None] * mixed_parts[level_index]
        denom = denom + share
    attended = (numer / denom[:, :, None]).reshape(tok_rows, feature_cols).astype(jnp.bfloat16)
    summed = lax.psum_scatter(
        lax.dot_general(
            out_weight, attended, (((0,), (1,)), ((), ())), preferred_element_type=jnp.float32
        ),
        "head",
        scatter_dimension=0,
        tiled=True,
    )
    return summed.T.astype(jnp.bfloat16)


def solution(mesh):
    placed = (P("ctx", "head"), P("ctx", "head"), P("ctx", "head"), P(), P("head", None))
    return jax.shard_map(
        local, mesh=mesh, in_specs=placed, out_specs=P("ctx", "head"), check_vma=False
    )
```

profile of v0, /device:TPU:1, one launch (start us, length us, event | category | flops | bytes accessed | tf_op | source)
XLA Modules:
  0.0 871.7 jit_solution(10860352837923659327)
XLA Ops:
  18.8 4.9 collective-permute-start.9
  71.0 27.1 %while.16 = (s32[]{:T(128)}, bf16[128,512]{1,0:T(8,128)(2,1)}, bf16[128,512]{1,0:T(8,128)(2,1)}, bf16[4,128,512]{2,1,0:T(8,128)(2,1)S(1)}, bf16[4,128,512]{2,1,0...) while((s32[]{:T(128)}, bf16[128,512]{1,0:T(8,128)(2,1)}, bf16[128,512]{1,0:T(8,128)(2,1)}, ...), condition=%wide.region_9.10_spmd, body=%wide.region_8.9_spmd.sunk | while | flops 131077 | bytes 2883796 | solution.py:62
  79.2 4.2 collective-permute-start.1
  88.4 4.2 collective-permute-start.1
  105.5 65.4 %while.17 = (s32[]{:T(128)}, bf16[64,512]{1,0:T(8,128)(2,1)}, bf16[64,512]{1,0:T(8,128)(2,1)S(1)}, bf16[8,64,512]{2,1,0:T(8,128)(2,1)S(1)}, bf16[8,64,512]{2,1,0...) while((s32[]{:T(128)}, bf16[64,512]{1,0:T(8,128)(2,1)}, bf16[64,512]{1,0:T(8,128)(2,1)S(1)}, ...), condition=%wide.region_16.17_spmd, body=%wide.region_15.16_spmd.sunk | while | flops 65541 | bytes 1442004 | solution.py:62
  105.5 4.2 collective-permute-start.3
  114.9 4.6 collective-permute-start.3
  124.3 4.5 collective-permute-start.3
  133.7 4.5 collective-permute-start.3
  143.0 4.5 collective-permute-start.3
  152.3 4.5 collective-permute-start.3
  161.6 4.5 collective-permute-start.3
  177.2 305.7 %while.19 = (s32[]{:T(128)}, bf16[16,512]{1,0:T(8,128)(2,1)S(1)}, bf16[16,512]{1,0:T(8,128)(2,1)S(1)}, bf16[32,16,512]{2,1,0:T(8,128)(2,1)S(1)}, bf16[32,16,512]...) while((s32[]{:T(128)}, bf16[16,512]{1,0:T(8,128)(2,1)S(1)}, bf16[16,512]{1,0:T(8,128)(2,1)S(1)}, ...), condition=%wide.region_30.31_spmd, body=%wide.region_29.30_spmd.sunk | while | flops 16389 | bytes 360660 | solution.py:62
  177.2 4.5 collective-permute-start.7
  185.1 5.0 collective-permute-start.7
  193.3 4.8 collective-permute-start.7
  201.7 5.1 collective-permute-start.7
  206.8 4.0 collective-permute-start.6
  211.7 5.4 collective-permute-start.7
  221.7 5.9 collective-permute-start.7
  231.7 6.4 collective-permute-start.7
  241.7 7.0 collective-permute-start.7
  252.0 6.7 collective-permute-start.7
  262.1 6.7 collective-permute-start.7
  272.1 6.7 collective-permute-start.7
  282.1 6.7 collective-permute-start.7
  292.2 6.7 collective-permute-start.7
  302.2 6.7 collective-permute-start.7
  312.3 6.7 collective-permute-start.7
  322.3 6.7 collective-permute-start.7
  332.3 6.7 collective-permute-start.7
  342.4 6.7 collective-permute-start.7
  352.4 6.7 collective-permute-start.7
  362.5 6.7 collective-permute-start.7
  372.5 6.7 collective-permute-start.7
  382.5 6.7 collective-permute-start.7
  392.6 6.7 collective-permute-start.7
  402.6 6.7 collective-permute-start.7
  412.7 6.7 collective-permute-start.7
  422.7 6.7 collective-permute-start.7
  432.7 6.7 collective-permute-start.7
  442.8 6.7 collective-permute-start.7
  452.8 6.7 collective-permute-start.7
  462.9 6.7 collective-permute-start.7
  472.9 6.7 collective-permute-start.7
  493.0 175.6 %while.18 = (s32[]{:T(128)}, bf16[32,512]{1,0:T(8,128)(2,1)}, bf16[32,512]{1,0:T(8,128)(2,1)}, bf16[16,32,512]{2,1,0:T(8,128)(2,1)}, bf16[16,32,512]{2,1,0:T(8,128)(2,1)S(1)}, /*index=5*/s32[]{:T(128)}, s32[]{:T(128)}, s32[]{:T(128)}) while((s32[]{:T(128)}, bf16[32,512]{1,0:T(8,128)(2,1)}, bf16[32,512]{1,0:T(8,128)(2,1)}, ...), condition=%wide.region_23.24_spmd, body=%wide.region_22.23_spmd.sunk | while | flops 32773 | bytes 721108 | solution.py:62
  493.0 6.7 collective-permute-start.5
  504.8 6.7 collective-permute-start.5
  516.6 6.8 collective-permute-start.5
  528.4 6.8 collective-permute-start.5
  540.2 6.8 collective-permute-start.5
  552.0 6.8 collective-permute-start.5
  563.8 6.9 collective-permute-start.5
  575.6 6.9 collective-permute-start.5
  587.1 7.0 collective-permute-start.5
  598.7 7.0 collective-permute-start.5
  610.4 7.1 collective-permute-start.5
  622.0 7.0 collective-permute-start.5
  633.7 7.0 collective-permute-start.5
  645.3 7.1 collective-permute-start.5
  656.9 7.0 collective-permute-start.5
  714.0 4.5 select_multiply_fusion
  746.1 3.9 convolution_bitcast_fusion
  750.0 112.7 %reduce-scatter.2.cloned.1.call-done = f32[512,512]{0,1:T(8,128)} async-done(((f32[2048,512]{0,1:T(8,128)}), f32[512,512]{0,1:T(8,128)}) %reduce-scatter.2.cloned.1.call-update) | async-done | bytes 1048592 | tf_op jit(solution)/shard_map/reduce_scatter | solution.py:176
  (746 shorter events, 381.7 us)
Async XLA Ops:
  6.5 856.2 %reduce-scatter.2.cloned.1.call-start = ((), (), s32[]{:S(2)}) async-start(), calls=%async_computation.1 | async-start | bytes 5242880 | tf_op jit(solution)/shard_map/reduce_scatter | solution.py:176
  18.8 684.6 %collective-permute-start.9 = (bf16[256,512]{1,0:T(8,128)(2,1)}, bf16[256,512]{1,0:T(8,128)(2,1)}, u32[]{:S(2)}, u32[]{:S(2)}) collective-permute-start(bf16[256,512]{1,0:T(8,128)(2,1)} %bitcast.298), channel_id=1, source_target_pairs={{0,4},{4,8},{8,12},{12,16},{16,20},{20,24},{24,28},{28,32},{32,36}... | collective-permute-start | bytes 786440 | tf_op jit(solution)/shard_map/while/body/eval_jaxpr/ppermute | solution.py:15
  24.4 679.0 %collective-permute-start.8 = (bf16[256,512]{1,0:T(8,128)(2,1)}, bf16[256,512]{1,0:T(8,128)(2,1)}, u32[]{:S(2)}, u32[]{:S(2)}) collective-permute-start(bf16[256,512]{1,0:T(8,128)(2,1)} %bitcast.299), channel_id=1, source_target_pairs={{0,4},{4,8},{8,12},{12,16},{16,20},{20,24},{24,28},{28,32},{32,36}... | collective-permute-start | bytes 786440 | tf_op jit(solution)/shard_map/while/body/eval_jaxpr/ppermute | solution.py:15
  71.2 5.3 collective-permute-start.1
  74.3 4.2 collective-permute-start
  79.2 6.5 collective-permute-start.1
  88.4 6.8 collective-permute-start.1
  92.6 4.7 collective-permute-start
  105.5 7.1 collective-permute-start.3
  109.8 4.5 collective-permute-start.2
  114.9 7.1 collective-permute-start.3
  124.3 7.0 collective-permute-start.3
  133.7 7.0 collective-permute-start.3
  143.0 7.0 collective-permute-start.3
  152.3 7.0 collective-permute-start.3
  161.6 7.0 collective-permute-start.3
  177.2 7.0 collective-permute-start.7
  185.1 7.3 collective-permute-start.7
  193.3 7.5 collective-permute-start.7
  201.7 9.1 %collective-permute-start.7 = (bf16[16,512]{1,0:T(8,128)(2,1)S(1)}, bf16[16,512]{1,0:T(8,128)(2,1)S(1)}, u32[]{:S(2)}, u32[]{:S(2)}) collective-permute-start(bf16[16,512]{1,0:T(8,128)(2,1)S(1)} %get-tuple-element.969), channel_id=1, source_target_pairs={{0,4},{4,8},{8,12},{12,16},{16,20},{20,24},{24,28},{28,32},{32,36}... | collective-permute-start | bytes 49160 | tf_op jit(solution)/shard_map/while/body/eval_jaxpr/ppermute | solution.py:15
  206.8 4.9 collective-permute-start.6
  211.7 9.1 %collective-permute-start.7 = (bf16[16,512]{1,0:T(8,128)(2,1)S(1)}, bf16[16,512]{1,0:T(8,128)(2,1)S(1)}, u32[]{:S(2)}, u32[]{:S(2)}) collective-permute-start(bf16[16,512]{1,0:T(8,128)(2,1)S(1)} %get-tuple-element.969), channel_id=1, source_target_pairs={{0,4},{4,8},{8,12},{12,16},{16,20},{20,24},{24,28},{28,32},{32,36}... | collective-permute-start | bytes 49160 | tf_op jit(solution)/shard_map/while/body/eval_jaxpr/ppermute | solution.py:15
  217.2 4.5 collective-permute-start.6
  221.7 9.1 %collective-permute-start.7 = (bf16[16,512]{1,0:T(8,128)(2,1)S(1)}, bf16[16,512]{1,0:T(8,128)(2,1)S(1)}, u32[]{:S(2)}, u32[]{:S(2)}) collective-permute-start(bf16[16,512]{1,0:T(8,128)(2,1)S(1)} %get-tuple-element.969), channel_id=1, source_target_pairs={{0,4},{4,8},{8,12},{12,16},{16,20},{20,24},{24,28},{28,32},{32,36}... | collective-permute-start | bytes 49160 | tf_op jit(solution)/shard_map/while/body/eval_jaxpr/ppermute | solution.py:15
  231.7 9.1 %collective-permute-start.7 = (bf16[16,512]{1,0:T(8,128)(2,1)S(1)}, bf16[16,512]{1,0:T(8,128)(2,1)S(1)}, u32[]{:S(2)}, u32[]{:S(2)}) collective-permute-start(bf16[16,512]{1,0:T(8,128)(2,1)S(1)} %get-tuple-element.969), channel_id=1, source_target_pairs={{0,4},{4,8},{8,12},{12,16},{16,20},{20,24},{24,28},{28,32},{32,36}... | collective-permute-start | bytes 49160 | tf_op jit(solution)/shard_map/while/body/eval_jaxpr/ppermute | solution.py:15
  241.7 9.4 %collective-permute-start.7 = (bf16[16,512]{1,0:T(8,128)(2,1)S(1)}, bf16[16,512]{1,0:T(8,128)(2,1)S(1)}, u32[]{:S(2)}, u32[]{:S(2)}) collective-permute-start(bf16[16,512]{1,0:T(8,128)(2,1)S(1)} %get-tuple-element.969), channel_id=1, source_target_pairs={{0,4},{4,8},{8,12},{12,16},{16,20},{20,24},{24,28},{28,32},{32,36}... | collective-permute-start | bytes 49160 | tf_op jit(solution)/shard_map/while/body/eval_jaxpr/ppermute | solution.py:15
  252.0 9.2 %collective-permute-start.7 = (bf16[16,512]{1,0:T(8,128)(2,1)S(1)}, bf16[16,512]{1,0:T(8,128)(2,1)S(1)}, u32[]{:S(2)}, u32[]{:S(2)}) collective-permute-start(bf16[16,512]{1,0:T(8,128)(2,1)S(1)} %get-tuple-element.969), channel_id=1, source_target_pairs={{0,4},{4,8},{8,12},{12,16},{16,20},{20,24},{24,28},{28,32},{32,36}... | collective-permute-start | bytes 49160 | tf_op jit(solution)/shard_map/while/body/eval_jaxpr/ppermute | solution.py:15
  262.1 9.2 %collective-permute-start.7 = (bf16[16,512]{1,0:T(8,128)(2,1)S(1)}, bf16[16,512]{1,0:T(8,128)(2,1)S(1)}, u32[]{:S(2)}, u32[]{:S(2)}) collective-permute-start(bf16[16,512]{1,0:T(8,128)(2,1)S(1)} %get-tuple-element.969), channel_id=1, source_target_pairs={{0,4},{4,8},{8,12},{12,16},{16,20},{20,24},{24,28},{28,32},{32,36}... | collective-permute-start | bytes 49160 | tf_op jit(solution)/shard_map/while/body/eval_jaxpr/ppermute | solution.py:15
  272.1 9.2 %collective-permute-start.7 = (bf16[16,512]{1,0:T(8,128)(2,1)S(1)}, bf16[16,512]{1,0:T(8,128)(2,1)S(1)}, u32[]{:S(2)}, u32[]{:S(2)}) collective-permute-start(bf16[16,512]{1,0:T(8,128)(2,1)S(1)} %get-tuple-element.969), channel_id=1, source_target_pairs={{0,4},{4,8},{8,12},{12,16},{16,20},{20,24},{24,28},{28,32},{32,36}... | collective-permute-start | bytes 49160 | tf_op jit(solution)/shard_map/while/body/eval_jaxpr/ppermute | solution.py:15
  282.1 9.2 %collective-permute-start.7 = (bf16[16,512]{1,0:T(8,128)(2,1)S(1)}, bf16[16,512]{1,0:T(8,128)(2,1)S(1)}, u32[]{:S(2)}, u32[]{:S(2)}) collective-permute-start(bf16[16,512]{1,0:T(8,128)(2,1)S(1)} %get-tuple-element.969), channel_id=1, source_target_pairs={{0,4},{4,8},{8,12},{12,16},{16,20},{20,24},{24,28},{28,32},{32,36}... | collective-permute-start | bytes 49160 | tf_op jit(solution)/shard_map/while/body/eval_jaxpr/ppermute | solution.py:15
  292.2 9.2 %collective-permute-start.7 = (bf16[16,512]{1,0:T(8,128)(2,1)S(1)}, bf16[16,512]{1,0:T(8,128)(2,1)S(1)}, u32[]{:S(2)}, u32[]{:S(2)}) collective-permute-start(bf16[16,512]{1,0:T(8,128)(2,1)S(1)} %get-tuple-element.969), channel_id=1, source_target_pairs={{0,4},{4,8},{8,12},{12,16},{16,20},{20,24},{24,28},{28,32},{32,36}... | collective-permute-start | bytes 49160 | tf_op jit(solution)/shard_map/while/body/eval_jaxpr/ppermute | solution.py:15
  302.2 9.2 %collective-permute-start.7 = (bf16[16,512]{1,0:T(8,128)(2,1)S(1)}, bf16[16,512]{1,0:T(8,128)(2,1)S(1)}, u32[]{:S(2)}, u32[]{:S(2)}) collective-permute-start(bf16[16,512]{1,0:T(8,128)(2,1)S(1)} %get-tuple-element.969), channel_id=1, source_target_pairs={{0,4},{4,8},{8,12},{12,16},{16,20},{20,24},{24,28},{28,32},{32,36}... | collective-permute-start | bytes 49160 | tf_op jit(solution)/shard_map/while/body/eval_jaxpr/ppermute | solution.py:15
  312.3 9.2 %collective-permute-start.7 = (bf16[16,512]{1,0:T(8,128)(2,1)S(1)}, bf16[16,512]{1,0:T(8,128)(2,1)S(1)}, u32[]{:S(2)}, u32[]{:S(2)}) collective-permute-start(bf16[16,512]{1,0:T(8,128)(2,1)S(1)} %get-tuple-element.969), channel_id=1, source_target_pairs={{0,4},{4,8},{8,12},{12,16},{16,20},{20,24},{24,28},{28,32},{32,36}... | collective-permute-start | bytes 49160 | tf_op jit(solution)/shard_map/while/body/eval_jaxpr/ppermute | solution.py:15
  322.3 9.2 %collective-permute-start.7 = (bf16[16,512]{1,0:T(8,128)(2,1)S(1)}, bf16[16,512]{1,0:T(8,128)(2,1)S(1)}, u32[]{:S(2)}, u32[]{:S(2)}) collective-permute-start(bf16[16,512]{1,0:T(8,128)(2,1)S(1)} %get-tuple-element.969), channel_id=1, source_target_pairs={{0,4},{4,8},{8,12},{12,16},{16,20},{20,24},{24,28},{28,32},{32,36}... | collective-permute-start | bytes 49160 | tf_op jit(solution)/shard_map/while/body/eval_jaxpr/ppermute | solution.py:15
  332.3 9.2 %collective-permute-start.7 = (bf16[16,512]{1,0:T(8,128)(2,1)S(1)}, bf16[16,512]{1,0:T(8,128)(2,1)S(1)}, u32[]{:S(2)}, u32[]{:S(2)}) collective-permute-start(bf16[16,512]{1,0:T(8,128)(2,1)S(1)} %get-tuple-element.969), channel_id=1, source_target_pairs={{0,4},{4,8},{8,12},{12,16},{16,20},{20,24},{24,28},{28,32},{32,36}... | collective-permute-start | bytes 49160 | tf_op jit(solution)/shard_map/while/body/eval_jaxpr/ppermute | solution.py:15
  342.4 9.2 %collective-permute-start.7 = (bf16[16,512]{1,0:T(8,128)(2,1)S(1)}, bf16[16,512]{1,0:T(8,128)(2,1)S(1)}, u32[]{:S(2)}, u32[]{:S(2)}) collective-permute-start(bf16[16,512]{1,0:T(8,128)(2,1)S(1)} %get-tuple-element.969), channel_id=1, source_target_pairs={{0,4},{4,8},{8,12},{12,16},{16,20},{20,24},{24,28},{28,32},{32,36}... | collective-permute-start | bytes 49160 | tf_op jit(solution)/shard_map/while/body/eval_jaxpr/ppermute | solution.py:15
  352.4 9.2 %collective-permute-start.7 = (bf16[16,512]{1,0:T(8,128)(2,1)S(1)}, bf16[16,512]{1,0:T(8,128)(2,1)S(1)}, u32[]{:S(2)}, u32[]{:S(2)}) collective-permute-start(bf16[16,512]{1,0:T(8,128)(2,1)S(1)} %get-tuple-element.969), channel_id=1, source_target_pairs={{0,4},{4,8},{8,12},{12,16},{16,20},{20,24},{24,28},{28,32},{32,36}... | collective-permute-start | bytes 49160 | tf_op jit(solution)/shard_map/while/body/eval_jaxpr/ppermute | solution.py:15
  362.5 9.2 %collective-permute-start.7 = (bf16[16,512]{1,0:T(8,128)(2,1)S(1)}, bf16[16,512]{1,0:T(8,128)(2,1)S(1)}, u32[]{:S(2)}, u32[]{:S(2)}) collective-permute-start(bf16[16,512]{1,0:T(8,128)(2,1)S(1)} %get-tuple-element.969), channel_id=1, source_target_pairs={{0,4},{4,8},{8,12},{12,16},{16,20},{20,24},{24,28},{28,32},{32,36}... | collective-permute-start | bytes 49160 | tf_op jit(solution)/shard_map/while/body/eval_jaxpr/ppermute | solution.py:15
  372.5 9.2 %collective-permute-start.7 = (bf16[16,512]{1,0:T(8,128)(2,1)S(1)}, bf16[16,512]{1,0:T(8,128)(2,1)S(1)}, u32[]{:S(2)}, u32[]{:S(2)}) collective-permute-start(bf16[16,512]{1,0:T(8,128)(2,1)S(1)} %get-tuple-element.969), channel_id=1, source_target_pairs={{0,4},{4,8},{8,12},{12,16},{16,20},{20,24},{24,28},{28,32},{32,36}... | collective-permute-start | bytes 49160 | tf_op jit(solution)/shard_map/while/body/eval_jaxpr/ppermute | solution.py:15
  382.5 9.2 %collective-permute-start.7 = (bf16[16,512]{1,0:T(8,128)(2,1)S(1)}, bf16[16,512]{1,0:T(8,128)(2,1)S(1)}, u32[]{:S(2)}, u32[]{:S(2)}) collective-permute-start(bf16[16,512]{1,0:T(8,128)(2,1)S(1)} %get-tuple-element.969), channel_id=1, source_target_pairs={{0,4},{4,8},{8,12},{12,16},{16,20},{20,24},{24,28},{28,32},{32,36}... | collective-permute-start | bytes 49160 | tf_op jit(solution)/shard_map/while/body/eval_jaxpr/ppermute | solution.py:15
  392.6 9.2 %collective-permute-start.7 = (bf16[16,512]{1,0:T(8,128)(2,1)S(1)}, bf16[16,512]{1,0:T(8,128)(2,1)S(1)}, u32[]{:S(2)}, u32[]{:S(2)}) collective-permute-start(bf16[16,512]{1,0:T(8,128)(2,1)S(1)} %get-tuple-element.969), channel_id=1, source_target_pairs={{0,4},{4,8},{8,12},{12,16},{16,20},{20,24},{24,28},{28,32},{32,36}... | collective-permute-start | bytes 49160 | tf_op jit(solution)/shard_map/while/body/eval_jaxpr/ppermute | solution.py:15
  402.6 9.2 %collective-permute-start.7 = (bf16[16,512]{1,0:T(8,128)(2,1)S(1)}, bf16[16,512]{1,0:T(8,128)(2,1)S(1)}, u32[]{:S(2)}, u32[]{:S(2)}) collective-permute-start(bf16[16,512]{1,0:T(8,128)(2,1)S(1)} %get-tuple-element.969), channel_id=1, source_target_pairs={{0,4},{4,8},{8,12},{12,16},{16,20},{20,24},{24,28},{28,32},{32,36}... | collective-permute-start | bytes 49160 | tf_op jit(solution)/shard_map/while/body/eval_jaxpr/ppermute | solution.py:15
  412.7 9.2 %collective-permute-start.7 = (bf16[16,512]{1,0:T(8,128)(2,1)S(1)}, bf16[16,512]{1,0:T(8,128)(2,1)S(1)}, u32[]{:S(2)}, u32[]{:S(2)}) collective-permute-start(bf16[16,512]{1,0:T(8,128)(2,1)S(1)} %get-tuple-element.969), channel_id=1, source_target_pairs={{0,4},{4,8},{8,12},{12,16},{16,20},{20,24},{24,28},{28,32},{32,36}... | collective-permute-start | bytes 49160 | tf_op jit(solution)/shard_map/while/body/eval_jaxpr/ppermute | solution.py:15
  422.7 9.2 %collective-permute-start.7 = (bf16[16,512]{1,0:T(8,128)(2,1)S(1)}, bf16[16,512]{1,0:T(8,128)(2,1)S(1)}, u32[]{:S(2)}, u32[]{:S(2)}) collective-permute-start(bf16[16,512]{1,0:T(8,128)(2,1)S(1)} %get-tuple-element.969), channel_id=1, source_target_pairs={{0,4},{4,8},{8,12},{12,16},{16,20},{20,24},{24,28},{28,32},{32,36}... | collective-permute-start | bytes 49160 | tf_op jit(solution)/shard_map/while/body/eval_jaxpr/ppermute | solution.py:15
  432.7 9.2 %collective-permute-start.7 = (bf16[16,512]{1,0:T(8,128)(2,1)S(1)}, bf16[16,512]{1,0:T(8,128)(2,1)S(1)}, u32[]{:S(2)}, u32[]{:S(2)}) collective-permute-start(bf16[16,512]{1,0:T(8,128)(2,1)S(1)} %get-tuple-element.969), channel_id=1, source_target_pairs={{0,4},{4,8},{8,12},{12,16},{16,20},{20,24},{24,28},{28,32},{32,36}... | collective-permute-start | bytes 49160 | tf_op jit(solution)/shard_map/while/body/eval_jaxpr/ppermute | solution.py:15
  442.8 9.2 %collective-permute-start.7 = (bf16[16,512]{1,0:T(8,128)(2,1)S(1)}, bf16[16,512]{1,0:T(8,128)(2,1)S(1)}, u32[]{:S(2)}, u32[]{:S(2)}) collective-permute-start(bf16[16,512]{1,0:T(8,128)(2,1)S(1)} %get-tuple-element.969), channel_id=1, source_target_pairs={{0,4},{4,8},{8,12},{12,16},{16,20},{20,24},{24,28},{28,32},{32,36}... | collective-permute-start | bytes 49160 | tf_op jit(solution)/shard_map/while/body/eval_jaxpr/ppermute | solution.py:15
  452.8 9.2 %collective-permute-start.7 = (bf16[16,512]{1,0:T(8,128)(2,1)S(1)}, bf16[16,512]{1,0:T(8,128)(2,1)S(1)}, u32[]{:S(2)}, u32[]{:S(2)}) collective-permute-start(bf16[16,512]{1,0:T(8,128)(2,1)S(1)} %get-tuple-element.969), channel_id=1, source_target_pairs={{0,4},{4,8},{8,12},{12,16},{16,20},{20,24},{24,28},{28,32},{32,36}... | collective-permute-start | bytes 49160 | tf_op jit(solution)/shard_map/while/body/eval_jaxpr/ppermute | solution.py:15
  462.9 9.2 %collective-permute-start.7 = (bf16[16,512]{1,0:T(8,128)(2,1)S(1)}, bf16[16,512]{1,0:T(8,128)(2,1)S(1)}, u32[]{:S(2)}, u32[]{:S(2)}) collective-permute-start(bf16[16,512]{1,0:T(8,128)(2,1)S(1)} %get-tuple-element.969), channel_id=1, source_target_pairs={{0,4},{4,8},{8,12},{12,16},{16,20},{20,24},{24,28},{28,32},{32,36}... | collective-permute-start | bytes 49160 | tf_op jit(solution)/shard_map/while/body/eval_jaxpr/ppermute | solution.py:15
  472.9 9.2 %collective-permute-start.7 = (bf16[16,512]{1,0:T(8,128)(2,1)S(1)}, bf16[16,512]{1,0:T(8,128)(2,1)S(1)}, u32[]{:S(2)}, u32[]{:S(2)}) collective-permute-start(bf16[16,512]{1,0:T(8,128)(2,1)S(1)} %get-tuple-element.969), channel_id=1, source_target_pairs={{0,4},{4,8},{8,12},{12,16},{16,20},{20,24},{24,28},{28,32},{32,36}... | collective-permute-start | bytes 49160 | tf_op jit(solution)/shard_map/while/body/eval_jaxpr/ppermute | solution.py:15
  493.0 9.9 %collective-permute-start.5 = (bf16[32,512]{1,0:T(8,128)(2,1)}, bf16[32,512]{1,0:T(8,128)(2,1)S(1)}, u32[]{:S(2)}, u32[]{:S(2)}) collective-permute-start(bf16[32,512]{1,0:T(8,128)(2,1)} %get-tuple-element.945), channel_id=1, source_target_pairs={{0,4},{4,8},{8,12},{12,16},{16,20},{20,24},{24,28},{28,32},{32,36}... | collective-permute-start | bytes 98312 | tf_op jit(solution)/shard_map/while/body/eval_jaxpr/ppermute | solution.py:15
  504.8 9.9 %collective-permute-start.5 = (bf16[32,512]{1,0:T(8,128)(2,1)}, bf16[32,512]{1,0:T(8,128)(2,1)S(1)}, u32[]{:S(2)}, u32[]{:S(2)}) collective-permute-start(bf16[32,512]{1,0:T(8,128)(2,1)} %get-tuple-element.945), channel_id=1, source_target_pairs={{0,4},{4,8},{8,12},{12,16},{16,20},{20,24},{24,28},{28,32},{32,36}... | collective-permute-start | bytes 98312 | tf_op jit(solution)/shard_map/while/body/eval_jaxpr/ppermute | solution.py:15
  516.6 10.0 %collective-permute-start.5 = (bf16[32,512]{1,0:T(8,128)(2,1)}, bf16[32,512]{1,0:T(8,128)(2,1)S(1)}, u32[]{:S(2)}, u32[]{:S(2)}) collective-permute-start(bf16[32,512]{1,0:T(8,128)(2,1)} %get-tuple-element.945), channel_id=1, source_target_pairs={{0,4},{4,8},{8,12},{12,16},{16,20},{20,24},{24,28},{28,32},{32,36}... | collective-permute-start | bytes 98312 | tf_op jit(solution)/shard_map/while/body/eval_jaxpr/ppermute | solution.py:15
  528.4 9.9 %collective-permute-start.5 = (bf16[32,512]{1,0:T(8,128)(2,1)}, bf16[32,512]{1,0:T(8,128)(2,1)S(1)}, u32[]{:S(2)}, u32[]{:S(2)}) collective-permute-start(bf16[32,512]{1,0:T(8,128)(2,1)} %get-tuple-element.945), channel_id=1, source_target_pairs={{0,4},{4,8},{8,12},{12,16},{16,20},{20,24},{24,28},{28,32},{32,36}... | collective-permute-start | bytes 98312 | tf_op jit(solution)/shard_map/while/body/eval_jaxpr/ppermute | solution.py:15
  540.2 9.9 %collective-permute-start.5 = (bf16[32,512]{1,0:T(8,128)(2,1)}, bf16[32,512]{1,0:T(8,128)(2,1)S(1)}, u32[]{:S(2)}, u32[]{:S(2)}) collective-permute-start(bf16[32,512]{1,0:T(8,128)(2,1)} %get-tuple-element.945), channel_id=1, source_target_pairs={{0,4},{4,8},{8,12},{12,16},{16,20},{20,24},{24,28},{28,32},{32,36}... | collective-permute-start | bytes 98312 | tf_op jit(solution)/shard_map/while/body/eval_jaxpr/ppermute | solution.py:15
  552.0 9.9 %collective-permute-start.5 = (bf16[32,512]{1,0:T(8,128)(2,1)}, bf16[32,512]{1,0:T(8,128)(2,1)S(1)}, u32[]{:S(2)}, u32[]{:S(2)}) collective-permute-start(bf16[32,512]{1,0:T(8,128)(2,1)} %get-tuple-element.945), channel_id=1, source_target_pairs={{0,4},{4,8},{8,12},{12,16},{16,20},{20,24},{24,28},{28,32},{32,36}... | collective-permute-start | bytes 98312 | tf_op jit(solution)/shard_map/while/body/eval_jaxpr/ppermute | solution.py:15
  563.8 9.9 %collective-permute-start.5 = (bf16[32,512]{1,0:T(8,128)(2,1)}, bf16[32,512]{1,0:T(8,128)(2,1)S(1)}, u32[]{:S(2)}, u32[]{:S(2)}) collective-permute-start(bf16[32,512]{1,0:T(8,128)(2,1)} %get-tuple-element.945), channel_id=1, source_target_pairs={{0,4},{4,8},{8,12},{12,16},{16,20},{20,24},{24,28},{28,32},{32,36}... | collective-permute-start | bytes 98312 | tf_op jit(solution)/shard_map/while/body/eval_jaxpr/ppermute | solution.py:15
  575.6 9.7 %collective-permute-start.5 = (bf16[32,512]{1,0:T(8,128)(2,1)}, bf16[32,512]{1,0:T(8,128)(2,1)S(1)}, u32[]{:S(2)}, u32[]{:S(2)}) collective-permute-start(bf16[32,512]{1,0:T(8,128)(2,1)} %get-tuple-element.945), channel_id=1, source_target_pairs={{0,4},{4,8},{8,12},{12,16},{16,20},{20,24},{24,28},{28,32},{32,36}... | collective-permute-start | bytes 98312 | tf_op jit(solution)/shard_map/while/body/eval_jaxpr/ppermute | solution.py:15
  587.1 9.8 %collective-permute-start.5 = (bf16[32,512]{1,0:T(8,128)(2,1)}, bf16[32,512]{1,0:T(8,128)(2,1)S(1)}, u32[]{:S(2)}, u32[]{:S(2)}) collective-permute-start(bf16[32,512]{1,0:T(8,128)(2,1)} %get-tuple-element.945), channel_id=1, source_target_pairs={{0,4},{4,8},{8,12},{12,16},{16,20},{20,24},{24,28},{28,32},{32,36}... | collective-permute-start | bytes 98312 | tf_op jit(solution)/shard_map/while/body/eval_jaxpr/ppermute | solution.py:15
  598.7 9.7 %collective-permute-start.5 = (bf16[32,512]{1,0:T(8,128)(2,1)}, bf16[32,512]{1,0:T(8,128)(2,1)S(1)}, u32[]{:S(2)}, u32[]{:S(2)}) collective-permute-start(bf16[32,512]{1,0:T(8,128)(2,1)} %get-tuple-element.945), channel_id=1, source_target_pairs={{0,4},{4,8},{8,12},{12,16},{16,20},{20,24},{24,28},{28,32},{32,36}... | collective-permute-start | bytes 98312 | tf_op jit(solution)/shard_map/while/body/eval_jaxpr/ppermute | solution.py:15
  610.4 9.8 %collective-permute-start.5 = (bf16[32,512]{1,0:T(8,128)(2,1)}, bf16[32,512]{1,0:T(8,128)(2,1)S(1)}, u32[]{:S(2)}, u32[]{:S(2)}) collective-permute-start(bf16[32,512]{1,0:T(8,128)(2,1)} %get-tuple-element.945), channel_id=1, source_target_pairs={{0,4},{4,8},{8,12},{12,16},{16,20},{20,24},{24,28},{28,32},{32,36}... | collective-permute-start | bytes 98312 | tf_op jit(solution)/shard_map/while/body/eval_jaxpr/ppermute | solution.py:15
  622.0 9.8 %collective-permute-start.5 = (bf16[32,512]{1,0:T(8,128)(2,1)}, bf16[32,512]{1,0:T(8,128)(2,1)S(1)}, u32[]{:S(2)}, u32[]{:S(2)}) collective-permute-start(bf16[32,512]{1,0:T(8,128)(2,1)} %get-tuple-element.945), channel_id=1, source_target_pairs={{0,4},{4,8},{8,12},{12,16},{16,20},{20,24},{24,28},{28,32},{32,36}... | collective-permute-start | bytes 98312 | tf_op jit(solution)/shard_map/while/body/eval_jaxpr/ppermute | solution.py:15
  633.7 9.7 %collective-permute-start.5 = (bf16[32,512]{1,0:T(8,128)(2,1)}, bf16[32,512]{1,0:T(8,128)(2,1)S(1)}, u32[]{:S(2)}, u32[]{:S(2)}) collective-permute-start(bf16[32,512]{1,0:T(8,128)(2,1)} %get-tuple-element.945), channel_id=1, source_target_pairs={{0,4},{4,8},{8,12},{12,16},{16,20},{20,24},{24,28},{28,32},{32,36}... | collective-permute-start | bytes 98312 | tf_op jit(solution)/shard_map/while/body/eval_jaxpr/ppermute | solution.py:15
  645.3 9.8 %collective-permute-start.5 = (bf16[32,512]{1,0:T(8,128)(2,1)}, bf16[32,512]{1,0:T(8,128)(2,1)S(1)}, u32[]{:S(2)}, u32[]{:S(2)}) collective-permute-start(bf16[32,512]{1,0:T(8,128)(2,1)} %get-tuple-element.945), channel_id=1, source_target_pairs={{0,4},{4,8},{8,12},{12,16},{16,20},{20,24},{24,28},{28,32},{32,36}... | collective-permute-start | bytes 98312 | tf_op jit(solution)/shard_map/while/body/eval_jaxpr/ppermute | solution.py:15
  656.9 9.8 %collective-permute-start.5 = (bf16[32,512]{1,0:T(8,128)(2,1)}, bf16[32,512]{1,0:T(8,128)(2,1)S(1)}, u32[]{:S(2)}, u32[]{:S(2)}) collective-permute-start(bf16[32,512]{1,0:T(8,128)(2,1)} %get-tuple-element.945), channel_id=1, source_target_pairs={{0,4},{4,8},{8,12},{12,16},{16,20},{20,24},{24,28},{28,32},{32,36}... | collective-permute-start | bytes 98312 | tf_op jit(solution)/shard_map/while/body/eval_jaxpr/ppermute | solution.py:15
  (112 other events, 2727.0 us)
Sparse Core Ops, SparseCore 0:
  750.1 112.5 reduce-scatter.1
where the time goes:
time: 878 us; the launch traced here: 872 us
  starting transfers between devices  487 us (55%)
  waiting for transfers between devices  153 us (17%)
  local copies, waits for them, and re-layouts  143 us (16%)
  other arithmetic  42.8 us (5%)
  matrix products  27.3 us (3%)
  between operations  14.4 us (2%)
    ppermute x114, starting transfers between devices, from_behind(): return lax.ppermute(block, axis, route)  487 us
    reduce_scatter x1, waiting for transfers between devices, local(): lax.psum_scatter(lax.dot_general(out_weight, attended, (((0,), (1,)), (()...  113 us
    ppermute x114, waiting for transfers between devices, from_behind(): return lax.ppermute(block, axis, route)  40.5 us
    while x112, local copies, waits for them, and re-layouts  27 us
  transfers between devices with their start and end apart: 115, of which 44 were waited for; matrix products, arithmetic and copies ran while one was open for 17% of the time, Pallas kernels for 0%

commit v1 on v0

v1 whole, which is shorter than its diff:
```python
import functools
import math

import jax
import jax.numpy as jnp
from jax import lax
from jax.experimental import pallas as pl
from jax.experimental.pallas import tpu as pltpu
from jax.sharding import PartitionSpec as P

HD = 128
F32 = jnp.float32
BF16 = jnp.bfloat16
TOK = 512
CHIP = 2 * TOK
GAIN = math.log2(math.e) / math.sqrt(HD)
CORE, Z, X1, X2, Y1 = 1, 2, 4, 8, 16
BLOCKS = {
    2: (0, 1),
    3: (0, 1, 2, 3),
    4: (0, 2, 4, 6, 1, 3, 5, 7),
    5: (0, 2, 4, 6, 1, 3, 5, 7, 8, 10, 12, 14, 9, 11, 13, 15),
}


def swap(block, bits, up_only=False):
    route = [(i, i ^ bits) for i in range(64) if not up_only or i < i ^ bits]
    return lax.ppermute(block, "ctx", route)


def ring(block, step):
    return lax.ppermute(block, "head", [(i, (i + step) % 4) for i in range(4)])


def params():
    return pltpu.CompilerParams(vmem_limit_bytes=24 * 1024 * 1024)


def used(off, level, j, first=0, count=None):
    r = 1 << level
    n = CHIP // r if count is None else count
    return pl.ds(off + first * r, n, stride=r)


def fill(buf, base, pos, mine, theirs):
    core = pos[0]
    here = pl.multiple_of(core * TOK, TOK)
    there = pl.multiple_of(TOK - core * TOK, TOK)
    for j in range(2):
        cols = pl.ds(pl.multiple_of(core * 256 + j * HD, HD), HD)
        buf[base + j, pl.ds(here, TOK), :] = mine[:, cols].astype(F32)
        buf[base + j, pl.ds(there, TOK), :] = theirs[:, j * HD : (j + 1) * HD].astype(F32)


def pick_kernel(pos, offs, k, v, rk, rv, g45, g3, g2, buf):
    fill(buf, 0, pos, k, rk)
    fill(buf, 2, pos, v, rv)
    for level, dst, row in ((5, g45, 0), (4, g45, 64), (3, g3, 0), (2, g2, 0)):
        n = CHIP >> level
        for j in range(2):
            rows = used(offs[level, pos[1] + j], level, j)
            dst[row + j * n : row + (j + 1) * n, :HD] = buf[j, rows, :].astype(BF16)
            dst[row + j * n : row + (j + 1) * n, HD:] = buf[2 + j, rows, :].astype(BF16)


def softmax_parts(scores, values):
    peak = jnp.max(scores, axis=-1, keepdims=True)
    expo = jnp.exp2((scores - peak) * GAIN)
    total = jnp.sum(expo, axis=-1, keepdims=True)
    mixed = jnp.dot(expo.astype(BF16), values, preferred_element_type=F32)
    return peak, total, mixed


def raw_scores(q, k):
    return lax.dot_general(q, k, (((1,), (1,)), ((), ())), preferred_element_type=F32)


def causal(q, k, v, first):
    n = q.shape[0]
    m = first + n
    s = raw_scores(q, k[:m])
    row = lax.broadcasted_iota(jnp.int32, (n, m), 0) + first
    col = lax.broadcasted_iota(jnp.int32, (n, m), 1)
    s = jnp.where(col <= row, s, -jnp.inf)
    return softmax_parts(s, v[:m])


def pack(peak, total):
    lane = lax.broadcasted_iota(jnp.int32, (peak.shape[0], HD), 1)
    return jnp.where(lane < HD // 2, peak, total)


def merge(acc, stat, j, rows, peak, total, mixed):
    old = stat[j, rows, :]
    old_peak, old_total = old[:, :1], old[:, HD // 2 : HD // 2 + 1]
    top = jnp.maximum(old_peak, peak)
    a = jnp.exp2((old_peak - top) * GAIN)
    b = jnp.exp2((peak - top) * GAIN)
    acc[j, rows, :] = acc[j, rows, :] * a + mixed * b
    stat[j, rows, :] = pack(top, old_total * a + total * b)


def near_kernel(pos, offs, q, k, v, rq, rk, rv, acc, stat, bq, buf):
    fill(buf, 0, pos, q, rq)
    fill(buf, 2, pos, k, rk)
    fill(buf, 4, pos, v, rv)
    row = 0
    for level in (5, 4, 3, 2):
        n = CHIP >> level
        for j in range(2):
            rows = used(offs[level, pos[1] + j], level, j)
            bq[row : row + n, :] = buf[j, rows, :].astype(BF16)
            row += n
    for j in range(2):
        for tile in range(2):
            span = slice(tile * TOK, (tile + 1) * TOK)
            qs, ks, vs = (buf[2 * i + j, span, :].astype(BF16) for i in range(3))
            for half in range(2):
                peak, total, mixed = causal(qs[half * 256 : half * 256 + 256], ks, vs, half * 256)
                at = slice(tile * TOK + half * 256, tile * TOK + half * 256 + 256)
                acc[j, at, :] = mixed
                stat[j, at, :] = pack(peak, total)
    for j in range(2):
        off = offs[1, pos[1] + j]
        qs, ks, vs = (buf[2 * i + j, used(off, 1, j), :].astype(BF16) for i in range(3))
        for half in range(2):
            part = causal(qs[half * 256 : half * 256 + 256], ks, vs, half * 256)
            merge(acc, stat, j, used(off, 1, j, half * 256, 256), *part)


def far_kernel(pos, offs, bias, acc0, stat0, bq, o45, o3, o2, a0, a1, a2, b, c, d, e, f, g, mine, other, acc, stat):
    acc[...] = acc0[...]
    stat[...] = stat0[...]
    quad = (o45, a0, a1, a2)
    for level in (2, 3, 4, 5):
        n = CHIP >> level
        qrow = {5: 0, 4: 64, 3: 192, 2: 448}[level]
        for j in range(2):
            at = slice(j * n, (j + 1) * n)
            if level == 2:
                parts = [o2[at], c[at]]
            elif level == 3:
                parts = [o3[at], b[at], d[at], d[256 + j * n : 256 + (j + 1) * n]]
            else:
                s = 64 if level == 4 else 0
                at = slice(s + j * n, s + (j + 1) * n)
                parts = [x[at] for x in quad]
                parts += [e[192 * i + s + j * n : 192 * i + s + (j + 1) * n] for i in range(4)]
                if level == 5:
                    for y in (f, g):
                        parts += [y[64 * i + j * n : 64 * i + (j + 1) * n] for i in range(4)]
            keys = jnp.concatenate([x[:, :HD] for x in parts], axis=0)
            values = jnp.concatenate([x[:, HD:] for x in parts], axis=0)
            s = raw_scores(bq[qrow + j * n : qrow + (j + 1) * n, :], keys)
            row = lax.broadcasted_iota(jnp.int32, s.shape, 0)
            col = lax.broadcasted_iota(jnp.int32, s.shape, 1)
            s = s + bias[level : level + 1, :]
            s = jnp.where((col < n) & (col > row), -jnp.inf, s)
            part = softmax_parts(s, values)
            merge(acc, stat, j, used(offs[level, pos[1] + j], level, j), *part)
    core = pos[0]
    for start, dst in ((core * TOK, mine), (TOK - core * TOK, other)):
        rows = pl.ds(pl.multiple_of(start, TOK), TOK)
        for j in range(2):
            total = stat[j, rows, :][:, HD // 2 : HD // 2 + 1]
            dst[:, j * HD : (j + 1) * HD] = (acc[j, rows, :] / total).astype(BF16)


def project(pos, mine, back, w, first, count, dest):
    core = pos[0]
    cols = pl.ds(pl.multiple_of(dest * TOK, TOK), TOK)
    near = pl.ds(pl.multiple_of(core * 256, 256), 256)
    far = pl.ds(pl.multiple_of(256 - core * 256, 256), 256)
    rows = slice(first, first + count)
    return jnp.dot(mine[rows, :], w[near, cols], preferred_element_type=F32) + jnp.dot(
        back[rows, :], w[far, cols], preferred_element_type=F32
    )


def opposite_kernel(pos, mine, back, w, up, down):
    dest = lax.rem(pos[3] + 2, 4)
    up[...] = project(pos, mine, back, w, 0, 256, dest).astype(BF16)
    down[...] = project(pos, mine, back, w, 256, 256, dest).astype(BF16)


def rest_kernel(pos, mine, back, w, up, down, up_late, down_late, own):
    after, before = lax.rem(pos[3] + 1, 4), lax.rem(pos[3] + 3, 4)
    up[...] = project(pos, mine, back, w, 256, 256, after).astype(BF16)
    down[...] = project(pos, mine, back, w, 0, 256, before).astype(BF16)
    up_late[...] = project(pos, mine, back, w, 0, 256, after)
    down_late[...] = project(pos, mine, back, w, 256, 256, before)
    for first in (0, 256):
        own[first : first + 256, :] = project(pos, mine, back, w, first, 256, pos[3])


SMEM = pl.BlockSpec(memory_space=pltpu.SMEM)
VMEM = pl.BlockSpec(memory_space=pltpu.VMEM)


def call(kernel, scalars, arrays, outs, scratch=(), flops=0, exps=0):
    nbytes = sum(a.size * a.dtype.itemsize for a in arrays)
    return pl.pallas_call(
        kernel,
        in_specs=[SMEM] * len(scalars) + [VMEM] * len(arrays),
        out_specs=[VMEM] * len(outs),
        out_shape=[jax.ShapeDtypeStruct(s, t) for s, t in outs],
        scratch_shapes=[pltpu.VMEM(s, F32) for s in scratch],
        compiler_params=params(),
        cost_estimate=pl.CostEstimate(flops=flops, bytes_accessed=nbytes, transcendentals=exps),
    )(*scalars, *arrays)


def local(q, k, v, offsets, w):
    ctx = lax.axis_index("ctx")
    head = lax.axis_index("head")
    core = ctx % 2
    chip = ctx // 2
    pos = jnp.stack([core, head * 4 + core * 2, chip, head]).astype(jnp.int32)

    def theirs(x):
        return lax.dynamic_slice_in_dim(x, 256 - core * 256, 256, 1)

    rk, rv, rq = (swap(theirs(x), CORE) for x in (k, v, q))
    g45, g3, g2 = call(
        pick_kernel,
        (pos, offsets),
        (k, v, rk, rv),
        [((192, 256), BF16), ((256, 256), BF16), ((512, 256), BF16)],
        [(4, CHIP, HD)],
    )
    a = [swap(g45, bits) for bits in (X1, X2, X1 | X2)]
    b = swap(g3, Z)
    c = swap(g2, Z, True)
    acc, stat, bq = call(
        near_kernel,
        (pos, offsets),
        (q, k, v, rq, rk, rv),
        [((2, CHIP, HD), F32), ((2, CHIP, HD), F32), ((960, HD), BF16)],
        [(6, CHIP, HD)],
        flops=6 * 4 * TOK * TOK * HD,
        exps=6 * TOK * TOK,
    )
    d = swap(jnp.concatenate([g3, b]), X1, True)
    e = swap(jnp.concatenate([g45] + a), Z)
    g5 = jnp.concatenate([g45[:64]] + [x[:64] for x in a])
    f = swap(g5, Y1, True)
    g = swap(g5, Y1 | Z, True)

    rows = [jnp.zeros((2, TOK), F32)]
    for level in (2, 3, 4, 5):
        span = chip % (1 << (level - 1))
        code = jnp.array(BLOCKS[level], jnp.int32)
        fine = (code == 0) | ((span ^ code) < span)
        rows.append(jnp.repeat(jnp.where(fine, 0.0, -jnp.inf).astype(F32), CHIP >> level)[None])
    bias = jnp.concatenate(rows)

    mine, other = call(
        far_kernel,
        (pos, offsets),
        (bias, acc, stat, bq, g45, g3, g2, *a, b, c, d, e, f, g),
        [((TOK, 256), BF16), ((TOK, 256), BF16)],
        [(2, CHIP, HD), (2, CHIP, HD)],
        flops=2 * 4 * TOK * TOK * HD,
        exps=2 * TOK * TOK,
    )
    back = swap(other, CORE)

    half = (256, TOK)
    up1, down1 = call(
        opposite_kernel, (pos,), (mine, back, w), [(half, BF16)] * 2, flops=2 * TOK * TOK * TOK
    )
    up1, down1 = ring(up1, 1), ring(down1, 3)
    up2, down2, up_late, down_late, own = call(
        rest_kernel,
        (pos,),
        (mine, back, w),
        [(half, BF16)] * 2 + [(half, F32)] * 2 + [((TOK, TOK), F32)],
        flops=6 * TOK * TOK * TOK,
    )
    up2, down2 = ring(up2, 1), ring(down2, 3)
    up3 = ring((up_late + up1.astype(F32)).astype(BF16), 1)
    down3 = ring((down_late + down1.astype(F32)).astype(BF16), 3)
    top = own[:256] + up3.astype(F32) + down2.astype(F32)
    bottom = own[256:] + up2.astype(F32) + down3.astype(F32)
    return jnp.concatenate([top, bottom]).astype(BF16)


def solution(mesh):
    placed = (P("ctx", "head"), P("ctx", "head"), P("ctx", "head"), P(), P("head", None))
    return jax.shard_map(
        local, mesh=mesh, in_specs=placed, out_specs=P("ctx", "head"), check_vma=False
    )
```

time: 878 us -> 101 us (0.12)
  starting transfers between devices: 487 us -> 33.9 us
  local copies, waits for them, and re-layouts: 143 us -> 14.2 us
  waiting for transfers between devices: 153 us -> 30.7 us
  other arithmetic: 42.8 us -> 5.23 us
  matrix products: 27.3 us -> 0 us
  Pallas kernels: 0 us -> 16.5 us
  between operations: 14.4 us -> 0.23 us
    ppermute x114 -> x19, starting transfers between devices: 487 us -> 33.9 us  [the longest x13 20.6 us: swap(): return lax.ppermute(block, 'ctx', route)]
    reduce_scatter x1 -> x0, waiting for transfers between devices: 113 us -> none  [local(): lax.psum_scatter(lax.dot_general(out_weight, attended, (((0,), (1,)), (()...]
    broadcast_in_dim x54 -> x4, local copies, waits for them, and re-layouts: 33.7 us -> 2.64 us  [the longest x3 2.05 us: local(): jnp.repeat(jnp.where(fine, 0.0, -jnp.inf).astype(F32), CHIP >> level)[None]]
    dot_general x13 -> x0, matrix products: 27.3 us -> none  [the longest x6 13.9 us: one_block(): jnp.einsum('vzp,pzl->vzl', weight_matrix, value_head_states, preferred_el...]
    while x112 -> x0, local copies, waits for them, and re-layouts: 27 us -> none
    reshape x16 -> x0, local copies, waits for them, and re-layouts: 20.2 us -> none  [the longest x12 17.3 us: select_rows(): series.reshape(rows_kept, dilation, head_count, series.shape[1] // head_c...]
    reduce_sum x11 -> x0, other arithmetic: 18.9 us -> none  [the longest x5 16.3 us: select_rows(): jnp.sum(masked, axis=1, dtype=series.dtype)]
    pallas_call x0 -> x5, Pallas kernels: none -> 16.5 us  [call(): pl.pallas_call(kernel, in_specs=[SMEM] * len(scalars) + [VMEM] * len(arra...]
  transfers between devices with their start and end apart: 115 -> 19, of which waited for: 44 -> 6; matrix products, arithmetic and copies ran while one was open for 17% -> 12% of each run, Pallas kernels for 0% -> 10%
where the time goes in v1:
time: 101 us
  starting transfers between devices  33.9 us (34%)
  waiting for transfers between devices  30.7 us (30%)
  Pallas kernels  16.5 us (16%)
  local copies, waits for them, and re-layouts  14.2 us (14%)
  other arithmetic  5.23 us (5%)
    ppermute x6, waiting for transfers between devices, ring(): return lax.ppermute(block, 'head', [(i, (i + step) % 4) for i in range(4)])  28 us
    ppermute x13, starting transfers between devices, swap(): return lax.ppermute(block, 'ctx', route)  20.6 us
    pallas_call x5, Pallas kernels, call(): pl.pallas_call(kernel, in_specs=[SMEM] * len(scalars) + [VMEM] * len(arra...  16.5 us
    ppermute x6, starting transfers between devices, ring(): return lax.ppermute(block, 'head', [(i, (i + step) % 4) for i in range(4)])  13.4 us
    unnamed x26, local copies, waits for them, and re-layouts  5.82 us
    dynamic_slice x3, local copies, waits for them, and re-layouts, theirs(): return lax.dynamic_slice_in_dim(x, 256 - core * 256, 256, 1)  3.74 us
    ppermute x13, waiting for transfers between devices, swap(): return lax.ppermute(block, 'ctx', route)  2.8 us
    broadcast_in_dim x3, local copies, waits for them, and re-layouts, local(): jnp.repeat(jnp.where(fine, 0.0, -jnp.inf).astype(F32), CHIP >> level)[None]  2.05 us
  transfers between devices with their start and end apart: 19, of which 6 were waited for; matrix products, arithmetic and copies ran while one was open for 12% of the time, Pallas kernels for 10%

profile of v1, /device:TPU:1, one launch (start us, length us, event | category | flops | bytes accessed | tf_op | source)
XLA Modules:
  0.0 100.9 jit_solution(10803344981147401986)
XLA Ops:
  0.0 1.0 constant_dynamic-slice_fusion.1
  1.0 3.3 %collective-permute-start.1 = (bf16[512,256]{1,0:T(8,128)(2,1)S(1)}, bf16[512,256]{1,0:T(8,128)(2,1)S(1)}, u32[]{:S(2)}, u32[]{:S(2)}) collective-permute-start(bf16[512,256]{1,0:T(8,128)(2,1)S(1)} %constant_dynamic-slice_fusion.1), channel_id=1, source_target_pairs={{0,4},{4,0},{8,12},{12,8},{16,20},{20,16},{24,28},{28,24},{32,36},... | collective-permute-start | bytes 786440 | tf_op jit(solution)/shard_map/ppermute | solution.py:28
  4.3 1.0 %constant_dynamic-slice_fusion.2 = bf16[512,256]{1,0:T(8,128)(2,1)S(1)} fusion(bf16[512,512]{1,0:T(8,128)(2,1)} %v.3, s32[]{:T(128)S(6)} %select_n.58), kind=kLoop, calls=%fused_computation.15 | loop fusion | bytes 524292 | tf_op jit(solution)/shard_map/dynamic_slice | solution.py:221
  5.4 0.0 copy-start.2
  5.4 0.1 collective-permute-start.2
  5.5 1.7 %constant_dynamic-slice_fusion = bf16[512,256]{1,0:T(8,128)(2,1)} fusion(bf16[512,512]{1,0:T(8,128)(2,1)} %q.1, s32[]{:T(128)S(6)} %select_n.58), kind=kLoop, calls=%fused_computation.13 | loop fusion | bytes 524292 | tf_op jit(solution)/shard_map/dynamic_slice | solution.py:221
  7.2 0.4 collective-permute-start
  7.7 0.7 or_select_fusion
  8.3 0.1 pad_add_fusion.pos
  8.4 0.1 broadcast_bitcast_fusion
  8.5 0.0 collective-permute-done.1.rk
  8.5 0.0 collective-permute-done.2.rv
  8.5 1.0 %copy-done.1 = bf16[512,512]{1,0:T(8,128)(2,1)S(1)} copy-done((bf16[512,512]{1,0:T(8,128)(2,1)S(1)}, bf16[512,512]{1,0:T(8,128)(2,1)}, u32[]{:S(2)}) %copy-start.1) | copy-done | bytes 524312
  9.5 1.0 %copy-done.3 = bf16[512,512]{1,0:T(8,128)(2,1)S(1)} copy-done((bf16[512,512]{1,0:T(8,128)(2,1)S(1)}, bf16[512,512]{1,0:T(8,128)(2,1)}, u32[]{:S(2)}) %copy-start.3) | copy-done | bytes 524312
  10.6 0.7 copy-done.6
  11.3 1.0 %shard_map.92 = (bf16[192,256]{1,0:T(8,128)(2,1)S(1)}, bf16[256,256]{1,0:T(8,128)(2,1)S(1)}, bf16[512,256]{1,0:T(8,128)(2,1)S(1)}) custom-call(s32[4]{0:T(128)S(1)} %pad_add_fusion.pos, s32[6,16]{1,0:T(8,128)S(1)} %copy-done.6, bf16[512,512]{1,0:T(8,128)(2,1)S(1)} %copy-done.1, bf16[512,512]{1,0:T(8,128)(2,1)S(1)} %copy-done.3, ...), custom_call_target="tpu_custom_call" | custom-call | bytes 1572864 | tf_op jit(solution)/shard_map/pallas_call | solution.py:202
  12.3 0.1 collective-permute-start.3
  12.4 1.9 %collective-permute-start.4 = (bf16[192,256]{1,0:T(8,128)(2,1)S(1)}, bf16[192,256]{1,0:T(8,128)(2,1)S(1)}, u32[]{:S(2)}, u32[]{:S(2)}) collective-permute-start(bf16[192,256]{1,0:T(8,128)(2,1)S(1)} %get-tuple-element.23.o45), channel_id=1, source_target_pairs={{0,32},{4,36},{8,40},{12,44},{16,48},{20,52},{24,56},{28,60},{32,0... | collective-permute-start | bytes 294920 | tf_op jit(solution)/shard_map/ppermute | solution.py:28
  14.3 1.9 %collective-permute-start.5 = (bf16[192,256]{1,0:T(8,128)(2,1)S(1)}, bf16[192,256]{1,0:T(8,128)(2,1)S(1)}, u32[]{:S(2)}, u32[]{:S(2)}) collective-permute-start(bf16[192,256]{1,0:T(8,128)(2,1)S(1)} %get-tuple-element.23.o45), channel_id=1, source_target_pairs={{0,48},{4,52},{8,56},{12,60},{16,32},{20,36},{24,40},{28,44},{32,1... | collective-permute-start | bytes 294920 | tf_op jit(solution)/shard_map/ppermute | solution.py:28
  16.2 0.0 collective-permute-start.6
  16.3 0.5 or_select_fusion.1
  16.8 3.4 %collective-permute-start.7 = (bf16[512,256]{1,0:T(8,128)(2,1)S(1)}, bf16[512,256]{1,0:T(8,128)(2,1)S(1)}, u32[]{:S(2)}, u32[]{:S(2)}) collective-permute-start(bf16[512,256]{1,0:T(8,128)(2,1)S(1)} %get-tuple-element.25.o2), channel_id=1, source_target_pairs={{0,8},{4,12},{16,24},{20,28},{32,40},{36,44},{48,56},{52,60},{64,7... | collective-permute-start | bytes 786440 | tf_op jit(solution)/shard_map/ppermute | solution.py:28
  20.2 0.0 collective-permute-done.4.a1
  20.2 1.6 %collective-permute-done.5.a2 = bf16[192,256]{1,0:T(8,128)(2,1)S(1)} collective-permute-done((bf16[192,256]{1,0:T(8,128)(2,1)S(1)}, bf16[192,256]{1,0:T(8,128)(2,1)S(1)}, u32[]{:S(2)}, u32[]{:S(2)}) %collective-permute-start.5) | collective-permute-done | bytes 98336 | tf_op jit(solution)/shard_map/ppermute | solution.py:28
  21.8 0.8 pad_maximum_fusion.1
  22.5 1.6 %collective-permute-start.9 = (bf16[768,256]{1,0:T(8,128)(2,1)}, bf16[768,256]{1,0:T(8,128)(2,1)S(1)}, u32[]{:S(2)}, u32[]{:S(2)}) collective-permute-start(bf16[768,256]{1,0:T(8,128)(2,1)} %pad_maximum_fusion.1), channel_id=1, source_target_pairs={{0,8},{4,12},{8,0},{12,4},{16,24},{20,28},{24,16},{28,20},{32,40},... | collective-permute-start | bytes 1179656 | tf_op jit(solution)/shard_map/ppermute | solution.py:28
  24.2 0.0 collective-permute-done.6.b
  24.2 0.7 pad_maximum_fusion.2
  24.9 1.3 %collective-permute-start.8 = (bf16[512,256]{1,0:T(8,128)(2,1)}, bf16[512,256]{1,0:T(8,128)(2,1)S(1)}, u32[]{:S(2)}, u32[]{:S(2)}) collective-permute-start(bf16[512,256]{1,0:T(8,128)(2,1)} %pad_maximum_fusion.2), channel_id=1, source_target_pairs={{0,16},{4,20},{8,24},{12,28},{32,48},{36,52},{40,56},{44,60},{64,8... | collective-permute-start | bytes 786440 | tf_op jit(solution)/shard_map/ppermute | solution.py:28
  26.2 0.7 pad_maximum_fusion.3
  26.9 3.2 %collective-permute-start.10 = (bf16[256,256]{1,0:T(8,128)(2,1)}, bf16[256,256]{1,0:T(8,128)(2,1)S(1)}, u32[]{:S(2)}, u32[]{:S(2)}) collective-permute-start(bf16[256,256]{1,0:T(8,128)(2,1)} %pad_maximum_fusion.3), channel_id=1, source_target_pairs={{0,64},{4,68},{8,72},{12,76},{16,80},{20,84},{24,88},{28,92},{32,9... | collective-permute-start | bytes 393224 | tf_op jit(solution)/shard_map/ppermute | solution.py:28
  30.1 1.9 %collective-permute-start.11 = (bf16[256,256]{1,0:T(8,128)(2,1)}, bf16[256,256]{1,0:T(8,128)(2,1)}, u32[]{:S(2)}, u32[]{:S(2)}) collective-permute-start(bf16[256,256]{1,0:T(8,128)(2,1)} %pad_maximum_fusion.3), channel_id=1, source_target_pairs={{0,72},{4,76},{8,64},{12,68},{16,88},{20,92},{24,80},{28,84},{32,1... | collective-permute-start | bytes 393224 | tf_op jit(solution)/shard_map/ppermute | solution.py:28
  32.1 0.6 or_select_fusion.2
  32.6 0.1 broadcast_in_dim.59
  32.7 0.7 broadcast_in_dim_reshape.15
  33.4 0.7 broadcast_in_dim.56
  34.1 0.7 broadcast_in_dim_reshape.14
  34.7 0.6 copy.10
  35.3 1.3 %broadcast_in_dim.53 = f32[4,128]{1,0:T(4,128)} broadcast(f32[4]{0:T(128)} %or_select_fusion.2), dimensions={0} | broadcast | bytes 2064 | tf_op jit(solution)/shard_map/broadcast_in_dim | solution.py:254
  36.6 0.6 broadcast_in_dim.47
  37.2 0.7 concatenate.16.bias
  37.9 0.0 copy-start.5
  38.0 1.0 %copy-done.5 = bf16[512,512]{1,0:T(8,128)(2,1)S(1)} copy-done((bf16[512,512]{1,0:T(8,128)(2,1)S(1)}, bf16[512,512]{1,0:T(8,128)(2,1)}, u32[]{:S(2)}) %copy-start.5) | copy-done | bytes 524312
  39.0 0.7 copy-done.7
  39.7 0.6 copy-done.9
  40.3 7.3 %shard_map.91 = (f32[2,1024,128]{2,1,0:T(8,128)S(1)}, f32[2,1024,128]{2,1,0:T(8,128)S(1)}, bf16[960,128]{1,0:T(8,128)(2,1)S(1)}) custom-call(s32[4]{0:T(128)S(1)} %copy-done.9, s32[6,16]{1,0:T(8,128)S(1)} %copy-done.7, bf16[512,512]{1,0:T(8,128)(2,1)S(1)} %copy-done.5, bf16[512,512]{1,0:T(8,128)(2,1)S(1)} %copy-done.2, bf16[512,512]{1,0:T(8,128)(2,1)S(1)} %copy-done.4, ...), custom_call_target="tpu_custom_call" | custom-call | flops 805306368 | bytes 2359296 | tf_op jit(solution)/shard_map/pallas_call | solution.py:202
  47.7 0.0 copy-start
  47.7 5.7 %shard_map.93 = (bf16[512,256]{1,0:T(8,128)(2,1)S(1)}, bf16[512,256]{1,0:T(8,128)(2,1)S(1)}) custom-call(s32[4]{0:T(128)S(1)} %copy-done.9, s32[6,16]{1,0:T(8,128)S(1)} %copy-done.7, f32[6,512]{1,0:T(8,128)S(1)} %concatenate.16.bias, f32[2,1024,128]{2,1,0:T(8,128)S(1)} %get-tuple-element.20.acc0, f32[2,1024,128]{2,1,0:T(8,128)S(1)} %get-tuple-element.21.stat0, ...), custom_call_target="tpu_custom_call" | custom-call | flops 268435456 | bytes 4452352 | tf_op jit(solution)/shard_map/pallas_call | solution.py:202
  53.4 1.3 %collective-permute-start.12 = (bf16[512,256]{1,0:T(8,128)(2,1)S(1)}, bf16[512,256]{1,0:T(8,128)(2,1)S(1)}, u32[]{:S(2)}, u32[]{:S(2)}) collective-permute-start(bf16[512,256]{1,0:T(8,128)(2,1)S(1)} %get-tuple-element.27), channel_id=1, source_target_pairs={{0,4},{4,0},{8,12},{12,8},{16,20},{20,16},{24,28},{28,24},{32,36},... | collective-permute-start | bytes 786440 | tf_op jit(solution)/shard_map/ppermute | solution.py:28
  54.7 1.2 %collective-permute-done.12.back = bf16[512,256]{1,0:T(8,128)(2,1)S(1)} collective-permute-done((bf16[512,256]{1,0:T(8,128)(2,1)S(1)}, bf16[512,256]{1,0:T(8,128)(2,1)S(1)}, u32[]{:S(2)}, u32[]{:S(2)}) %collective-permute-start.12) | collective-permute-done | bytes 262176 | tf_op jit(solution)/shard_map/ppermute | solution.py:28
  55.9 1.0 shard_map.95
  56.8 5.6 %collective-permute-start.17 = (bf16[256,512]{1,0:T(8,128)(2,1)S(1)}, bf16[256,512]{1,0:T(8,128)(2,1)S(1)}, u32[]{:S(2)}, u32[]{:S(2)}) collective-permute-start(bf16[256,512]{1,0:T(8,128)(2,1)S(1)} %get-tuple-element.34), channel_id=1, source_target_pairs={{0,3},{1,0},{2,1},{3,2},{4,7},{5,4},{6,5},{7,6},{8,11},{9,8},{10,9... | collective-permute-start | bytes 786440 | tf_op jit(solution)/shard_map/ppermute | solution.py:32
  62.5 1.5 %shard_map.94 = (bf16[256,512]{1,0:T(8,128)(2,1)S(1)}, bf16[256,512]{1,0:T(8,128)(2,1)S(1)}, f32[256,512]{1,0:T(8,128)S(1)}, f32[256,512]{1,0:T(8,128)S(1)}, f32[512,512]{1,0:T(8,128)S(1)}) custom-call(s32[4]{0:T(128)S(1)} %copy-done.9, bf16[512,256]{1,0:T(8,128)(2,1)S(1)} %get-tuple-element.26.mine, bf16[512,256]{1,0:T(8,128)(2,1)S(1)} %collective-permute-done.12.back, ...), custom_call_target="tpu_custom_call" | custom-call | flops 805306368 | bytes 2621440 | tf_op jit(solution)/shard_map/pallas_call | solution.py:202
  64.0 3.6 %collective-permute-start.15 = (bf16[256,512]{1,0:T(8,128)(2,1)S(1)}, bf16[256,512]{1,0:T(8,128)(2,1)S(1)}, u32[]{:S(2)}, u32[]{:S(2)}) collective-permute-start(bf16[256,512]{1,0:T(8,128)(2,1)S(1)} %get-tuple-element.31), channel_id=1, source_target_pairs={{0,3},{1,0},{2,1},{3,2},{4,7},{5,4},{6,5},{7,6},{8,11},{9,8},{10,9... | collective-permute-start | bytes 786440 | tf_op jit(solution)/shard_map/ppermute | solution.py:32
  67.7 7.3 %collective-permute-done.17 = bf16[256,512]{1,0:T(8,128)(2,1)S(1)} collective-permute-done((bf16[256,512]{1,0:T(8,128)(2,1)S(1)}, bf16[256,512]{1,0:T(8,128)(2,1)S(1)}, u32[]{:S(2)}, u32[]{:S(2)}) %collective-permute-start.17) | collective-permute-done | bytes 262176 | tf_op jit(solution)/shard_map/ppermute | solution.py:32
  75.0 0.1 add_convert_fusion.1
  75.0 4.0 %collective-permute-start.18 = (bf16[256,512]{1,0:T(8,128)(2,1)S(1)}, bf16[256,512]{1,0:T(8,128)(2,1)S(1)}, u32[]{:S(2)}, u32[]{:S(2)}) collective-permute-start(bf16[256,512]{1,0:T(8,128)(2,1)S(1)} %add_convert_fusion.1), channel_id=1, source_target_pairs={{0,3},{1,0},{2,1},{3,2},{4,7},{5,4},{6,5},{7,6},{8,11},{9,8},{10,9... | collective-permute-start | bytes 786440 | tf_op jit(solution)/shard_map/ppermute | solution.py:32
  79.0 0.1 add_convert_fusion.3
  79.1 0.1 collective-permute-start.14
  79.2 9.6 %collective-permute-done.15 = bf16[256,512]{1,0:T(8,128)(2,1)S(1)} collective-permute-done((bf16[256,512]{1,0:T(8,128)(2,1)S(1)}, bf16[256,512]{1,0:T(8,128)(2,1)S(1)}, u32[]{:S(2)}, u32[]{:S(2)}) %collective-permute-start.15) | collective-permute-done | bytes 262176 | tf_op jit(solution)/shard_map/ppermute | solution.py:32
  88.8 5.7 %collective-permute-done.18 = bf16[256,512]{1,0:T(8,128)(2,1)S(1)} collective-permute-done((bf16[256,512]{1,0:T(8,128)(2,1)S(1)}, bf16[256,512]{1,0:T(8,128)(2,1)S(1)}, u32[]{:S(2)}, u32[]{:S(2)}) %collective-permute-start.18) | collective-permute-done | bytes 262176 | tf_op jit(solution)/shard_map/ppermute | solution.py:32
  94.4 5.4 %collective-permute-done.14 = bf16[256,512]{1,0:T(8,128)(2,1)S(1)} collective-permute-done((bf16[256,512]{1,0:T(8,128)(2,1)S(1)}, bf16[256,512]{1,0:T(8,128)(2,1)S(1)}, u32[]{:S(2)}, u32[]{:S(2)}) %collective-permute-start.14) | collective-permute-done | bytes 262176 | tf_op jit(solution)/shard_map/ppermute | solution.py:32
  99.9 0.2 add_convert_fusion.2
  100.1 0.8 pad_maximum_fusion
  (31 shorter events, 0.1 us)
Async XLA Ops:
  0.0 16.2 %copy-start.10 = (s32[8]{0:T(128)S(1)}, s32[8]{0:T(128)}, u32[]{:S(2)}) copy-start(s32[8]{0:T(128)} %constant.90.clone) | copy-start | bytes 100
  0.0 16.3 %copy-start.11 = (pred[8]{0:T(512)(128)(4,1)S(1)}, pred[8]{0:T(512)(128)(4,1)}, u32[]{:S(2)}) copy-start(pred[8]{0:T(512)(128)(4,1)} %constant.92) | copy-start | bytes 28
  1.0 7.5 %collective-permute-start.1 = (bf16[512,256]{1,0:T(8,128)(2,1)S(1)}, bf16[512,256]{1,0:T(8,128)(2,1)S(1)}, u32[]{:S(2)}, u32[]{:S(2)}) collective-permute-start(bf16[512,256]{1,0:T(8,128)(2,1)S(1)} %constant_dynamic-slice_fusion.1), channel_id=1, source_target_pairs={{0,4},{4,0},{8,12},{12,8},{16,20},{20,16},{24,28},{28,24},{32,36},... | collective-permute-start | bytes 786440 | tf_op jit(solution)/shard_map/ppermute | solution.py:28
  4.3 33.6 %copy-start.4 = (bf16[512,512]{1,0:T(8,128)(2,1)S(1)}, bf16[512,512]{1,0:T(8,128)(2,1)}, u32[]{:S(2)}) copy-start(bf16[512,512]{1,0:T(8,128)(2,1)} %v.3) | copy-start | bytes 1572868
  5.4 32.6 %copy-start.2 = (bf16[512,512]{1,0:T(8,128)(2,1)S(1)}, bf16[512,512]{1,0:T(8,128)(2,1)}, u32[]{:S(2)}) copy-start(bf16[512,512]{1,0:T(8,128)(2,1)} %k.3) | copy-start | bytes 1572868
  5.4 3.1 %collective-permute-start.2 = (bf16[512,256]{1,0:T(8,128)(2,1)S(1)}, bf16[512,256]{1,0:T(8,128)(2,1)S(1)}, u32[]{:S(2)}, u32[]{:S(2)}) collective-permute-start(bf16[512,256]{1,0:T(8,128)(2,1)S(1)} %constant_dynamic-slice_fusion.2), channel_id=1, source_target_pairs={{0,4},{4,0},{8,12},{12,8},{16,20},{20,16},{24,28},{28,24},{32,36},... | collective-permute-start | bytes 786440 | tf_op jit(solution)/shard_map/ppermute | solution.py:28
  7.2 22.9 %collective-permute-start = (bf16[512,256]{1,0:T(8,128)(2,1)}, bf16[512,256]{1,0:T(8,128)(2,1)}, u32[]{:S(2)}, u32[]{:S(2)}) collective-permute-start(bf16[512,256]{1,0:T(8,128)(2,1)} %constant_dynamic-slice_fusion), channel_id=1, source_target_pairs={{0,4},{4,0},{8,12},{12,8},{16,20},{20,16},{24,28},{28,24},{32,36},... | collective-permute-start | bytes 786440 | tf_op jit(solution)/shard_map/ppermute | solution.py:28
  8.4 3.9 %copy-start.8 = (s32[4]{0:T(128)}, s32[4]{0:T(128)S(1)}, u32[]{:S(2)}) copy-start(s32[4]{0:T(128)S(1)} %pad_add_fusion.pos) | copy-start | bytes 52
  8.5 1.0 %copy-start.1 = (bf16[512,512]{1,0:T(8,128)(2,1)S(1)}, bf16[512,512]{1,0:T(8,128)(2,1)}, u32[]{:S(2)}) copy-start(bf16[512,512]{1,0:T(8,128)(2,1)} %k.3) | copy-start | bytes 1572868
  9.5 1.0 %copy-start.3 = (bf16[512,512]{1,0:T(8,128)(2,1)S(1)}, bf16[512,512]{1,0:T(8,128)(2,1)}, u32[]{:S(2)}) copy-start(bf16[512,512]{1,0:T(8,128)(2,1)} %v.3) | copy-start | bytes 1572868
  10.6 0.7 copy-start.6
  12.3 4.5 %collective-permute-start.3 = (bf16[192,256]{1,0:T(8,128)(2,1)S(1)}, bf16[192,256]{1,0:T(8,128)(2,1)S(1)}, u32[]{:S(2)}, u32[]{:S(2)}) collective-permute-start(bf16[192,256]{1,0:T(8,128)(2,1)S(1)} %get-tuple-element.23.o45), channel_id=1, source_target_pairs={{0,16},{4,20},{8,24},{12,28},{16,0},{20,4},{24,8},{28,12},{32,48},... | collective-permute-start | bytes 294920 | tf_op jit(solution)/shard_map/ppermute | solution.py:28
  12.4 7.8 %collective-permute-start.4 = (bf16[192,256]{1,0:T(8,128)(2,1)S(1)}, bf16[192,256]{1,0:T(8,128)(2,1)S(1)}, u32[]{:S(2)}, u32[]{:S(2)}) collective-permute-start(bf16[192,256]{1,0:T(8,128)(2,1)S(1)} %get-tuple-element.23.o45), channel_id=1, source_target_pairs={{0,32},{4,36},{8,40},{12,44},{16,48},{20,52},{24,56},{28,60},{32,0... | collective-permute-start | bytes 294920 | tf_op jit(solution)/shard_map/ppermute | solution.py:28
  14.3 7.5 %collective-permute-start.5 = (bf16[192,256]{1,0:T(8,128)(2,1)S(1)}, bf16[192,256]{1,0:T(8,128)(2,1)S(1)}, u32[]{:S(2)}, u32[]{:S(2)}) collective-permute-start(bf16[192,256]{1,0:T(8,128)(2,1)S(1)} %get-tuple-element.23.o45), channel_id=1, source_target_pairs={{0,48},{4,52},{8,56},{12,60},{16,32},{20,36},{24,40},{28,44},{32,1... | collective-permute-start | bytes 294920 | tf_op jit(solution)/shard_map/ppermute | solution.py:28
  16.2 8.0 %collective-permute-start.6 = (bf16[256,256]{1,0:T(8,128)(2,1)S(1)}, bf16[256,256]{1,0:T(8,128)(2,1)S(1)}, u32[]{:S(2)}, u32[]{:S(2)}) collective-permute-start(bf16[256,256]{1,0:T(8,128)(2,1)S(1)} %get-tuple-element.24.o3), channel_id=1, source_target_pairs={{0,8},{4,12},{8,0},{12,4},{16,24},{20,28},{24,16},{28,20},{32,40},... | collective-permute-start | bytes 393224 | tf_op jit(solution)/shard_map/ppermute | solution.py:28
  16.8 30.8 %collective-permute-start.7 = (bf16[512,256]{1,0:T(8,128)(2,1)S(1)}, bf16[512,256]{1,0:T(8,128)(2,1)S(1)}, u32[]{:S(2)}, u32[]{:S(2)}) collective-permute-start(bf16[512,256]{1,0:T(8,128)(2,1)S(1)} %get-tuple-element.25.o2), channel_id=1, source_target_pairs={{0,8},{4,12},{16,24},{20,28},{32,40},{36,44},{48,56},{52,60},{64,7... | collective-permute-start | bytes 786440 | tf_op jit(solution)/shard_map/ppermute | solution.py:28
  22.5 25.1 %collective-permute-start.9 = (bf16[768,256]{1,0:T(8,128)(2,1)}, bf16[768,256]{1,0:T(8,128)(2,1)S(1)}, u32[]{:S(2)}, u32[]{:S(2)}) collective-permute-start(bf16[768,256]{1,0:T(8,128)(2,1)} %pad_maximum_fusion.1), channel_id=1, source_target_pairs={{0,8},{4,12},{8,0},{12,4},{16,24},{20,28},{24,16},{28,20},{32,40},... | collective-permute-start | bytes 1179656 | tf_op jit(solution)/shard_map/ppermute | solution.py:28
  24.9 22.7 %collective-permute-start.8 = (bf16[512,256]{1,0:T(8,128)(2,1)}, bf16[512,256]{1,0:T(8,128)(2,1)S(1)}, u32[]{:S(2)}, u32[]{:S(2)}) collective-permute-start(bf16[512,256]{1,0:T(8,128)(2,1)} %pad_maximum_fusion.2), channel_id=1, source_target_pairs={{0,16},{4,20},{8,24},{12,28},{32,48},{36,52},{40,56},{44,60},{64,8... | collective-permute-start | bytes 786440 | tf_op jit(solution)/shard_map/ppermute | solution.py:28
  26.9 20.7 %collective-permute-start.10 = (bf16[256,256]{1,0:T(8,128)(2,1)}, bf16[256,256]{1,0:T(8,128)(2,1)S(1)}, u32[]{:S(2)}, u32[]{:S(2)}) collective-permute-start(bf16[256,256]{1,0:T(8,128)(2,1)} %pad_maximum_fusion.3), channel_id=1, source_target_pairs={{0,64},{4,68},{8,72},{12,76},{16,80},{20,84},{24,88},{28,92},{32,9... | collective-permute-start | bytes 393224 | tf_op jit(solution)/shard_map/ppermute | solution.py:28
  30.1 17.5 %collective-permute-start.11 = (bf16[256,256]{1,0:T(8,128)(2,1)}, bf16[256,256]{1,0:T(8,128)(2,1)}, u32[]{:S(2)}, u32[]{:S(2)}) collective-permute-start(bf16[256,256]{1,0:T(8,128)(2,1)} %pad_maximum_fusion.3), channel_id=1, source_target_pairs={{0,72},{4,76},{8,64},{12,68},{16,88},{20,92},{24,80},{28,84},{32,1... | collective-permute-start | bytes 393224 | tf_op jit(solution)/shard_map/ppermute | solution.py:28
  37.9 1.0 %copy-start.5 = (bf16[512,512]{1,0:T(8,128)(2,1)S(1)}, bf16[512,512]{1,0:T(8,128)(2,1)}, u32[]{:S(2)}) copy-start(bf16[512,512]{1,0:T(8,128)(2,1)} %q.1) | copy-start | bytes 1572868
  39.0 0.7 copy-start.7
  39.7 0.6 copy-start.9
  47.7 8.2 %copy-start = (bf16[512,2048]{1,0:T(8,128)(2,1)S(1)}, bf16[512,2048]{1,0:T(8,128)(2,1)}, u32[]{:S(2)}) copy-start(bf16[512,2048]{1,0:T(8,128)(2,1)} %w.3) | copy-start | bytes 6291460
  53.4 2.5 %collective-permute-start.12 = (bf16[512,256]{1,0:T(8,128)(2,1)S(1)}, bf16[512,256]{1,0:T(8,128)(2,1)S(1)}, u32[]{:S(2)}, u32[]{:S(2)}) collective-permute-start(bf16[512,256]{1,0:T(8,128)(2,1)S(1)} %get-tuple-element.27), channel_id=1, source_target_pairs={{0,4},{4,0},{8,12},{12,8},{16,20},{20,16},{24,28},{28,24},{32,36},... | collective-permute-start | bytes 786440 | tf_op jit(solution)/shard_map/ppermute | solution.py:28
  56.8 18.1 %collective-permute-start.17 = (bf16[256,512]{1,0:T(8,128)(2,1)S(1)}, bf16[256,512]{1,0:T(8,128)(2,1)S(1)}, u32[]{:S(2)}, u32[]{:S(2)}) collective-permute-start(bf16[256,512]{1,0:T(8,128)(2,1)S(1)} %get-tuple-element.34), channel_id=1, source_target_pairs={{0,3},{1,0},{2,1},{3,2},{4,7},{5,4},{6,5},{7,6},{8,11},{9,8},{10,9... | collective-permute-start | bytes 786440 | tf_op jit(solution)/shard_map/ppermute | solution.py:32
  62.5 16.5 %collective-permute-start.13 = (bf16[256,512]{1,0:T(8,128)(2,1)S(1)}, bf16[256,512]{1,0:T(8,128)(2,1)S(1)}, u32[]{:S(2)}, u32[]{:S(2)}) collective-permute-start(bf16[256,512]{1,0:T(8,128)(2,1)S(1)} %get-tuple-element.30), channel_id=1, source_target_pairs={{0,1},{1,2},{2,3},{3,0},{4,5},{5,6},{6,7},{7,4},{8,9},{9,10},{10,1... | collective-permute-start | bytes 786440 | tf_op jit(solution)/shard_map/ppermute | solution.py:32
  64.0 24.7 %collective-permute-start.15 = (bf16[256,512]{1,0:T(8,128)(2,1)S(1)}, bf16[256,512]{1,0:T(8,128)(2,1)S(1)}, u32[]{:S(2)}, u32[]{:S(2)}) collective-permute-start(bf16[256,512]{1,0:T(8,128)(2,1)S(1)} %get-tuple-element.31), channel_id=1, source_target_pairs={{0,3},{1,0},{2,1},{3,2},{4,7},{5,4},{6,5},{7,6},{8,11},{9,8},{10,9... | collective-permute-start | bytes 786440 | tf_op jit(solution)/shard_map/ppermute | solution.py:32
  67.7 21.1 %collective-permute-start.16 = (bf16[256,512]{1,0:T(8,128)(2,1)S(1)}, bf16[256,512]{1,0:T(8,128)(2,1)S(1)}, u32[]{:S(2)}, u32[]{:S(2)}) collective-permute-start(bf16[256,512]{1,0:T(8,128)(2,1)S(1)} %get-tuple-element.32), channel_id=1, source_target_pairs={{0,1},{1,2},{2,3},{3,0},{4,5},{5,6},{6,7},{7,4},{8,9},{9,10},{10,1... | collective-permute-start | bytes 786440 | tf_op jit(solution)/shard_map/ppermute | solution.py:32
  75.0 19.4 %collective-permute-start.18 = (bf16[256,512]{1,0:T(8,128)(2,1)S(1)}, bf16[256,512]{1,0:T(8,128)(2,1)S(1)}, u32[]{:S(2)}, u32[]{:S(2)}) collective-permute-start(bf16[256,512]{1,0:T(8,128)(2,1)S(1)} %add_convert_fusion.1), channel_id=1, source_target_pairs={{0,3},{1,0},{2,1},{3,2},{4,7},{5,4},{6,5},{7,6},{8,11},{9,8},{10,9... | collective-permute-start | bytes 786440 | tf_op jit(solution)/shard_map/ppermute | solution.py:32
  79.1 20.8 %collective-permute-start.14 = (bf16[256,512]{1,0:T(8,128)(2,1)S(1)}, bf16[256,512]{1,0:T(8,128)(2,1)S(1)}, u32[]{:S(2)}, u32[]{:S(2)}) collective-permute-start(bf16[256,512]{1,0:T(8,128)(2,1)S(1)} %add_convert_fusion.3), channel_id=1, source_target_pairs={{0,1},{1,2},{2,3},{3,0},{4,5},{5,6},{6,7},{7,4},{8,9},{9,10},{10,1... | collective-permute-start | bytes 786440 | tf_op jit(solution)/shard_map/ppermute | solution.py:32

commit v2 on v1

v2 whole, which is shorter than its diff:
```python
import math

import jax
import jax.numpy as jnp
from jax import lax
from jax.experimental import pallas as pl
from jax.experimental.pallas import tpu as pltpu
from jax.sharding import PartitionSpec as P

HD = 128
F32 = jnp.float32
BF16 = jnp.bfloat16
TOK = 512
CHIP = 2 * TOK
GAIN = math.log2(math.e) / math.sqrt(HD)
CORE, Z, X1, X2, Y1 = 1, 2, 4, 8, 16


def swap(block, bits):
    return lax.ppermute(block, "ctx", [(i, i ^ bits) for i in range(64)])


def cross(block, bits):
    return lax.ppermute(block, "head", [(i, i ^ bits) for i in range(4)])


def used(off, level, first=0, count=None):
    r = 1 << level
    n = CHIP // r if count is None else count
    return pl.ds(off + first * r, n, stride=r)


def halves(pos):
    here = pl.multiple_of(pos[0] * TOK, TOK)
    there = pl.multiple_of(TOK - pos[0] * TOK, TOK)
    return pl.ds(here, TOK), pl.ds(there, TOK)


def split_kernel(pos, q, k, v, okv, oq, mkv, mq, sems):
    mine = pl.ds(pl.multiple_of(pos[0] * 256, 256), 256)
    theirs = pl.ds(pl.multiple_of(256 - pos[0] * 256, 256), 256)
    moves = (
        (k, theirs, okv.at[0]),
        (v, theirs, okv.at[1]),
        (q, theirs, oq),
        (k, mine, mkv.at[0]),
        (v, mine, mkv.at[1]),
        (q, mine, mq),
    )
    copies = [
        pltpu.make_async_copy(src.at[:, cols], dst, sems.at[i])
        for i, (src, cols, dst) in enumerate(moves)
    ]
    for copy in copies:
        copy.start()
    for copy in copies:
        copy.wait()


def fill(buf, base, pos, mine, theirs):
    here, there = halves(pos)
    for j in range(2):
        cols = slice(j * HD, (j + 1) * HD)
        buf[base + j, here, :] = mine[:, cols].astype(F32)
        buf[base + j, there, :] = theirs[:, cols].astype(F32)


def pick_kernel(pos, offs, mkv, rkv, after, g45, g345, g32, buf):
    del after
    for i in range(2):
        fill(buf, 2 * i, pos, mkv.at[i], rkv.at[i])
    places = {5: ((g45, 0), (g345, 0)), 4: ((g45, 64), (g345, 64)), 3: ((g345, 192), (g32, 0)), 2: ((g32, 256),)}
    for level, where in places.items():
        n = CHIP >> level
        for j in range(2):
            rows = used(offs[level, pos[1] + j], level)
            for i in range(2):
                part = buf[2 * i + j, rows, :].astype(BF16)
                for dst, row in where:
                    dst[row + j * n : row + (j + 1) * n, i * HD : (i + 1) * HD] = part


def softmax_parts(scores, values):
    peak = jnp.max(scores, axis=-1, keepdims=True)
    expo = jnp.exp2((scores - peak) * GAIN)
    total = jnp.sum(expo, axis=-1, keepdims=True)
    mixed = jnp.dot(expo.astype(BF16), values, preferred_element_type=F32)
    return peak, total, mixed


def raw_scores(q, k):
    return lax.dot_general(q, k, (((1,), (1,)), ((), ())), preferred_element_type=F32)


def causal(q, k, v, half):
    n = q.shape[0]
    row = lax.broadcasted_iota(jnp.int32, (n, n), 0)
    col = lax.broadcasted_iota(jnp.int32, (n, n), 1)
    s = jnp.where(col <= row, raw_scores(q, k[half * n : (half + 1) * n]), -jnp.inf)
    if half:
        s = jnp.concatenate([raw_scores(q, k[:n]), s], axis=1)
    return softmax_parts(s, v[: (half + 1) * n])


def pack(peak, total):
    lane = lax.broadcasted_iota(jnp.int32, (peak.shape[0], HD), 1)
    return jnp.where(lane < HD // 2, peak, total)


def merge(acc, stat, j, rows, peak, total, mixed):
    old = stat[j, rows, :]
    old_peak, old_total = old[:, :1], old[:, HD // 2 : HD // 2 + 1]
    top = jnp.maximum(old_peak, peak)
    a = jnp.exp2((old_peak - top) * GAIN)
    b = jnp.exp2((peak - top) * GAIN)
    acc[j, rows, :] = acc[j, rows, :] * a + mixed * b
    stat[j, rows, :] = pack(top, old_total * a + total * b)


def tile_kernel(q, kv, after, acc, stat):
    del after
    for j in range(2):
        cols = slice(j * HD, (j + 1) * HD)
        for half in range(2):
            at = slice(half * 256, half * 256 + 256)
            peak, total, mixed = causal(q[at, cols], kv[0, :, cols], kv[1, :, cols], half)
            acc[j, at, :] = mixed
            stat[j, at, :] = pack(peak, total)


def regroup_kernel(g45, a0, a1, a2, zb, after, e, g5, d):
    del after
    for i, part in enumerate((g45, a0, a1, a2)):
        e[192 * i : 192 * (i + 1), :] = part[:192, :]
        g5[64 * i : 64 * (i + 1), :] = part[:64, :]
    d[...] = zb[:256, :]


def far_scores(pos, q, keys, level):
    n = q.shape[0]
    span = lax.rem(pos[2], 1 << (level - 1))
    block = lax.broadcasted_iota(jnp.int32, (1, TOK), 1) // n
    if level <= 3:
        code = block
    else:
        code = ((block & 3) << 1) | ((block >> 2) & 1) | (block & 8)
    bias = jnp.where((block == 0) | ((span ^ code) < span), 0.0, -jnp.inf)
    s = raw_scores(q, keys) + bias
    row = lax.broadcasted_iota(jnp.int32, s.shape, 0)
    col = lax.broadcasted_iota(jnp.int32, s.shape, 1)
    return jnp.where((col < n) & (col > row), -jnp.inf, s)


def far_level(pos, offs, acc, stat, level, j, q, parts):
    keys = jnp.concatenate([x[:, :HD] for x in parts], axis=0)
    values = jnp.concatenate([x[:, HD:] for x in parts], axis=0)
    part = softmax_parts(far_scores(pos, q, keys, level), values)
    merge(acc, stat, j, used(offs[level, pos[1] + j], level), *part)


def near_kernel(pos, offs, mq, mkv, rq, rkv, acc_m, stat_m, acc_r, stat_r, g32, zb, after, acc, stat, bq, buf):
    del after
    fill(buf, 0, pos, mq, rq)
    for i in range(2):
        fill(buf, 2 + 2 * i, pos, mkv.at[i], rkv.at[i])
    here, there = halves(pos)
    for j in range(2):
        acc[j, here, :] = acc_m[j]
        acc[j, there, :] = acc_r[j]
        stat[j, here, :] = stat_m[j]
        stat[j, there, :] = stat_r[j]
    row = 0
    for level in (5, 4, 3):
        n = CHIP >> level
        for j in range(2):
            bq[row : row + n, :] = buf[j, used(offs[level, pos[1] + j], level), :].astype(BF16)
            row += n
    for j in range(2):
        off = offs[1, pos[1] + j]
        qs, ks, vs = (buf[2 * i + j, used(off, 1), :].astype(BF16) for i in range(3))
        for half in range(2):
            part = causal(qs[half * 256 : half * 256 + 256], ks, vs, half)
            merge(acc, stat, j, used(off, 1, half * 256, 256), *part)
    for j in range(2):
        at = slice(256 + j * 256, 512 + j * 256)
        q = buf[j, used(offs[2, pos[1] + j], 2), :].astype(BF16)
        far_level(pos, offs, acc, stat, 2, j, q, [g32[at], zb[at]])


def far_kernel(pos, offs, acc0, stat0, bq, g45, g32, a0, a1, a2, zb, d, e, f, g, mine, other, acc, stat):
    acc[...] = acc0[...]
    stat[...] = stat0[...]
    quad = (g45, a0, a1, a2)
    for level in (3, 4, 5):
        n = CHIP >> level
        qrow = {5: 0, 4: 64, 3: 192}[level]
        for j in range(2):
            at = slice(j * n, (j + 1) * n)
            if level == 3:
                parts = [g32[at], zb[at], a0[192 + j * n : 192 + (j + 1) * n], d[at]]
            else:
                s = 64 if level == 4 else 0
                at = slice(s + j * n, s + (j + 1) * n)
                parts = [x[at] for x in quad]
                parts += [e[192 * i + s + j * n : 192 * i + s + (j + 1) * n] for i in range(4)]
                if level == 5:
                    for y in (f, g):
                        parts += [y[64 * i + j * n : 64 * i + (j + 1) * n] for i in range(4)]
            q = bq[qrow + j * n : qrow + (j + 1) * n, :]
            far_level(pos, offs, acc, stat, level, j, q, parts)
    here, there = halves(pos)
    for rows, dst in ((there, other), (here, mine)):
        for j in range(2):
            total = stat[j, rows, :][:, HD // 2 : HD // 2 + 1]
            dst[:, j * HD : (j + 1) * HD] = (acc[j, rows, :] / total).astype(BF16)


def project(pos, mine, back, w, first, dest):
    cols = pl.ds(pl.multiple_of(dest * TOK, TOK), TOK)
    near = pl.ds(pl.multiple_of(pos[0] * 256, 256), 256)
    far = pl.ds(pl.multiple_of(256 - pos[0] * 256, 256), 256)
    rows = slice(first, first + 256)
    return jnp.dot(mine[rows, :], w[near, cols], preferred_element_type=F32) + jnp.dot(
        back[rows, :], w[far, cols], preferred_element_type=F32
    )


def opposite_kernel(pos, mine, back, w, up, down):
    up[...] = project(pos, mine, back, w, 0, pos[3] ^ 2).astype(BF16)
    down[...] = project(pos, mine, back, w, 256, pos[3] ^ 2).astype(BF16)


def rest_kernel(pos, mine, back, w, after, up, down, up_late, down_late, own):
    del after
    up[...] = project(pos, mine, back, w, 0, pos[3] ^ 1).astype(BF16)
    down[...] = project(pos, mine, back, w, 256, pos[3] ^ 3).astype(BF16)
    up_late[...] = project(pos, mine, back, w, 0, pos[3] ^ 3)
    down_late[...] = project(pos, mine, back, w, 256, pos[3] ^ 1)
    for first in (0, 256):
        own[first : first + 256, :] = project(pos, mine, back, w, first, pos[3])


def relay_kernel(late, came, out):
    out[...] = (late[...] + came[...].astype(F32)).astype(BF16)


def final_kernel(own, up2, up3, down2, down3, out):
    out[:256, :] = (own[:256, :] + up2[...].astype(F32) + up3[...].astype(F32)).astype(BF16)
    out[256:, :] = (own[256:, :] + down2[...].astype(F32) + down3[...].astype(F32)).astype(BF16)


SMEM = pl.BlockSpec(memory_space=pltpu.SMEM)
VMEM = pl.BlockSpec(memory_space=pltpu.VMEM)
ANY = pl.BlockSpec(memory_space=pl.ANY)


def call(kernel, scalars, arrays, outs, scratch=(), flops=0, exps=0, unread=(), anywhere=False):
    nbytes = sum(a.size * a.dtype.itemsize for a in arrays)
    shapes = [s if not isinstance(s, tuple) else pltpu.VMEM(s, F32) for s in scratch]
    return pl.pallas_call(
        kernel,
        in_specs=[SMEM] * len(scalars)
        + [ANY if anywhere else VMEM] * len(arrays)
        + [ANY] * len(unread),
        out_specs=[VMEM] * len(outs),
        out_shape=[jax.ShapeDtypeStruct(s, t) for s, t in outs],
        scratch_shapes=shapes,
        compiler_params=pltpu.CompilerParams(vmem_limit_bytes=24 * 1024 * 1024),
        cost_estimate=pl.CostEstimate(flops=flops, bytes_accessed=nbytes, transcendentals=exps),
    )(*scalars, *arrays, *unread)


def local(q, k, v, offsets, w):
    ctx = lax.axis_index("ctx")
    head = lax.axis_index("head")
    core = ctx % 2
    pos = jnp.stack([core, head * 4 + core * 2, ctx // 2, head]).astype(jnp.int32)
    unit = 4 * TOK * TOK * HD
    part = (TOK, 256)
    state = (2, TOK, HD)

    okv, oq, mkv, mq = call(
        split_kernel,
        (pos,),
        (q, k, v),
        [((2,) + part, BF16), (part, BF16)] * 2,
        [pltpu.SemaphoreType.DMA((6,))],
        anywhere=True,
    )
    rkv, rq = swap(okv, CORE), swap(oq, CORE)
    acc_m, stat_m = call(tile_kernel, (), (mq, mkv), [(state, F32)] * 2, flops=2 * unit, unread=(oq,))
    g45, g345, g32 = call(
        pick_kernel,
        (pos, offsets),
        (mkv, rkv),
        [((192, 256), BF16), ((448, 256), BF16), ((768, 256), BF16)],
        [(4, CHIP, HD)],
        unread=(acc_m,),
    )
    zb = swap(g32, Z)
    a0, a1, a2 = swap(g345, X1), swap(g45, X2), swap(g45, X1 | X2)
    acc_r, stat_r = call(tile_kernel, (), (rq, rkv), [(state, F32)] * 2, flops=2 * unit, unread=(g45,))
    e, g5, d = call(
        regroup_kernel,
        (),
        (g45, a0, a1, a2, zb),
        [((768, 256), BF16), ((256, 256), BF16), ((256, 256), BF16)],
        unread=(acc_r,),
    )
    far_e, far_f, far_g, far_d = swap(e, Z), swap(g5, Y1), swap(g5, Y1 | Z), swap(d, X1)
    acc, stat, bq = call(
        near_kernel,
        (pos, offsets),
        (mq, mkv, rq, rkv, acc_m, stat_m, acc_r, stat_r, g32, zb),
        [((2, CHIP, HD), F32), ((2, CHIP, HD), F32), ((448, HD), BF16)],
        [(6, CHIP, HD)],
        flops=3 * unit,
        unread=(g5,),
    )
    mine, other = call(
        far_kernel,
        (pos, offsets),
        (acc, stat, bq, g45, g32, a0, a1, a2, zb, far_d, far_e, far_f, far_g),
        [(part, BF16)] * 2,
        [(2, CHIP, HD), (2, CHIP, HD)],
        flops=unit,
    )
    back = swap(other, CORE)

    half = (256, TOK)
    up1, down1 = call(opposite_kernel, (pos,), (mine, back, w), [(half, BF16)] * 2, flops=2 * TOK**3)
    came_up, came_down = cross(up1, 1), cross(down1, 3)
    up2, down2, up_late, down_late, own = call(
        rest_kernel,
        (pos,),
        (mine, back, w),
        [(half, BF16)] * 2 + [(half, F32)] * 2 + [((TOK, TOK), F32)],
        flops=6 * TOK**3,
        unread=(up1,),
    )
    up2, down2 = cross(up2, 1), cross(down2, 3)
    up3 = cross(call(relay_kernel, (), (up_late, came_up), [(half, BF16)])[0], 3)
    down3 = cross(call(relay_kernel, (), (down_late, came_down), [(half, BF16)])[0], 1)
    return call(final_kernel, (), (own, up2, up3, down2, down3), [((TOK, TOK), BF16)])[0]


def solution(mesh):
    placed = (P("ctx", "head"), P("ctx", "head"), P("ctx", "head"), P(), P("head", None))
    return jax.shard_map(
        local, mesh=mesh, in_specs=placed, out_specs=P("ctx", "head"), check_vma=False
    )
```

time: 101 us -> 85.2 us (0.84)
  local copies, waits for them, and re-layouts: 14.2 us -> 3.13 us
  starting transfers between devices: 33.9 us -> 23 us
  waiting for transfers between devices: 30.7 us -> 40.6 us
  other arithmetic: 5.23 us -> 0.08 us
  Pallas kernels: 16.5 us -> 17.8 us
    ppermute x19 -> x17, starting transfers between devices: 33.9 us -> 23 us  [the longest x11 12.1 us: swap(): return lax.ppermute(block, 'ctx', [(i, i ^ bits) for i in range(64)])]
    ppermute x19 -> x17, waiting for transfers between devices: 30.7 us -> 40.6 us  [the longest x6 27.8 us: cross(): return lax.ppermute(block, 'head', [(i, i ^ bits) for i in range(4)])]
    dynamic_slice x3 -> x0, local copies, waits for them, and re-layouts: 3.74 us -> none  [theirs(): return lax.dynamic_slice_in_dim(x, 256 - core * 256, 256, 1)]
    concatenate x4 -> x0, other arithmetic: 2.99 us -> none  [the longest x1 0.83 us: local(): return jnp.concatenate([top, bottom]).astype(BF16)]
    unnamed x26 -> x10, local copies, waits for them, and re-layouts: 5.82 us -> 3.13 us
    broadcast_in_dim x4 -> x0, local copies, waits for them, and re-layouts: 2.64 us -> none  [the longest x3 2.05 us: local(): jnp.repeat(jnp.where(fine, 0.0, -jnp.inf).astype(F32), CHIP >> level)[None]]
    select_n x4 -> x0, other arithmetic: 1.79 us -> none  [local(): jnp.where(fine, 0.0, -jnp.inf).astype(F32)]
    another operation x2 -> x0, local copies, waits for them, and re-layouts: 1.33 us -> none  [local(): jnp.repeat(jnp.where(fine, 0.0, -jnp.inf).astype(F32), CHIP >> level)[None]]
  transfers between devices with their start and end apart: 19 -> 17, of which waited for: 6 -> 8; matrix products, arithmetic and copies ran while one was open for 12% -> 0% of each run, Pallas kernels for 10% -> 12%
where the time goes in v2:
time: 85.2 us; the launch traced here: 84.7 us
  waiting for transfers between devices  40.6 us (48%)
  starting transfers between devices  23 us (27%)
  Pallas kernels  17.8 us (21%)
  local copies, waits for them, and re-layouts  3.13 us (4%)
    ppermute x6, waiting for transfers between devices, cross(): return lax.ppermute(block, 'head', [(i, i ^ bits) for i in range(4)])  27.8 us
    pallas_call x12, Pallas kernels, call(): pl.pallas_call(kernel, in_specs=[SMEM] * len(scalars) + [ANY if anywhere...  17.8 us
    ppermute x11, waiting for transfers between devices, swap(): return lax.ppermute(block, 'ctx', [(i, i ^ bits) for i in range(64)])  12.8 us
    ppermute x11, starting transfers between devices, swap(): return lax.ppermute(block, 'ctx', [(i, i ^ bits) for i in range(64)])  12.1 us
    ppermute x6, starting transfers between devices, cross(): return lax.ppermute(block, 'head', [(i, i ^ bits) for i in range(4)])  10.9 us
    unnamed x10, local copies, waits for them, and re-layouts  3.13 us
  transfers between devices with their start and end apart: 17, of which 8 were waited for; matrix products, arithmetic and copies ran while one was open for 0% of the time, Pallas kernels for 12%

profile of v2, /device:TPU:1, one launch (start us, length us, event | category | flops | bytes accessed | tf_op | source)
XLA Modules:
  0.0 84.7 jit_solution(6530049441277442843)
XLA Ops:
  0.0 0.0 copy-start.4
  0.0 0.1 pad_add_fusion.pos
  0.1 0.0 copy-start.1
  0.1 1.0 %copy-done.1 = bf16[512,512]{1,0:T(8,128)(2,1)S(1)} copy-done((bf16[512,512]{1,0:T(8,128)(2,1)S(1)}, bf16[512,512]{1,0:T(8,128)(2,1)}, u32[]{:S(2)}) %copy-start.1) | copy-done | bytes 524312
  1.1 0.0 copy-start.2
  1.1 1.0 %copy-done.2 = bf16[512,512]{1,0:T(8,128)(2,1)S(1)} copy-done((bf16[512,512]{1,0:T(8,128)(2,1)S(1)}, bf16[512,512]{1,0:T(8,128)(2,1)}, u32[]{:S(2)}) %copy-start.2) | copy-done | bytes 524312
  2.2 0.0 copy-start.3
  2.2 1.0 %copy-done.3 = bf16[512,512]{1,0:T(8,128)(2,1)S(1)} copy-done((bf16[512,512]{1,0:T(8,128)(2,1)S(1)}, bf16[512,512]{1,0:T(8,128)(2,1)}, u32[]{:S(2)}) %copy-start.3) | copy-done | bytes 524312
  3.2 0.7 shard_map.55
  3.9 3.3 %collective-permute-start.1 = (bf16[2,512,256]{2,1,0:T(8,128)(2,1)S(1)}, bf16[2,512,256]{2,1,0:T(8,128)(2,1)S(1)}, u32[]{:S(2)}, u32[]{:S(2)}) collective-permute-start(bf16[2,512,256]{2,1,0:T(8,128)(2,1)S(1)} %get-tuple-element.34), channel_id=1, source_target_pairs={{0,4},{4,0},{8,12},{12,8},{16,20},{20,16},{24,28},{28,24},{32,36},... | collective-permute-start | bytes 1572872 | tf_op jit(solution)/shard_map/ppermute | solution.py:20
  7.3 1.3 %shard_map.56 = (f32[2,512,128]{2,1,0:T(8,128)S(1)}, f32[2,512,128]{2,1,0:T(8,128)S(1)}) custom-call(bf16[512,256]{1,0:T(8,128)(2,1)S(1)} %get-tuple-element.31.q.mq, bf16[2,512,256]{2,1,0:T(8,128)(2,1)S(1)} %get-tuple-element.32.kv.mkv, bf16[512,256]{1,0:T(8,128)(2,1)S(1)} %get-tuple-element.33.after), custom_call_target="tpu_custom_call" | custom-call | flops 268435456 | bytes 786432 | tf_op jit(solution)/shard_map/pallas_call | solution.py:260
  8.6 0.2 collective-permute-done.1.rkv.kv
  8.8 0.0 copy-done.4
  8.8 1.0 %shard_map.57 = (bf16[192,256]{1,0:T(8,128)(2,1)S(1)}, bf16[448,256]{1,0:T(8,128)(2,1)S(1)}, bf16[768,256]{1,0:T(8,128)(2,1)S(1)}) custom-call(s32[4]{0:T(128)S(1)} %pad_add_fusion.pos, s32[6,16]{1,0:T(8,128)S(1)} %copy-done.4, bf16[2,512,256]{2,1,0:T(8,128)(2,1)S(1)} %get-tuple-element.32.kv.mkv, bf16[2,512,256]{2,1,0:T(8,128)(2,1)S(1)} %collective-permute-done.1.rkv.kv, ...), custom_call_target="tpu_custom_call" | custom-call | bytes 1048576 | tf_op jit(solution)/shard_map/pallas_call | solution.py:260
  9.8 0.1 collective-permute-start.2
  9.9 0.5 collective-permute-start
  10.5 1.2 %collective-permute-start.3 = (bf16[448,256]{1,0:T(8,128)(2,1)S(1)}, bf16[448,256]{1,0:T(8,128)(2,1)S(1)}, u32[]{:S(2)}, u32[]{:S(2)}) collective-permute-start(bf16[448,256]{1,0:T(8,128)(2,1)S(1)} %get-tuple-element.41), channel_id=1, source_target_pairs={{0,16},{4,20},{8,24},{12,28},{16,0},{20,4},{24,8},{28,12},{32,48},... | collective-permute-start | bytes 688136 | tf_op jit(solution)/shard_map/ppermute | solution.py:20
  11.7 1.8 %collective-permute-start.5 = (bf16[192,256]{1,0:T(8,128)(2,1)S(1)}, bf16[192,256]{1,0:T(8,128)(2,1)S(1)}, u32[]{:S(2)}, u32[]{:S(2)}) collective-permute-start(bf16[192,256]{1,0:T(8,128)(2,1)S(1)} %get-tuple-element.37.after.g45), channel_id=1, source_target_pairs={{0,48},{4,52},{8,56},{12,60},{16,32},{20,36},{24,40},{28,44},{32,1... | collective-permute-start | bytes 294920 | tf_op jit(solution)/shard_map/ppermute | solution.py:20
  13.5 0.6 collective-permute-start.4
  14.1 0.0 collective-permute-done.q.rq
  14.1 1.3 %shard_map.58 = (f32[2,512,128]{2,1,0:T(8,128)S(1)}, f32[2,512,128]{2,1,0:T(8,128)S(1)}) custom-call(bf16[512,256]{1,0:T(8,128)(2,1)S(1)} %collective-permute-done.q.rq, bf16[2,512,256]{2,1,0:T(8,128)(2,1)S(1)} %collective-permute-done.1.rkv.kv, bf16[192,256]{1,0:T(8,128)(2,1)S(1)} %get-tuple-element.37.after.g45), custom_call_target="tpu_custom_call" | custom-call | flops 268435456 | bytes 786432 | tf_op jit(solution)/shard_map/pallas_call | solution.py:260
  15.5 1.5 %collective-permute-done.5.a2 = bf16[192,256]{1,0:T(8,128)(2,1)S(1)} collective-permute-done((bf16[192,256]{1,0:T(8,128)(2,1)S(1)}, bf16[192,256]{1,0:T(8,128)(2,1)S(1)}, u32[]{:S(2)}, u32[]{:S(2)}) %collective-permute-start.5) | collective-permute-done | bytes 98336 | tf_op jit(solution)/shard_map/ppermute | solution.py:20
  17.0 5.0 %collective-permute-done.4.a1 = bf16[192,256]{1,0:T(8,128)(2,1)S(1)} collective-permute-done((bf16[192,256]{1,0:T(8,128)(2,1)S(1)}, bf16[192,256]{1,0:T(8,128)(2,1)S(1)}, u32[]{:S(2)}, u32[]{:S(2)}) %collective-permute-start.4) | collective-permute-done | bytes 98336 | tf_op jit(solution)/shard_map/ppermute | solution.py:20
  22.0 0.0 collective-permute-done.3.a0
  22.0 0.0 collective-permute-done.2.zb
  22.1 0.1 collective-permute-start.7
  22.2 0.1 collective-permute-start.6
  22.3 2.4 %collective-permute-start.9 = (bf16[256,256]{1,0:T(8,128)(2,1)S(1)}, bf16[256,256]{1,0:T(8,128)(2,1)S(1)}, u32[]{:S(2)}, u32[]{:S(2)}) collective-permute-start(bf16[256,256]{1,0:T(8,128)(2,1)S(1)} %get-tuple-element.42.after), channel_id=1, source_target_pairs={{0,72},{4,76},{8,64},{12,68},{16,88},{20,92},{24,80},{28,84},{32,1... | collective-permute-start | bytes 393224 | tf_op jit(solution)/shard_map/ppermute | solution.py:20
  24.6 0.2 collective-permute-start.8
  24.8 6.1 %shard_map.60 = (f32[2,1024,128]{2,1,0:T(8,128)S(1)}, f32[2,1024,128]{2,1,0:T(8,128)S(1)}, bf16[448,128]{1,0:T(8,128)(2,1)S(1)}) custom-call(s32[4]{0:T(128)S(1)} %pad_add_fusion.pos, s32[6,16]{1,0:T(8,128)S(1)} %copy-done.4, bf16[512,256]{1,0:T(8,128)(2,1)S(1)} %get-tuple-element.31.q.mq, bf16[2,512,256]{2,1,0:T(8,128)(2,1)S(1)} %get-tuple-element.32.kv.mkv, ...), custom_call_target="tpu_custom_call" | custom-call | flops 402653184 | bytes 4456448 | tf_op jit(solution)/shard_map/pallas_call | solution.py:260
  30.9 0.0 collective-permute-done.6.d
  30.9 4.9 %collective-permute-done.9.g = bf16[256,256]{1,0:T(8,128)(2,1)S(1)} collective-permute-done((bf16[256,256]{1,0:T(8,128)(2,1)S(1)}, bf16[256,256]{1,0:T(8,128)(2,1)S(1)}, u32[]{:S(2)}, u32[]{:S(2)}) %collective-permute-start.9) | collective-permute-done | bytes 131104 | tf_op jit(solution)/shard_map/ppermute | solution.py:20
  35.8 0.0 collective-permute-done.8.f
  35.8 0.0 collective-permute-done.7.e
  35.8 0.0 copy-start
  35.8 3.6 %shard_map.61 = (bf16[512,256]{1,0:T(8,128)(2,1)S(1)}, bf16[512,256]{1,0:T(8,128)(2,1)S(1)}) custom-call(s32[4]{0:T(128)S(1)} %pad_add_fusion.pos, s32[6,16]{1,0:T(8,128)S(1)} %copy-done.4, f32[2,1024,128]{2,1,0:T(8,128)S(1)} %get-tuple-element.43.acc0, f32[2,1024,128]{2,1,0:T(8,128)S(1)} %get-tuple-element.44.stat0, ...), custom_call_target="tpu_custom_call" | custom-call | flops 134217728 | bytes 4308992 | tf_op jit(solution)/shard_map/pallas_call | solution.py:260
  39.4 1.8 %collective-permute-start.10 = (bf16[512,256]{1,0:T(8,128)(2,1)S(1)}, bf16[512,256]{1,0:T(8,128)(2,1)S(1)}, u32[]{:S(2)}, u32[]{:S(2)}) collective-permute-start(bf16[512,256]{1,0:T(8,128)(2,1)S(1)} %get-tuple-element.49), channel_id=1, source_target_pairs={{0,4},{4,0},{8,12},{12,8},{16,20},{20,16},{24,28},{28,24},{32,36},... | collective-permute-start | bytes 786440 | tf_op jit(solution)/shard_map/ppermute | solution.py:20
  41.2 1.2 %collective-permute-done.10.back = bf16[512,256]{1,0:T(8,128)(2,1)S(1)} collective-permute-done((bf16[512,256]{1,0:T(8,128)(2,1)S(1)}, bf16[512,256]{1,0:T(8,128)(2,1)S(1)}, u32[]{:S(2)}, u32[]{:S(2)}) %collective-permute-start.10) | collective-permute-done | bytes 262176 | tf_op jit(solution)/shard_map/ppermute | solution.py:20
  42.3 0.0 copy-done
  42.3 1.0 %shard_map.62 = (bf16[256,512]{1,0:T(8,128)(2,1)S(1)}, bf16[256,512]{1,0:T(8,128)(2,1)S(1)}) custom-call(s32[4]{0:T(128)S(1)} %pad_add_fusion.pos, bf16[512,256]{1,0:T(8,128)(2,1)S(1)} %get-tuple-element.48.mine, bf16[512,256]{1,0:T(8,128)(2,1)S(1)} %collective-permute-done.10.back, bf16[512,2048]{1,0:T(8,128)(2,1)S(1)} %copy-done), custom_call_target="tpu_custom_call" | custom-call | flops 268435456 | bytes 2621440 | tf_op jit(solution)/shard_map/pallas_call | solution.py:260
  43.3 3.1 %collective-permute-start.12 = (bf16[256,512]{1,0:T(8,128)(2,1)S(1)}, bf16[256,512]{1,0:T(8,128)(2,1)S(1)}, u32[]{:S(2)}, u32[]{:S(2)}) collective-permute-start(bf16[256,512]{1,0:T(8,128)(2,1)S(1)} %get-tuple-element.50.after), channel_id=1, source_target_pairs={{0,1},{1,0},{2,3},{3,2},{4,5},{5,4},{6,7},{7,6},{8,9},{9,8},{10,11... | collective-permute-start | bytes 786440 | tf_op jit(solution)/shard_map/ppermute | solution.py:24
  46.4 3.3 %collective-permute-start.15 = (bf16[256,512]{1,0:T(8,128)(2,1)S(1)}, bf16[256,512]{1,0:T(8,128)(2,1)S(1)}, u32[]{:S(2)}, u32[]{:S(2)}) collective-permute-start(bf16[256,512]{1,0:T(8,128)(2,1)S(1)} %get-tuple-element.56), channel_id=1, source_target_pairs={{0,3},{1,2},{2,1},{3,0},{4,7},{5,6},{6,5},{7,4},{8,11},{9,10},{10,... | collective-permute-start | bytes 786440 | tf_op jit(solution)/shard_map/ppermute | solution.py:24
  49.7 1.5 %shard_map.63 = (bf16[256,512]{1,0:T(8,128)(2,1)S(1)}, bf16[256,512]{1,0:T(8,128)(2,1)S(1)}, f32[256,512]{1,0:T(8,128)S(1)}, f32[256,512]{1,0:T(8,128)S(1)}, f32[512,512]{1,0:T(8,128)S(1)}) custom-call(s32[4]{0:T(128)S(1)} %pad_add_fusion.pos, bf16[512,256]{1,0:T(8,128)(2,1)S(1)} %get-tuple-element.48.mine, ...), custom_call_target="tpu_custom_call" | custom-call | flops 805306368 | bytes 2621440 | tf_op jit(solution)/shard_map/pallas_call | solution.py:260
  51.3 1.3 %collective-permute-start.11 = (bf16[256,512]{1,0:T(8,128)(2,1)S(1)}, bf16[256,512]{1,0:T(8,128)(2,1)S(1)}, u32[]{:S(2)}, u32[]{:S(2)}) collective-permute-start(bf16[256,512]{1,0:T(8,128)(2,1)S(1)} %get-tuple-element.52), channel_id=1, source_target_pairs={{0,1},{1,0},{2,3},{3,2},{4,5},{5,4},{6,7},{7,6},{8,9},{9,8},{10,11... | collective-permute-start | bytes 786440 | tf_op jit(solution)/shard_map/ppermute | solution.py:24
  52.5 0.0 collective-permute-start.14
  52.5 9.2 %collective-permute-done.12.came = bf16[256,512]{1,0:T(8,128)(2,1)S(1)} collective-permute-done((bf16[256,512]{1,0:T(8,128)(2,1)S(1)}, bf16[256,512]{1,0:T(8,128)(2,1)S(1)}, u32[]{:S(2)}, u32[]{:S(2)}) %collective-permute-start.12) | collective-permute-done | bytes 262176 | tf_op jit(solution)/shard_map/ppermute | solution.py:24
  61.7 0.1 shard_map.64
  61.8 0.1 collective-permute-start.13
  61.9 0.0 collective-permute-done.15.came
  61.9 0.1 shard_map.65
  61.9 3.1 %collective-permute-start.16 = (bf16[256,512]{1,0:T(8,128)(2,1)S(1)}, bf16[256,512]{1,0:T(8,128)(2,1)S(1)}, u32[]{:S(2)}, u32[]{:S(2)}) collective-permute-start(bf16[256,512]{1,0:T(8,128)(2,1)S(1)} %shard_map.65), channel_id=1, source_target_pairs={{0,1},{1,0},{2,3},{3,2},{4,5},{5,4},{6,7},{7,6},{8,9},{9,8},{10,11... | collective-permute-start | bytes 786440 | tf_op jit(solution)/shard_map/ppermute | solution.py:24
  65.1 4.7 %collective-permute-done.11.up2 = bf16[256,512]{1,0:T(8,128)(2,1)S(1)} collective-permute-done((bf16[256,512]{1,0:T(8,128)(2,1)S(1)}, bf16[256,512]{1,0:T(8,128)(2,1)S(1)}, u32[]{:S(2)}, u32[]{:S(2)}) %collective-permute-start.11) | collective-permute-done | bytes 262176 | tf_op jit(solution)/shard_map/ppermute | solution.py:24
  69.8 0.0 collective-permute-done.14.down2
  69.8 13.9 %collective-permute-done.13.up3 = bf16[256,512]{1,0:T(8,128)(2,1)S(1)} collective-permute-done((bf16[256,512]{1,0:T(8,128)(2,1)S(1)}, bf16[256,512]{1,0:T(8,128)(2,1)S(1)}, u32[]{:S(2)}, u32[]{:S(2)}) %collective-permute-start.13) | collective-permute-done | bytes 262176 | tf_op jit(solution)/shard_map/ppermute | solution.py:24
  83.7 0.0 collective-permute-done.16.down3
  83.7 1.0 %shard_map.66 = bf16[512,512]{1,0:T(8,128)(2,1)} custom-call(f32[512,512]{1,0:T(8,128)S(1)} %get-tuple-element.51.own, bf16[256,512]{1,0:T(8,128)(2,1)S(1)} %collective-permute-done.11.up2, bf16[256,512]{1,0:T(8,128)(2,1)S(1)} %collective-permute-done.13.up3, bf16[256,512]{1,0:T(8,128)(2,1)S(1)} %collective-permute-done.14.down2, ...), custom_call_target="tpu_custom_call" | custom-call | bytes 2097152 | tf_op jit(solution)/shard_map/pallas_call | solution.py:260
  (1 shorter events, 0.0 us)
Async XLA Ops:
  0.0 8.8 %copy-start.4 = (s32[6,16]{1,0:T(8,128)S(1)}, s32[6,16]{1,0:T(8,128)}, u32[]{:S(2)}) copy-start(s32[6,16]{1,0:T(8,128)} %offs.5) | copy-start | bytes 1156
  0.1 1.0 %copy-start.1 = (bf16[512,512]{1,0:T(8,128)(2,1)S(1)}, bf16[512,512]{1,0:T(8,128)(2,1)}, u32[]{:S(2)}) copy-start(bf16[512,512]{1,0:T(8,128)(2,1)} %q.1) | copy-start | bytes 1572868
  1.1 1.0 %copy-start.2 = (bf16[512,512]{1,0:T(8,128)(2,1)S(1)}, bf16[512,512]{1,0:T(8,128)(2,1)}, u32[]{:S(2)}) copy-start(bf16[512,512]{1,0:T(8,128)(2,1)} %k.1) | copy-start | bytes 1572868
  2.2 1.0 %copy-start.3 = (bf16[512,512]{1,0:T(8,128)(2,1)S(1)}, bf16[512,512]{1,0:T(8,128)(2,1)}, u32[]{:S(2)}) copy-start(bf16[512,512]{1,0:T(8,128)(2,1)} %v.1) | copy-start | bytes 1572868
  3.9 4.9 %collective-permute-start.1 = (bf16[2,512,256]{2,1,0:T(8,128)(2,1)S(1)}, bf16[2,512,256]{2,1,0:T(8,128)(2,1)S(1)}, u32[]{:S(2)}, u32[]{:S(2)}) collective-permute-start(bf16[2,512,256]{2,1,0:T(8,128)(2,1)S(1)} %get-tuple-element.34), channel_id=1, source_target_pairs={{0,4},{4,0},{8,12},{12,8},{16,20},{20,16},{24,28},{28,24},{32,36},... | collective-permute-start | bytes 1572872 | tf_op jit(solution)/shard_map/ppermute | solution.py:20
  9.8 12.2 %collective-permute-start.2 = (bf16[768,256]{1,0:T(8,128)(2,1)S(1)}, bf16[768,256]{1,0:T(8,128)(2,1)S(1)}, u32[]{:S(2)}, u32[]{:S(2)}) collective-permute-start(bf16[768,256]{1,0:T(8,128)(2,1)S(1)} %get-tuple-element.40.g32), channel_id=1, source_target_pairs={{0,8},{4,12},{8,0},{12,4},{16,24},{20,28},{24,16},{28,20},{32,40},... | collective-permute-start | bytes 1179656 | tf_op jit(solution)/shard_map/ppermute | solution.py:20
  9.9 4.2 %collective-permute-start = (bf16[512,256]{1,0:T(8,128)(2,1)S(1)}, bf16[512,256]{1,0:T(8,128)(2,1)S(1)}, u32[]{:S(2)}, u32[]{:S(2)}) collective-permute-start(bf16[512,256]{1,0:T(8,128)(2,1)S(1)} %get-tuple-element.33.after), channel_id=1, source_target_pairs={{0,4},{4,0},{8,12},{12,8},{16,20},{20,16},{24,28},{28,24},{32,36},... | collective-permute-start | bytes 786440 | tf_op jit(solution)/shard_map/ppermute | solution.py:20
  10.5 11.5 %collective-permute-start.3 = (bf16[448,256]{1,0:T(8,128)(2,1)S(1)}, bf16[448,256]{1,0:T(8,128)(2,1)S(1)}, u32[]{:S(2)}, u32[]{:S(2)}) collective-permute-start(bf16[448,256]{1,0:T(8,128)(2,1)S(1)} %get-tuple-element.41), channel_id=1, source_target_pairs={{0,16},{4,20},{8,24},{12,28},{16,0},{20,4},{24,8},{28,12},{32,48},... | collective-permute-start | bytes 688136 | tf_op jit(solution)/shard_map/ppermute | solution.py:20
  11.7 5.3 %collective-permute-start.5 = (bf16[192,256]{1,0:T(8,128)(2,1)S(1)}, bf16[192,256]{1,0:T(8,128)(2,1)S(1)}, u32[]{:S(2)}, u32[]{:S(2)}) collective-permute-start(bf16[192,256]{1,0:T(8,128)(2,1)S(1)} %get-tuple-element.37.after.g45), channel_id=1, source_target_pairs={{0,48},{4,52},{8,56},{12,60},{16,32},{20,36},{24,40},{28,44},{32,1... | collective-permute-start | bytes 294920 | tf_op jit(solution)/shard_map/ppermute | solution.py:20
  13.5 8.5 %collective-permute-start.4 = (bf16[192,256]{1,0:T(8,128)(2,1)S(1)}, bf16[192,256]{1,0:T(8,128)(2,1)S(1)}, u32[]{:S(2)}, u32[]{:S(2)}) collective-permute-start(bf16[192,256]{1,0:T(8,128)(2,1)S(1)} %get-tuple-element.37.after.g45), channel_id=1, source_target_pairs={{0,32},{4,36},{8,40},{12,44},{16,48},{20,52},{24,56},{28,60},{32,0... | collective-permute-start | bytes 294920 | tf_op jit(solution)/shard_map/ppermute | solution.py:20
  22.1 13.8 %collective-permute-start.7 = (bf16[768,256]{1,0:T(8,128)(2,1)S(1)}, bf16[768,256]{1,0:T(8,128)(2,1)S(1)}, u32[]{:S(2)}, u32[]{:S(2)}) collective-permute-start(bf16[768,256]{1,0:T(8,128)(2,1)S(1)} %get-tuple-element.47), channel_id=1, source_target_pairs={{0,8},{4,12},{8,0},{12,4},{16,24},{20,28},{24,16},{28,20},{32,40},... | collective-permute-start | bytes 1179656 | tf_op jit(solution)/shard_map/ppermute | solution.py:20
  22.2 8.8 %collective-permute-start.6 = (bf16[256,256]{1,0:T(8,128)(2,1)S(1)}, bf16[256,256]{1,0:T(8,128)(2,1)S(1)}, u32[]{:S(2)}, u32[]{:S(2)}) collective-permute-start(bf16[256,256]{1,0:T(8,128)(2,1)S(1)} %get-tuple-element.46), channel_id=1, source_target_pairs={{0,16},{4,20},{8,24},{12,28},{16,0},{20,4},{24,8},{28,12},{32,48},... | collective-permute-start | bytes 393224 | tf_op jit(solution)/shard_map/ppermute | solution.py:20
  22.3 13.6 %collective-permute-start.9 = (bf16[256,256]{1,0:T(8,128)(2,1)S(1)}, bf16[256,256]{1,0:T(8,128)(2,1)S(1)}, u32[]{:S(2)}, u32[]{:S(2)}) collective-permute-start(bf16[256,256]{1,0:T(8,128)(2,1)S(1)} %get-tuple-element.42.after), channel_id=1, source_target_pairs={{0,72},{4,76},{8,64},{12,68},{16,88},{20,92},{24,80},{28,84},{32,1... | collective-permute-start | bytes 393224 | tf_op jit(solution)/shard_map/ppermute | solution.py:20
  24.6 11.2 %collective-permute-start.8 = (bf16[256,256]{1,0:T(8,128)(2,1)S(1)}, bf16[256,256]{1,0:T(8,128)(2,1)S(1)}, u32[]{:S(2)}, u32[]{:S(2)}) collective-permute-start(bf16[256,256]{1,0:T(8,128)(2,1)S(1)} %get-tuple-element.42.after), channel_id=1, source_target_pairs={{0,64},{4,68},{8,72},{12,76},{16,80},{20,84},{24,88},{28,92},{32,9... | collective-permute-start | bytes 393224 | tf_op jit(solution)/shard_map/ppermute | solution.py:20
  35.8 6.5 %copy-start = (bf16[512,2048]{1,0:T(8,128)(2,1)S(1)}, bf16[512,2048]{1,0:T(8,128)(2,1)}, u32[]{:S(2)}) copy-start(bf16[512,2048]{1,0:T(8,128)(2,1)} %w.3) | copy-start | bytes 6291460
  39.4 2.9 %collective-permute-start.10 = (bf16[512,256]{1,0:T(8,128)(2,1)S(1)}, bf16[512,256]{1,0:T(8,128)(2,1)S(1)}, u32[]{:S(2)}, u32[]{:S(2)}) collective-permute-start(bf16[512,256]{1,0:T(8,128)(2,1)S(1)} %get-tuple-element.49), channel_id=1, source_target_pairs={{0,4},{4,0},{8,12},{12,8},{16,20},{20,16},{24,28},{28,24},{32,36},... | collective-permute-start | bytes 786440 | tf_op jit(solution)/shard_map/ppermute | solution.py:20
  43.3 18.4 %collective-permute-start.12 = (bf16[256,512]{1,0:T(8,128)(2,1)S(1)}, bf16[256,512]{1,0:T(8,128)(2,1)S(1)}, u32[]{:S(2)}, u32[]{:S(2)}) collective-permute-start(bf16[256,512]{1,0:T(8,128)(2,1)S(1)} %get-tuple-element.50.after), channel_id=1, source_target_pairs={{0,1},{1,0},{2,3},{3,2},{4,5},{5,4},{6,7},{7,6},{8,9},{9,8},{10,11... | collective-permute-start | bytes 786440 | tf_op jit(solution)/shard_map/ppermute | solution.py:24
  46.4 15.5 %collective-permute-start.15 = (bf16[256,512]{1,0:T(8,128)(2,1)S(1)}, bf16[256,512]{1,0:T(8,128)(2,1)S(1)}, u32[]{:S(2)}, u32[]{:S(2)}) collective-permute-start(bf16[256,512]{1,0:T(8,128)(2,1)S(1)} %get-tuple-element.56), channel_id=1, source_target_pairs={{0,3},{1,2},{2,1},{3,0},{4,7},{5,6},{6,5},{7,4},{8,11},{9,10},{10,... | collective-permute-start | bytes 786440 | tf_op jit(solution)/shard_map/ppermute | solution.py:24
  51.3 18.5 %collective-permute-start.11 = (bf16[256,512]{1,0:T(8,128)(2,1)S(1)}, bf16[256,512]{1,0:T(8,128)(2,1)S(1)}, u32[]{:S(2)}, u32[]{:S(2)}) collective-permute-start(bf16[256,512]{1,0:T(8,128)(2,1)S(1)} %get-tuple-element.52), channel_id=1, source_target_pairs={{0,1},{1,0},{2,3},{3,2},{4,5},{5,4},{6,7},{7,6},{8,9},{9,8},{10,11... | collective-permute-start | bytes 786440 | tf_op jit(solution)/shard_map/ppermute | solution.py:24
  52.5 17.3 %collective-permute-start.14 = (bf16[256,512]{1,0:T(8,128)(2,1)S(1)}, bf16[256,512]{1,0:T(8,128)(2,1)S(1)}, u32[]{:S(2)}, u32[]{:S(2)}) collective-permute-start(bf16[256,512]{1,0:T(8,128)(2,1)S(1)} %get-tuple-element.54), channel_id=1, source_target_pairs={{0,3},{1,2},{2,1},{3,0},{4,7},{5,6},{6,5},{7,4},{8,11},{9,10},{10,... | collective-permute-start | bytes 786440 | tf_op jit(solution)/shard_map/ppermute | solution.py:24
  61.8 21.9 %collective-permute-start.13 = (bf16[256,512]{1,0:T(8,128)(2,1)S(1)}, bf16[256,512]{1,0:T(8,128)(2,1)S(1)}, u32[]{:S(2)}, u32[]{:S(2)}) collective-permute-start(bf16[256,512]{1,0:T(8,128)(2,1)S(1)} %shard_map.64), channel_id=1, source_target_pairs={{0,3},{1,2},{2,1},{3,0},{4,7},{5,6},{6,5},{7,4},{8,11},{9,10},{10,... | collective-permute-start | bytes 786440 | tf_op jit(solution)/shard_map/ppermute | solution.py:24
  61.9 21.8 %collective-permute-start.16 = (bf16[256,512]{1,0:T(8,128)(2,1)S(1)}, bf16[256,512]{1,0:T(8,128)(2,1)S(1)}, u32[]{:S(2)}, u32[]{:S(2)}) collective-permute-start(bf16[256,512]{1,0:T(8,128)(2,1)S(1)} %shard_map.65), channel_id=1, source_target_pairs={{0,1},{1,0},{2,3},{3,2},{4,5},{5,4},{6,7},{7,6},{8,9},{9,8},{10,11... | collective-permute-start | bytes 786440 | tf_op jit(solution)/shard_map/ppermute | solution.py:24

commit v3 on v2

v3 whole, which is shorter than its diff:
```python
import math

import jax
import jax.numpy as jnp
from jax import lax
from jax.experimental import pallas as pl
from jax.experimental.pallas import tpu as pltpu
from jax.sharding import PartitionSpec as P

HD = 128
F32 = jnp.float32
BF16 = jnp.bfloat16
TOK = 512
CHIP = 2 * TOK
MIB = 1024 * 1024
GAIN = math.log2(math.e) / math.sqrt(HD)
CORE, Z, X1, X2, Y1 = 1, 2, 4, 8, 16


def swap(block, bits):
    return lax.ppermute(block, "ctx", [(i, i ^ bits) for i in range(64)])


def cross(block, bits):
    return lax.ppermute(block, "head", [(i, i ^ bits) for i in range(4)])


def used(off, level, first=0, count=None):
    r = 1 << level
    n = CHIP // r if count is None else count
    return pl.ds(off + first * r, n, stride=r)


def halves(pos):
    here = pl.multiple_of(pos[0] * TOK, TOK)
    there = pl.multiple_of(TOK - pos[0] * TOK, TOK)
    return pl.ds(here, TOK), pl.ds(there, TOK)


def run_copies(moves, sems):
    copies = [pltpu.make_async_copy(src, dst, sems.at[i]) for i, (src, dst) in enumerate(moves)]
    for copy in copies:
        copy.start()
    for copy in copies:
        copy.wait()


def theirs_kernel(k, v, okv, sems):
    core = lax.rem(lax.axis_index("ctx"), 2)
    theirs = pl.ds(pl.multiple_of(256 - core * 256, 256), 256)
    run_copies([(k.at[:, theirs], okv.at[0]), (v.at[:, theirs], okv.at[1])], sems)


def mine_columns_kernel(q, k, v, after, oq, mkv, mq, sems):
    del after
    core = lax.rem(lax.axis_index("ctx"), 2)
    theirs = pl.ds(pl.multiple_of(256 - core * 256, 256), 256)
    mine = pl.ds(pl.multiple_of(core * 256, 256), 256)
    moves = [(q.at[:, theirs], oq), (q.at[:, mine], mq)]
    moves += [(k.at[:, mine], mkv.at[0]), (v.at[:, mine], mkv.at[1])]
    run_copies(moves, sems)


def fill(buf, base, pos, mine, theirs):
    here, there = halves(pos)
    for j in range(2):
        cols = slice(j * HD, (j + 1) * HD)
        buf[base + j, here, :] = mine[:, cols].astype(F32)
        buf[base + j, there, :] = theirs[:, cols].astype(F32)


def pick_kernel(pos, offs, mkv, rkv, after, g34, g2, g53, g5, buf):
    del after
    for i in range(2):
        fill(buf, 2 * i, pos, mkv.at[i], rkv.at[i])
    places = {3: ((g34, 0), (g53, 64)), 4: ((g34, 256),), 5: ((g53, 0), (g5, 0)), 2: ((g2, 0),)}
    for level, where in places.items():
        n = CHIP >> level
        for j in range(2):
            rows = used(offs[level, pos[1] + j], level)
            for i in range(2):
                part = buf[2 * i + j, rows, :].astype(BF16)
                for dst, row in where:
                    dst[row + j * n : row + (j + 1) * n, i * HD : (i + 1) * HD] = part


def raw_scores(q, k):
    return lax.dot_general(q, k, (((1,), (1,)), ((), ())), preferred_element_type=F32)


def softmax_parts(scores, values):
    peaks = [jnp.max(s, axis=-1, keepdims=True) for s in scores]
    expos = [jnp.exp2((s - m) * GAIN).astype(BF16) for s, m in zip(scores, peaks)]
    parts = []
    for m, e, v in zip(peaks, expos, values):
        wide = jnp.concatenate([v, jnp.ones_like(v)], axis=1)
        mixed = jnp.dot(e, wide, preferred_element_type=F32)
        parts.append((jnp.broadcast_to(m, (m.shape[0], HD)), mixed[:, HD:], mixed[:, :HD]))
    return parts


def causal_scores(q, k):
    row = lax.broadcasted_iota(jnp.int32, (256, 256), 0)
    col = lax.broadcasted_iota(jnp.int32, (256, 256), 1)
    first = jnp.where(col <= row, raw_scores(q[:256], k[:256]), -jnp.inf)
    last = jnp.where(col <= row, raw_scores(q[256:], k[256:]), -jnp.inf)
    return [first, jnp.concatenate([raw_scores(q[256:], k[:256]), last], axis=1)]


def merge(state, j, rows, part):
    acc, peak, total = state
    m, t, o = part
    old = peak[j, rows, :]
    top = jnp.maximum(old, m)
    a = jnp.exp2((old - top) * GAIN)
    b = jnp.exp2((m - top) * GAIN)
    acc[j, rows, :] = acc[j, rows, :] * a + o * b
    total[j, rows, :] = total[j, rows, :] * a + t * b
    peak[j, rows, :] = top


def tile(start, q, kv, state):
    acc, peak, total = state
    for j in range(2):
        cols = slice(j * HD, (j + 1) * HD)
        values = kv[1, :, cols]
        parts = softmax_parts(causal_scores(q[:, cols], kv[0, :, cols]), [values[:256], values])
        for half, (m, t, o) in enumerate(parts):
            rows = pl.ds(pl.multiple_of(start + half * 256, 256), 256)
            acc[j, rows, :] = o
            total[j, rows, :] = t
            peak[j, rows, :] = m


def own_tile_kernel(pos, q, kv, after, *state):
    del after
    tile(pos[0] * TOK, q, kv, state)


def other_tile_kernel(pos, acc0, peak0, total0, q, kv, after, *state):
    del acc0, peak0, total0, after
    tile(TOK - pos[0] * TOK, q, kv, state)


def gather_kernel(g5, a0, a1, a2, after, out):
    del after
    for i, part in enumerate((g5, a0, a1, a2)):
        out[64 * i : 64 * (i + 1), :] = part[:64, :]


def pair_kernel(g34, zb, p1, p2):
    for dst in (p1, p2):
        dst[:128, :] = g34[256:, :]
        dst[128:256, :] = zb[256:, :]
    p1[256:, :] = zb[:256, :]


def far_scores(pos, q, blocks, level):
    n = q.shape[0]
    span = lax.rem(pos[2], 1 << (level - 1))
    code = lax.broadcasted_iota(jnp.int32, (1, TOK), 1) // n
    if level == 5:
        code = ((code & 3) << 1) | ((code >> 2) & 1) | (code & 8)
    bias = jnp.where((code == 0) | ((span ^ code) < span), 0.0, -jnp.inf)
    s = raw_scores(q, jnp.concatenate([x[:, :HD] for x in blocks], axis=0)) + bias
    row = lax.broadcasted_iota(jnp.int32, s.shape, 0)
    col = lax.broadcasted_iota(jnp.int32, s.shape, 1)
    return jnp.where((col < n) & (col > row), -jnp.inf, s)


def far_values(blocks):
    return jnp.concatenate([x[:, HD:] for x in blocks], axis=0)


def near_kernel(pos, offs, acc0, peak0, total0, mq, mkv, rq, rkv, g2, z2, after, acc, peak, total, bq, buf):
    del acc0, peak0, total0, after
    state = (acc, peak, total)
    fill(buf, 0, pos, mq, rq)
    for i in range(2):
        fill(buf, 2 + 2 * i, pos, mkv.at[i], rkv.at[i])
    row = 0
    for level in (5, 4, 3):
        n = CHIP >> level
        for j in range(2):
            bq[row : row + n, :] = buf[j, used(offs[level, pos[1] + j], level), :].astype(BF16)
            row += n
    for j in range(2):
        off = offs[1, pos[1] + j]
        qs, ks, vs = (buf[2 * i + j, used(off, 1), :].astype(BF16) for i in range(3))
        parts = softmax_parts(causal_scores(qs, ks), [vs[:256], vs])
        for half, part in enumerate(parts):
            merge(state, j, used(off, 1, half * 256, 256), part)
    rows = [used(offs[2, pos[1] + j], 2) for j in range(2)]
    blocks = [[x[j * 256 : (j + 1) * 256] for x in (g2, z2)] for j in range(2)]
    scores = [far_scores(pos, buf[j, rows[j], :].astype(BF16), blocks[j], 2) for j in range(2)]
    parts = softmax_parts(scores, [far_values(b) for b in blocks])
    for j in range(2):
        merge(state, j, rows[j], parts[j])


def finish(acc, total, rows, dst):
    for j in range(2):
        dst[:, j * HD : (j + 1) * HD] = (acc[j, rows, :] * (1.0 / total[j, rows, :])).astype(BF16)


def far_kernel(
    pos, offs, acc0, peak0, total0, bq, g34, g5, a0, a1, a2, zb, h1, h2, h3, e, f, g, acc, peak, total, other
):
    del acc0, peak0, total0
    work = []
    for level, qrow in ((3, 192), (4, 64), (5, 0)):
        n = CHIP >> level
        for j in range(2):

            def cut(ref, row):
                return ref[row + j * n : row + (j + 1) * n]

            if level == 3:
                blocks = [cut(g34, 0), cut(zb, 0), cut(a0, 64), cut(h1, 256)]
            elif level == 4:
                blocks = [cut(g34, 256), cut(zb, 256)]
                blocks += [cut(x, row) for x in (h1, h2, h3) for row in (0, 128)]
            else:
                blocks = [cut(x, 0) for x in (g5, a0, a1, a2)]
                blocks += [cut(x, 64 * i) for x in (e, f, g) for i in range(4)]
            rows = used(offs[level, pos[1] + j], level)
            scores = far_scores(pos, cut(bq, qrow), blocks, level)
            work.append((j, rows, scores, far_values(blocks)))
    parts = softmax_parts([x[2] for x in work], [x[3] for x in work])
    for (j, rows, _, _), part in zip(work, parts):
        merge((acc, peak, total), j, rows, part)
    finish(acc, total, halves(pos)[1], other)


def dots(pos, far, rows, w, dest):
    start = 256 - pos[0] * 256 if far else pos[0] * 256
    at = pl.ds(pl.multiple_of(start, 256), 256)
    cols = pl.ds(pl.multiple_of(dest * TOK, TOK), TOK)
    return jnp.dot(rows, w[at, cols], preferred_element_type=F32)


def project(pos, mine, back, w, first, dest):
    rows = slice(first, first + 256)
    return dots(pos, False, mine[rows, :], w, dest) + dots(pos, True, back[rows, :], w, dest)


def mine_kernel(pos, acc, total, w, after, mine, part):
    del after
    finish(acc, total, halves(pos)[0], mine)
    part[...] = dots(pos, False, mine[...], w, pos[3] ^ 2)


def opposite_kernel(pos, part, back, w, up, down):
    up[...] = (part[:256, :] + dots(pos, True, back[:256, :], w, pos[3] ^ 2)).astype(BF16)
    down[...] = (part[256:, :] + dots(pos, True, back[256:, :], w, pos[3] ^ 2)).astype(BF16)


def rest_kernel(pos, mine, back, w, after, up, down, up_late, down_late, own):
    del after
    up[...] = project(pos, mine, back, w, 0, pos[3] ^ 1).astype(BF16)
    down[...] = project(pos, mine, back, w, 256, pos[3] ^ 3).astype(BF16)
    up_late[...] = project(pos, mine, back, w, 0, pos[3] ^ 3)
    down_late[...] = project(pos, mine, back, w, 256, pos[3] ^ 1)
    for first in (0, 256):
        own[first : first + 256, :] = project(pos, mine, back, w, first, pos[3])


def relay_kernel(late, came, out):
    out[...] = (late[...] + came[...].astype(F32)).astype(BF16)


def final_kernel(own, up2, up3, down2, down3, out, buf, sems):
    copies = []
    for i in range(4):
        rows = slice(i * 128, (i + 1) * 128)
        part = slice(i % 2 * 128, i % 2 * 128 + 128)
        a, b = (up2, up3) if i < 2 else (down2, down3)
        buf[rows, :] = (own[rows, :] + a[part, :].astype(F32) + b[part, :].astype(F32)).astype(BF16)
        copy = pltpu.make_async_copy(buf.at[rows, :], out.at[rows, :], sems.at[i])
        copy.start()
        copies.append(copy)
    for copy in copies:
        copy.wait()


SMEM = pl.BlockSpec(memory_space=pltpu.SMEM)
VMEM = pl.BlockSpec(memory_space=pltpu.VMEM)
ANY = pl.BlockSpec(memory_space=pl.ANY)


def call(
    kernel, scalars, arrays, outs, scratch=(), flops=0, unread=(), inside=VMEM, outside=VMEM, inplace=0, grant=24
):
    nbytes = sum(a.size * a.dtype.itemsize for a in arrays)
    return pl.pallas_call(
        kernel,
        in_specs=[SMEM] * len(scalars) + [inside] * len(arrays) + [ANY] * len(unread),
        out_specs=[outside] * len(outs),
        out_shape=[jax.ShapeDtypeStruct(s, t) for s, t in outs],
        scratch_shapes=list(scratch),
        input_output_aliases={len(scalars) + i: i for i in range(inplace)},
        compiler_params=pltpu.CompilerParams(vmem_limit_bytes=grant * MIB),
        cost_estimate=pl.CostEstimate(flops=flops, bytes_accessed=nbytes, transcendentals=0),
    )(*scalars, *arrays, *unread)


def local(q, k, v, offsets, w):
    ctx = lax.axis_index("ctx")
    head = lax.axis_index("head")
    core = ctx % 2
    pos = jnp.stack([core, head * 4 + core * 2, ctx // 2, head]).astype(jnp.int32)
    unit = 4 * TOK * TOK * HD
    part = (TOK, 256)

    def rows(n):
        return ((n, 256), BF16)

    q, k, v = (pltpu.with_memory_space_constraint(x, pltpu.HBM) for x in (q, k, v))
    sems = pltpu.SemaphoreType.DMA
    okv = call(theirs_kernel, (), (k, v), [((2,) + part, BF16)], [sems((2,))], inside=ANY)[0]
    rkv = swap(okv, CORE)
    oq, mkv, mq = call(
        mine_columns_kernel,
        (),
        (q, k, v),
        [(part, BF16), ((2,) + part, BF16), (part, BF16)],
        [sems((4,))],
        inside=ANY,
        unread=(okv,),
    )
    rq = swap(oq, CORE)
    states = [((2, CHIP, HD), F32)] * 3
    state = call(own_tile_kernel, (pos,), (mq, mkv), states, flops=2 * unit, unread=(oq,))
    g34, g2, g53, g5 = call(
        pick_kernel,
        (pos, offsets),
        (mkv, rkv),
        [rows(384), rows(512), rows(320), rows(64)],
        [pltpu.VMEM((4, CHIP, HD), F32)],
        unread=(state[0],),
    )
    zb = swap(g34, Z)
    a0, a1, a2 = swap(g53, X1), swap(g5, X2), swap(g5, X1 | X2)
    z2 = swap(g2, Z)
    state = call(
        other_tile_kernel, (pos,), (*state, rq, rkv), states, flops=2 * unit, unread=(g34,), inplace=3
    )
    p1, p2 = call(pair_kernel, (), (g34, zb), [rows(512), rows(256)])
    h1, h2, h3 = swap(p1, X1), swap(p2, X2), swap(p2, X1 | X2)
    x5 = call(gather_kernel, (), (g5, a0, a1, a2), [rows(256)], unread=(state[0],))[0]
    e, f, g = swap(x5, Z), swap(x5, Y1), swap(x5, Y1 | Z)
    *state, bq = call(
        near_kernel,
        (pos, offsets),
        (*state, mq, mkv, rq, rkv, g2, z2),
        states + [((448, HD), BF16)],
        [pltpu.VMEM((6, CHIP, HD), F32)],
        flops=3 * unit,
        unread=(x5,),
        inplace=3,
    )
    acc, _, total, other = call(
        far_kernel,
        (pos, offsets),
        (*state, bq, g34, g5, a0, a1, a2, zb, h1, h2, h3, e, f, g),
        states + [rows(TOK)],
        flops=unit,
        inplace=3,
    )
    back = swap(other, CORE)

    half = (256, TOK)
    mine, opposite = call(
        mine_kernel, (pos,), (acc, total, w), [rows(TOK), ((TOK, TOK), F32)], flops=TOK**3, unread=(other,)
    )
    up1, down1 = call(opposite_kernel, (pos,), (opposite, back, w), [(half, BF16)] * 2, flops=TOK**3)
    came_up, came_down = cross(up1, 1), cross(down1, 3)
    up2, down2, up_late, down_late, own = call(
        rest_kernel,
        (pos,),
        (mine, back, w),
        [(half, BF16)] * 2 + [(half, F32)] * 2 + [((TOK, TOK), F32)],
        flops=6 * TOK**3,
        unread=(up1,),
    )
    up2, down2 = cross(up2, 1), cross(down2, 3)
    up3 = cross(call(relay_kernel, (), (up_late, came_up), [(half, BF16)])[0], 3)
    down3 = cross(call(relay_kernel, (), (down_late, came_down), [(half, BF16)])[0], 1)
    return call(
        final_kernel,
        (),
        (own, up2, up3, down2, down3),
        [((TOK, TOK), BF16)],
        [pltpu.VMEM((TOK, TOK), BF16), pltpu.SemaphoreType.DMA((4,))],
        outside=ANY,
    )[0]


def solution(mesh):
    placed = (P("ctx", "head"), P("ctx", "head"), P("ctx", "head"), P(), P("head", None))
    return jax.shard_map(
        local, mesh=mesh, in_specs=placed, out_specs=P("ctx", "head"), check_vma=False
    )
```

time: 85.2 us -> 78.3 us (0.919)
  waiting for transfers between devices: 40.6 us -> 34.6 us
  starting transfers between devices: 23 us -> 28.6 us
  Pallas kernels: 17.8 us -> 14.6 us
  local copies, waits for them, and re-layouts: 3.13 us -> 0.01 us
    ppermute x11 -> x14, waiting for transfers between devices: 12.8 us -> 6.85 us  [swap(): return lax.ppermute(block, 'ctx', [(i, i ^ bits) for i in range(64)])]
    ppermute x11 -> x14, starting transfers between devices: 12.1 us -> 16.9 us  [swap(): return lax.ppermute(block, 'ctx', [(i, i ^ bits) for i in range(64)])]
    pallas_call x12 -> x15, Pallas kernels: 17.8 us -> 14.6 us  [call(): pl.pallas_call(kernel, in_specs=[SMEM] * len(scalars) + [inside] * len(ar...]
    unnamed x10 -> x4, local copies, waits for them, and re-layouts: 3.13 us -> 0.01 us
  transfers between devices with their start and end apart: 17 -> 20, of which waited for: 8 -> 11; matrix products, arithmetic and copies ran while one was open for 0% -> 0% of each run, Pallas kernels for 12% -> 13%
where the time goes in v3:
time: 78.3 us; the launch traced here: 78.2 us
  waiting for transfers between devices  34.6 us (44%)
  starting transfers between devices  28.6 us (37%)
  Pallas kernels  14.6 us (19%)
    ppermute x6, waiting for transfers between devices, cross(): return lax.ppermute(block, 'head', [(i, i ^ bits) for i in range(4)])  27.8 us
    ppermute x14, starting transfers between devices, swap(): return lax.ppermute(block, 'ctx', [(i, i ^ bits) for i in range(64)])  16.9 us
    pallas_call x15, Pallas kernels, call(): pl.pallas_call(kernel, in_specs=[SMEM] * len(scalars) + [inside] * len(ar...  14.6 us
    ppermute x6, starting transfers between devices, cross(): return lax.ppermute(block, 'head', [(i, i ^ bits) for i in range(4)])  11.6 us
    ppermute x14, waiting for transfers between devices, swap(): return lax.ppermute(block, 'ctx', [(i, i ^ bits) for i in range(64)])  6.85 us
  transfers between devices with their start and end apart: 20, of which 11 were waited for; matrix products, arithmetic and copies ran while one was open for 0% of the time, Pallas kernels for 13%

profile of v3, /device:TPU:1, one launch (start us, length us, event | category | flops | bytes accessed | tf_op | source)
XLA Modules:
  0.0 78.2 jit_solution(11598887814423126902)
XLA Ops:
  0.0 0.0 copy-start.1
  0.0 1.1 %shard_map.55.after = bf16[2,512,256]{2,1,0:T(8,128)(2,1)S(1)} custom-call(bf16[512,512]{1,0:T(8,128)(2,1)} %k.3, bf16[512,512]{1,0:T(8,128)(2,1)} %v.3), custom_call_target="tpu_custom_call" | custom-call | bytes 1048576 | tf_op jit(solution)/shard_map/pallas_call | solution.py:295
  1.1 3.3 %collective-permute-start.1 = (bf16[2,512,256]{2,1,0:T(8,128)(2,1)S(1)}, bf16[2,512,256]{2,1,0:T(8,128)(2,1)S(1)}, u32[]{:S(2)}, u32[]{:S(2)}) collective-permute-start(bf16[2,512,256]{2,1,0:T(8,128)(2,1)S(1)} %shard_map.55.after), channel_id=1, source_target_pairs={{0,4},{4,0},{8,12},{12,8},{16,20},{20,16},{24,28},{28,24},{32,36},... | collective-permute-start | bytes 1572872 | tf_op jit(solution)/shard_map/ppermute | solution.py:21
  4.4 1.2 %shard_map.56 = (bf16[512,256]{1,0:T(8,128)(2,1)S(1)}, bf16[2,512,256]{2,1,0:T(8,128)(2,1)S(1)}, bf16[512,256]{1,0:T(8,128)(2,1)S(1)}) custom-call(bf16[512,512]{1,0:T(8,128)(2,1)} %q.1, bf16[512,512]{1,0:T(8,128)(2,1)} %k.3, bf16[512,512]{1,0:T(8,128)(2,1)} %v.3, bf16[2,512,256]{2,1,0:T(8,128)(2,1)S(1)} %shard_map.55.after), custom_call_target="tpu_custom_call" | custom-call | bytes 1572864 | tf_op jit(solution)/shard_map/pallas_call | solution.py:295
  5.6 0.1 collective-permute-start
  5.7 0.1 pad_add_fusion.pos
  5.8 1.5 %shard_map.57 = (f32[2,1024,128]{2,1,0:T(8,128)S(1)}, f32[2,1024,128]{2,1,0:T(8,128)S(1)}, f32[2,1024,128]{2,1,0:T(8,128)S(1)}) custom-call(s32[4]{0:T(128)S(1)} %pad_add_fusion.pos, bf16[512,256]{1,0:T(8,128)(2,1)S(1)} %get-tuple-element.36.q.mq, bf16[2,512,256]{2,1,0:T(8,128)(2,1)S(1)} %get-tuple-element.37.kv.mkv, ...), custom_call_target="tpu_custom_call" | custom-call | flops 268435456 | bytes 786432 | tf_op jit(solution)/shard_map/pallas_call | solution.py:295
  7.3 0.0 collective-permute-done.1.rkv.kv
  7.3 0.0 copy-done.1
  7.3 1.0 %shard_map.58 = (bf16[384,256]{1,0:T(8,128)(2,1)S(1)}, bf16[512,256]{1,0:T(8,128)(2,1)S(1)}, bf16[320,256]{1,0:T(8,128)(2,1)S(1)}, bf16[64,256]{1,0:T(8,128)(2,1)S(1)}) custom-call(s32[4]{0:T(128)S(1)} %pad_add_fusion.pos, s32[6,16]{1,0:T(8,128)S(1)} %copy-done.1, bf16[2,512,256]{2,1,0:T(8,128)(2,1)S(1)} %get-tuple-element.37.kv.mkv, ...), custom_call_target="tpu_custom_call" | custom-call | bytes 1048576 | tf_op jit(solution)/shard_map/pallas_call | solution.py:295
  8.4 0.1 collective-permute-start.6
  8.5 1.1 %collective-permute-start.3 = (bf16[320,256]{1,0:T(8,128)(2,1)S(1)}, bf16[320,256]{1,0:T(8,128)(2,1)S(1)}, u32[]{:S(2)}, u32[]{:S(2)}) collective-permute-start(bf16[320,256]{1,0:T(8,128)(2,1)S(1)} %get-tuple-element.48), channel_id=1, source_target_pairs={{0,16},{4,20},{8,24},{12,28},{16,0},{20,4},{24,8},{28,12},{32,48},... | collective-permute-start | bytes 491528 | tf_op jit(solution)/shard_map/ppermute | solution.py:21
  9.6 0.3 collective-permute-start.2
  9.9 2.2 %collective-permute-start.4 = (bf16[64,256]{1,0:T(8,128)(2,1)S(1)}, bf16[64,256]{1,0:T(8,128)(2,1)S(1)}, u32[]{:S(2)}, u32[]{:S(2)}) collective-permute-start(bf16[64,256]{1,0:T(8,128)(2,1)S(1)} %get-tuple-element.47.g5), channel_id=1, source_target_pairs={{0,32},{4,36},{8,40},{12,44},{16,48},{20,52},{24,56},{28,60},{32,0... | collective-permute-start | bytes 98312 | tf_op jit(solution)/shard_map/ppermute | solution.py:21
  12.1 0.0 collective-permute-done.q.rq
  12.1 1.7 %collective-permute-start.5 = (bf16[64,256]{1,0:T(8,128)(2,1)S(1)}, bf16[64,256]{1,0:T(8,128)(2,1)S(1)}, u32[]{:S(2)}, u32[]{:S(2)}) collective-permute-start(bf16[64,256]{1,0:T(8,128)(2,1)S(1)} %get-tuple-element.47.g5), channel_id=1, source_target_pairs={{0,48},{4,52},{8,56},{12,60},{16,32},{20,36},{24,40},{28,44},{32,1... | collective-permute-start | bytes 98312 | tf_op jit(solution)/shard_map/ppermute | solution.py:21
  13.8 1.5 %shard_map.59 = (f32[2,1024,128]{2,1,0:T(8,128)S(1)}, f32[2,1024,128]{2,1,0:T(8,128)S(1)}, f32[2,1024,128]{2,1,0:T(8,128)S(1)}) custom-call(s32[4]{0:T(128)S(1)} %pad_add_fusion.pos, f32[2,1024,128]{2,1,0:T(8,128)S(1)} %get-tuple-element.39.after.acc0, ...), custom_call_target="tpu_custom_call", output_to_operand_aliasing={{0}: (1, {}), {1}: (2, {}), {2}: (3, {})} | custom-call | flops 268435456 | bytes 3932160 | tf_op jit(solution)/shard_map/pallas_call | solution.py:295
  15.3 0.6 collective-permute-done.4.a1
  15.9 0.3 collective-permute-done.5.a2
  16.2 0.0 collective-permute-done.3.a0
  16.2 1.5 %collective-permute-start.10 = (bf16[256,256]{1,0:T(8,128)(2,1)S(1)}, bf16[256,256]{1,0:T(8,128)(2,1)S(1)}, u32[]{:S(2)}, u32[]{:S(2)}) collective-permute-start(bf16[256,256]{1,0:T(8,128)(2,1)S(1)} %shard_map.60.after), channel_id=1, source_target_pairs={{0,8},{4,12},{8,0},{12,4},{16,24},{20,28},{24,16},{28,20},{32,40},... | collective-permute-start | bytes 393224 | tf_op jit(solution)/shard_map/ppermute | solution.py:21
  17.7 0.0 collective-permute-done.6.zb
  17.8 0.1 collective-permute-start.7
  17.9 1.4 %collective-permute-start.11 = (bf16[256,256]{1,0:T(8,128)(2,1)S(1)}, bf16[256,256]{1,0:T(8,128)(2,1)S(1)}, u32[]{:S(2)}, u32[]{:S(2)}) collective-permute-start(bf16[256,256]{1,0:T(8,128)(2,1)S(1)} %shard_map.60.after), channel_id=1, source_target_pairs={{0,64},{4,68},{8,72},{12,76},{16,80},{20,84},{24,88},{28,92},{32,9... | collective-permute-start | bytes 393224 | tf_op jit(solution)/shard_map/ppermute | solution.py:21
  19.3 0.0 collective-permute-start.12
  19.3 0.8 %collective-permute-done.2.z2 = bf16[512,256]{1,0:T(8,128)(2,1)S(1)} collective-permute-done((bf16[512,256]{1,0:T(8,128)(2,1)S(1)}, bf16[512,256]{1,0:T(8,128)(2,1)S(1)}, u32[]{:S(2)}, u32[]{:S(2)}) %collective-permute-start.2) | collective-permute-done | bytes 262176 | tf_op jit(solution)/shard_map/ppermute | solution.py:21
  20.1 1.9 %collective-permute-start.8 = (bf16[256,256]{1,0:T(8,128)(2,1)S(1)}, bf16[256,256]{1,0:T(8,128)(2,1)S(1)}, u32[]{:S(2)}, u32[]{:S(2)}) collective-permute-start(bf16[256,256]{1,0:T(8,128)(2,1)S(1)} %get-tuple-element.54), channel_id=1, source_target_pairs={{0,32},{4,36},{8,40},{12,44},{16,48},{20,52},{24,56},{28,60},{32,0... | collective-permute-start | bytes 393224 | tf_op jit(solution)/shard_map/ppermute | solution.py:21
  22.0 0.9 %collective-permute-done.10.e = bf16[256,256]{1,0:T(8,128)(2,1)S(1)} collective-permute-done((bf16[256,256]{1,0:T(8,128)(2,1)S(1)}, bf16[256,256]{1,0:T(8,128)(2,1)S(1)}, u32[]{:S(2)}, u32[]{:S(2)}) %collective-permute-start.10) | collective-permute-done | bytes 131104 | tf_op jit(solution)/shard_map/ppermute | solution.py:21
  22.9 0.2 collective-permute-start.9
  23.0 2.4 %shard_map.61 = (f32[2,1024,128]{2,1,0:T(8,128)S(1)}, f32[2,1024,128]{2,1,0:T(8,128)S(1)}, f32[2,1024,128]{2,1,0:T(8,128)S(1)}, bf16[448,128]{1,0:T(8,128)(2,1)S(1)}) custom-call(s32[4]{0:T(128)S(1)} %pad_add_fusion.pos, s32[6,16]{1,0:T(8,128)S(1)} %copy-done.1, ...), custom_call_target="tpu_custom_call", output_to_operand_aliasing={{0}: (2, {}), {1}: (3, {}), {2}: (4, {})} | custom-call | flops 402653184 | bytes 5242880 | tf_op jit(solution)/shard_map/pallas_call | solution.py:295
  25.5 0.0 collective-permute-done.11.f
  25.5 0.0 collective-permute-done.12.g
  25.5 1.2 %collective-permute-done.8.h2 = bf16[256,256]{1,0:T(8,128)(2,1)S(1)} collective-permute-done((bf16[256,256]{1,0:T(8,128)(2,1)S(1)}, bf16[256,256]{1,0:T(8,128)(2,1)S(1)}, u32[]{:S(2)}, u32[]{:S(2)}) %collective-permute-start.8) | collective-permute-done | bytes 131104 | tf_op jit(solution)/shard_map/ppermute | solution.py:21
  26.7 2.8 %collective-permute-done.9.h3 = bf16[256,256]{1,0:T(8,128)(2,1)S(1)} collective-permute-done((bf16[256,256]{1,0:T(8,128)(2,1)S(1)}, bf16[256,256]{1,0:T(8,128)(2,1)S(1)}, u32[]{:S(2)}, u32[]{:S(2)}) %collective-permute-start.9) | collective-permute-done | bytes 131104 | tf_op jit(solution)/shard_map/ppermute | solution.py:21
  29.5 0.0 collective-permute-done.7.h1
  29.5 0.0 copy-start
  29.5 1.6 %shard_map.63 = (f32[2,1024,128]{2,1,0:T(8,128)S(1)}, f32[2,1024,128]{2,1,0:T(8,128)S(1)}, f32[2,1024,128]{2,1,0:T(8,128)S(1)}, bf16[512,256]{1,0:T(8,128)(2,1)S(1)}) custom-call(s32[4]{0:T(128)S(1)} %pad_add_fusion.pos, s32[6,16]{1,0:T(8,128)S(1)} %copy-done.1, ...), custom_call_target="tpu_custom_call", output_to_operand_aliasing={{0}: (2, {}), {1}: (3, {}), {2}: (4, {})} | custom-call | flops 134217728 | bytes 4833280 | tf_op jit(solution)/shard_map/pallas_call | solution.py:295
  31.1 3.0 %collective-permute-start.13 = (bf16[512,256]{1,0:T(8,128)(2,1)S(1)}, bf16[512,256]{1,0:T(8,128)(2,1)S(1)}, u32[]{:S(2)}, u32[]{:S(2)}) collective-permute-start(bf16[512,256]{1,0:T(8,128)(2,1)S(1)} %get-tuple-element.57.after), channel_id=1, source_target_pairs={{0,4},{4,0},{8,12},{12,8},{16,20},{20,16},{24,28},{28,24},{32,36},... | collective-permute-start | bytes 786440 | tf_op jit(solution)/shard_map/ppermute | solution.py:21
  34.1 0.0 copy-done
  34.1 0.9 %shard_map.64 = (bf16[512,256]{1,0:T(8,128)(2,1)S(1)}, f32[512,512]{1,0:T(8,128)S(1)}) custom-call(s32[4]{0:T(128)S(1)} %pad_add_fusion.pos, f32[2,1024,128]{2,1,0:T(8,128)S(1)} %get-tuple-element.55.acc, f32[2,1024,128]{2,1,0:T(8,128)S(1)} %get-tuple-element.56.total, bf16[512,2048]{1,0:T(8,128)(2,1)S(1)} %copy-done, ...), custom_call_target="tpu_custom_call" | custom-call | flops 134217728 | bytes 4194304 | tf_op jit(solution)/shard_map/pallas_call | solution.py:295
  34.9 0.3 collective-permute-done.13.back
  35.2 0.8 %shard_map.65 = (bf16[256,512]{1,0:T(8,128)(2,1)S(1)}, bf16[256,512]{1,0:T(8,128)(2,1)S(1)}) custom-call(s32[4]{0:T(128)S(1)} %pad_add_fusion.pos, f32[512,512]{1,0:T(8,128)S(1)} %get-tuple-element.59.part, bf16[512,256]{1,0:T(8,128)(2,1)S(1)} %collective-permute-done.13.back, bf16[512,2048]{1,0:T(8,128)(2,1)S(1)} %copy-done), custom_call_target="tpu_custom_call" | custom-call | flops 134217728 | bytes 3407872 | tf_op jit(solution)/shard_map/pallas_call | solution.py:295
  36.1 4.4 %collective-permute-start.18 = (bf16[256,512]{1,0:T(8,128)(2,1)S(1)}, bf16[256,512]{1,0:T(8,128)(2,1)S(1)}, u32[]{:S(2)}, u32[]{:S(2)}) collective-permute-start(bf16[256,512]{1,0:T(8,128)(2,1)S(1)} %get-tuple-element.66), channel_id=1, source_target_pairs={{0,3},{1,2},{2,1},{3,0},{4,7},{5,6},{6,5},{7,4},{8,11},{9,10},{10,... | collective-permute-start | bytes 786440 | tf_op jit(solution)/shard_map/ppermute | solution.py:25
  40.5 1.2 %collective-permute-start.15 = (bf16[256,512]{1,0:T(8,128)(2,1)S(1)}, bf16[256,512]{1,0:T(8,128)(2,1)S(1)}, u32[]{:S(2)}, u32[]{:S(2)}) collective-permute-start(bf16[256,512]{1,0:T(8,128)(2,1)S(1)} %get-tuple-element.60.after), channel_id=1, source_target_pairs={{0,1},{1,0},{2,3},{3,2},{4,5},{5,4},{6,7},{7,6},{8,9},{9,8},{10,11... | collective-permute-start | bytes 786440 | tf_op jit(solution)/shard_map/ppermute | solution.py:25
  41.7 1.5 %shard_map.66 = (bf16[256,512]{1,0:T(8,128)(2,1)S(1)}, bf16[256,512]{1,0:T(8,128)(2,1)S(1)}, f32[256,512]{1,0:T(8,128)S(1)}, f32[256,512]{1,0:T(8,128)S(1)}, f32[512,512]{1,0:T(8,128)S(1)}) custom-call(s32[4]{0:T(128)S(1)} %pad_add_fusion.pos, bf16[512,256]{1,0:T(8,128)(2,1)S(1)} %get-tuple-element.58.mine, ...), custom_call_target="tpu_custom_call" | custom-call | flops 805306368 | bytes 2621440 | tf_op jit(solution)/shard_map/pallas_call | solution.py:295
  43.2 1.2 %collective-permute-start.14 = (bf16[256,512]{1,0:T(8,128)(2,1)S(1)}, bf16[256,512]{1,0:T(8,128)(2,1)S(1)}, u32[]{:S(2)}, u32[]{:S(2)}) collective-permute-start(bf16[256,512]{1,0:T(8,128)(2,1)S(1)} %get-tuple-element.62), channel_id=1, source_target_pairs={{0,1},{1,0},{2,3},{3,2},{4,5},{5,4},{6,7},{7,6},{8,9},{9,8},{10,11... | collective-permute-start | bytes 786440 | tf_op jit(solution)/shard_map/ppermute | solution.py:25
  44.5 0.1 collective-permute-start.17
  44.6 9.5 %collective-permute-done.18.came = bf16[256,512]{1,0:T(8,128)(2,1)S(1)} collective-permute-done((bf16[256,512]{1,0:T(8,128)(2,1)S(1)}, bf16[256,512]{1,0:T(8,128)(2,1)S(1)}, u32[]{:S(2)}, u32[]{:S(2)}) %collective-permute-start.18) | collective-permute-done | bytes 262176 | tf_op jit(solution)/shard_map/ppermute | solution.py:25
  54.1 3.5 %collective-permute-start.19 = (bf16[256,512]{1,0:T(8,128)(2,1)S(1)}, bf16[256,512]{1,0:T(8,128)(2,1)S(1)}, u32[]{:S(2)}, u32[]{:S(2)}) collective-permute-start(bf16[256,512]{1,0:T(8,128)(2,1)S(1)} %shard_map.68), channel_id=1, source_target_pairs={{0,1},{1,0},{2,3},{3,2},{4,5},{5,4},{6,7},{7,6},{8,9},{9,8},{10,11... | collective-permute-start | bytes 786440 | tf_op jit(solution)/shard_map/ppermute | solution.py:25
  57.6 0.0 collective-permute-done.15.came
  57.6 1.2 %collective-permute-start.16 = (bf16[256,512]{1,0:T(8,128)(2,1)S(1)}, bf16[256,512]{1,0:T(8,128)(2,1)S(1)}, u32[]{:S(2)}, u32[]{:S(2)}) collective-permute-start(bf16[256,512]{1,0:T(8,128)(2,1)S(1)} %shard_map.67), channel_id=1, source_target_pairs={{0,3},{1,2},{2,1},{3,0},{4,7},{5,6},{6,5},{7,4},{8,11},{9,10},{10,... | collective-permute-start | bytes 786440 | tf_op jit(solution)/shard_map/ppermute | solution.py:25
  58.9 10.1 %collective-permute-done.14.up2 = bf16[256,512]{1,0:T(8,128)(2,1)S(1)} collective-permute-done((bf16[256,512]{1,0:T(8,128)(2,1)S(1)}, bf16[256,512]{1,0:T(8,128)(2,1)S(1)}, u32[]{:S(2)}, u32[]{:S(2)}) %collective-permute-start.14) | collective-permute-done | bytes 262176 | tf_op jit(solution)/shard_map/ppermute | solution.py:25
  69.0 0.0 collective-permute-done.17.down2
  69.0 5.8 %collective-permute-done.19.down3 = bf16[256,512]{1,0:T(8,128)(2,1)S(1)} collective-permute-done((bf16[256,512]{1,0:T(8,128)(2,1)S(1)}, bf16[256,512]{1,0:T(8,128)(2,1)S(1)}, u32[]{:S(2)}, u32[]{:S(2)}) %collective-permute-start.19) | collective-permute-done | bytes 262176 | tf_op jit(solution)/shard_map/ppermute | solution.py:25
  74.8 2.4 %collective-permute-done.16.up3 = bf16[256,512]{1,0:T(8,128)(2,1)S(1)} collective-permute-done((bf16[256,512]{1,0:T(8,128)(2,1)S(1)}, bf16[256,512]{1,0:T(8,128)(2,1)S(1)}, u32[]{:S(2)}, u32[]{:S(2)}) %collective-permute-start.16) | collective-permute-done | bytes 262176 | tf_op jit(solution)/shard_map/ppermute | solution.py:25
  77.1 0.9 %shard_map.69 = bf16[512,512]{1,0:T(8,128)(2,1)} custom-call(f32[512,512]{1,0:T(8,128)S(1)} %get-tuple-element.61.own, bf16[256,512]{1,0:T(8,128)(2,1)S(1)} %collective-permute-done.14.up2, bf16[256,512]{1,0:T(8,128)(2,1)S(1)} %collective-permute-done.16.up3, bf16[256,512]{1,0:T(8,128)(2,1)S(1)} %collective-permute-done.17.down2, ...), custom_call_target="tpu_custom_call" | custom-call | bytes 2097152 | tf_op jit(solution)/shard_map/pallas_call | solution.py:295
  (4 shorter events, 0.1 us)
Async XLA Ops:
  0.0 7.3 %copy-start.1 = (s32[6,16]{1,0:T(8,128)S(1)}, s32[6,16]{1,0:T(8,128)}, u32[]{:S(2)}) copy-start(s32[6,16]{1,0:T(8,128)} %offs.5) | copy-start | bytes 1156
  1.1 6.3 %collective-permute-start.1 = (bf16[2,512,256]{2,1,0:T(8,128)(2,1)S(1)}, bf16[2,512,256]{2,1,0:T(8,128)(2,1)S(1)}, u32[]{:S(2)}, u32[]{:S(2)}) collective-permute-start(bf16[2,512,256]{2,1,0:T(8,128)(2,1)S(1)} %shard_map.55.after), channel_id=1, source_target_pairs={{0,4},{4,0},{8,12},{12,8},{16,20},{20,16},{24,28},{28,24},{32,36},... | collective-permute-start | bytes 1572872 | tf_op jit(solution)/shard_map/ppermute | solution.py:21
  5.6 6.5 %collective-permute-start = (bf16[512,256]{1,0:T(8,128)(2,1)S(1)}, bf16[512,256]{1,0:T(8,128)(2,1)S(1)}, u32[]{:S(2)}, u32[]{:S(2)}) collective-permute-start(bf16[512,256]{1,0:T(8,128)(2,1)S(1)} %get-tuple-element.38.after), channel_id=1, source_target_pairs={{0,4},{4,0},{8,12},{12,8},{16,20},{20,16},{24,28},{28,24},{32,36},... | collective-permute-start | bytes 786440 | tf_op jit(solution)/shard_map/ppermute | solution.py:21
  8.4 9.4 %collective-permute-start.6 = (bf16[384,256]{1,0:T(8,128)(2,1)S(1)}, bf16[384,256]{1,0:T(8,128)(2,1)S(1)}, u32[]{:S(2)}, u32[]{:S(2)}) collective-permute-start(bf16[384,256]{1,0:T(8,128)(2,1)S(1)} %get-tuple-element.42.after.g34), channel_id=1, source_target_pairs={{0,8},{4,12},{8,0},{12,4},{16,24},{20,28},{24,16},{28,20},{32,40},... | collective-permute-start | bytes 589832 | tf_op jit(solution)/shard_map/ppermute | solution.py:21
  8.5 7.7 %collective-permute-start.3 = (bf16[320,256]{1,0:T(8,128)(2,1)S(1)}, bf16[320,256]{1,0:T(8,128)(2,1)S(1)}, u32[]{:S(2)}, u32[]{:S(2)}) collective-permute-start(bf16[320,256]{1,0:T(8,128)(2,1)S(1)} %get-tuple-element.48), channel_id=1, source_target_pairs={{0,16},{4,20},{8,24},{12,28},{16,0},{20,4},{24,8},{28,12},{32,48},... | collective-permute-start | bytes 491528 | tf_op jit(solution)/shard_map/ppermute | solution.py:21
  9.6 10.5 %collective-permute-start.2 = (bf16[512,256]{1,0:T(8,128)(2,1)S(1)}, bf16[512,256]{1,0:T(8,128)(2,1)S(1)}, u32[]{:S(2)}, u32[]{:S(2)}) collective-permute-start(bf16[512,256]{1,0:T(8,128)(2,1)S(1)} %get-tuple-element.46.g2), channel_id=1, source_target_pairs={{0,8},{4,12},{8,0},{12,4},{16,24},{20,28},{24,16},{28,20},{32,40},... | collective-permute-start | bytes 786440 | tf_op jit(solution)/shard_map/ppermute | solution.py:21
  9.9 6.0 %collective-permute-start.4 = (bf16[64,256]{1,0:T(8,128)(2,1)S(1)}, bf16[64,256]{1,0:T(8,128)(2,1)S(1)}, u32[]{:S(2)}, u32[]{:S(2)}) collective-permute-start(bf16[64,256]{1,0:T(8,128)(2,1)S(1)} %get-tuple-element.47.g5), channel_id=1, source_target_pairs={{0,32},{4,36},{8,40},{12,44},{16,48},{20,52},{24,56},{28,60},{32,0... | collective-permute-start | bytes 98312 | tf_op jit(solution)/shard_map/ppermute | solution.py:21
  12.1 4.1 %collective-permute-start.5 = (bf16[64,256]{1,0:T(8,128)(2,1)S(1)}, bf16[64,256]{1,0:T(8,128)(2,1)S(1)}, u32[]{:S(2)}, u32[]{:S(2)}) collective-permute-start(bf16[64,256]{1,0:T(8,128)(2,1)S(1)} %get-tuple-element.47.g5), channel_id=1, source_target_pairs={{0,48},{4,52},{8,56},{12,60},{16,32},{20,36},{24,40},{28,44},{32,1... | collective-permute-start | bytes 98312 | tf_op jit(solution)/shard_map/ppermute | solution.py:21
  16.2 6.7 %collective-permute-start.10 = (bf16[256,256]{1,0:T(8,128)(2,1)S(1)}, bf16[256,256]{1,0:T(8,128)(2,1)S(1)}, u32[]{:S(2)}, u32[]{:S(2)}) collective-permute-start(bf16[256,256]{1,0:T(8,128)(2,1)S(1)} %shard_map.60.after), channel_id=1, source_target_pairs={{0,8},{4,12},{8,0},{12,4},{16,24},{20,28},{24,16},{28,20},{32,40},... | collective-permute-start | bytes 393224 | tf_op jit(solution)/shard_map/ppermute | solution.py:21
  17.8 11.7 %collective-permute-start.7 = (bf16[512,256]{1,0:T(8,128)(2,1)S(1)}, bf16[512,256]{1,0:T(8,128)(2,1)S(1)}, u32[]{:S(2)}, u32[]{:S(2)}) collective-permute-start(bf16[512,256]{1,0:T(8,128)(2,1)S(1)} %get-tuple-element.53), channel_id=1, source_target_pairs={{0,16},{4,20},{8,24},{12,28},{16,0},{20,4},{24,8},{28,12},{32,48},... | collective-permute-start | bytes 786440 | tf_op jit(solution)/shard_map/ppermute | solution.py:21
  17.9 7.6 %collective-permute-start.11 = (bf16[256,256]{1,0:T(8,128)(2,1)S(1)}, bf16[256,256]{1,0:T(8,128)(2,1)S(1)}, u32[]{:S(2)}, u32[]{:S(2)}) collective-permute-start(bf16[256,256]{1,0:T(8,128)(2,1)S(1)} %shard_map.60.after), channel_id=1, source_target_pairs={{0,64},{4,68},{8,72},{12,76},{16,80},{20,84},{24,88},{28,92},{32,9... | collective-permute-start | bytes 393224 | tf_op jit(solution)/shard_map/ppermute | solution.py:21
  19.3 6.2 %collective-permute-start.12 = (bf16[256,256]{1,0:T(8,128)(2,1)S(1)}, bf16[256,256]{1,0:T(8,128)(2,1)S(1)}, u32[]{:S(2)}, u32[]{:S(2)}) collective-permute-start(bf16[256,256]{1,0:T(8,128)(2,1)S(1)} %shard_map.60.after), channel_id=1, source_target_pairs={{0,72},{4,76},{8,64},{12,68},{16,88},{20,92},{24,80},{28,84},{32,1... | collective-permute-start | bytes 393224 | tf_op jit(solution)/shard_map/ppermute | solution.py:21
  20.1 6.6 %collective-permute-start.8 = (bf16[256,256]{1,0:T(8,128)(2,1)S(1)}, bf16[256,256]{1,0:T(8,128)(2,1)S(1)}, u32[]{:S(2)}, u32[]{:S(2)}) collective-permute-start(bf16[256,256]{1,0:T(8,128)(2,1)S(1)} %get-tuple-element.54), channel_id=1, source_target_pairs={{0,32},{4,36},{8,40},{12,44},{16,48},{20,52},{24,56},{28,60},{32,0... | collective-permute-start | bytes 393224 | tf_op jit(solution)/shard_map/ppermute | solution.py:21
  22.9 6.6 %collective-permute-start.9 = (bf16[256,256]{1,0:T(8,128)(2,1)S(1)}, bf16[256,256]{1,0:T(8,128)(2,1)S(1)}, u32[]{:S(2)}, u32[]{:S(2)}) collective-permute-start(bf16[256,256]{1,0:T(8,128)(2,1)S(1)} %get-tuple-element.54), channel_id=1, source_target_pairs={{0,48},{4,52},{8,56},{12,60},{16,32},{20,36},{24,40},{28,44},{32,1... | collective-permute-start | bytes 393224 | tf_op jit(solution)/shard_map/ppermute | solution.py:21
  29.5 4.6 %copy-start = (bf16[512,2048]{1,0:T(8,128)(2,1)S(1)}, bf16[512,2048]{1,0:T(8,128)(2,1)}, u32[]{:S(2)}) copy-start(bf16[512,2048]{1,0:T(8,128)(2,1)} %w.5) | copy-start | bytes 6291460
  31.1 4.1 %collective-permute-start.13 = (bf16[512,256]{1,0:T(8,128)(2,1)S(1)}, bf16[512,256]{1,0:T(8,128)(2,1)S(1)}, u32[]{:S(2)}, u32[]{:S(2)}) collective-permute-start(bf16[512,256]{1,0:T(8,128)(2,1)S(1)} %get-tuple-element.57.after), channel_id=1, source_target_pairs={{0,4},{4,0},{8,12},{12,8},{16,20},{20,16},{24,28},{28,24},{32,36},... | collective-permute-start | bytes 786440 | tf_op jit(solution)/shard_map/ppermute | solution.py:21
  36.1 18.0 %collective-permute-start.18 = (bf16[256,512]{1,0:T(8,128)(2,1)S(1)}, bf16[256,512]{1,0:T(8,128)(2,1)S(1)}, u32[]{:S(2)}, u32[]{:S(2)}) collective-permute-start(bf16[256,512]{1,0:T(8,128)(2,1)S(1)} %get-tuple-element.66), channel_id=1, source_target_pairs={{0,3},{1,2},{2,1},{3,0},{4,7},{5,6},{6,5},{7,4},{8,11},{9,10},{10,... | collective-permute-start | bytes 786440 | tf_op jit(solution)/shard_map/ppermute | solution.py:25
  40.5 17.1 %collective-permute-start.15 = (bf16[256,512]{1,0:T(8,128)(2,1)S(1)}, bf16[256,512]{1,0:T(8,128)(2,1)S(1)}, u32[]{:S(2)}, u32[]{:S(2)}) collective-permute-start(bf16[256,512]{1,0:T(8,128)(2,1)S(1)} %get-tuple-element.60.after), channel_id=1, source_target_pairs={{0,1},{1,0},{2,3},{3,2},{4,5},{5,4},{6,7},{7,6},{8,9},{9,8},{10,11... | collective-permute-start | bytes 786440 | tf_op jit(solution)/shard_map/ppermute | solution.py:25
  43.2 25.8 %collective-permute-start.14 = (bf16[256,512]{1,0:T(8,128)(2,1)S(1)}, bf16[256,512]{1,0:T(8,128)(2,1)S(1)}, u32[]{:S(2)}, u32[]{:S(2)}) collective-permute-start(bf16[256,512]{1,0:T(8,128)(2,1)S(1)} %get-tuple-element.62), channel_id=1, source_target_pairs={{0,1},{1,0},{2,3},{3,2},{4,5},{5,4},{6,7},{7,6},{8,9},{9,8},{10,11... | collective-permute-start | bytes 786440 | tf_op jit(solution)/shard_map/ppermute | solution.py:25
  44.5 24.5 %collective-permute-start.17 = (bf16[256,512]{1,0:T(8,128)(2,1)S(1)}, bf16[256,512]{1,0:T(8,128)(2,1)S(1)}, u32[]{:S(2)}, u32[]{:S(2)}) collective-permute-start(bf16[256,512]{1,0:T(8,128)(2,1)S(1)} %get-tuple-element.64), channel_id=1, source_target_pairs={{0,3},{1,2},{2,1},{3,0},{4,7},{5,6},{6,5},{7,4},{8,11},{9,10},{10,... | collective-permute-start | bytes 786440 | tf_op jit(solution)/shard_map/ppermute | solution.py:25
  54.1 20.6 %collective-permute-start.19 = (bf16[256,512]{1,0:T(8,128)(2,1)S(1)}, bf16[256,512]{1,0:T(8,128)(2,1)S(1)}, u32[]{:S(2)}, u32[]{:S(2)}) collective-permute-start(bf16[256,512]{1,0:T(8,128)(2,1)S(1)} %shard_map.68), channel_id=1, source_target_pairs={{0,1},{1,0},{2,3},{3,2},{4,5},{5,4},{6,7},{7,6},{8,9},{9,8},{10,11... | collective-permute-start | bytes 786440 | tf_op jit(solution)/shard_map/ppermute | solution.py:25
  57.6 19.5 %collective-permute-start.16 = (bf16[256,512]{1,0:T(8,128)(2,1)S(1)}, bf16[256,512]{1,0:T(8,128)(2,1)S(1)}, u32[]{:S(2)}, u32[]{:S(2)}) collective-permute-start(bf16[256,512]{1,0:T(8,128)(2,1)S(1)} %shard_map.67), channel_id=1, source_target_pairs={{0,3},{1,2},{2,1},{3,0},{4,7},{5,6},{6,5},{7,4},{8,11},{9,10},{10,... | collective-permute-start | bytes 786440 | tf_op jit(solution)/shard_map/ppermute | solution.py:25

commit v4 on v3

--- a/solution.py
+++ b/solution.py
@@ -69,19 +69,16 @@
         buf[base + j, there, :] = theirs[:, cols].astype(F32)
 
 
-def pick_kernel(pos, offs, mkv, rkv, after, g34, g2, g53, g5, buf):
-    del after
+def pick_kernel(pos, offs, mkv, rkv, g34, g2, g5, buf):
     for i in range(2):
         fill(buf, 2 * i, pos, mkv.at[i], rkv.at[i])
-    places = {3: ((g34, 0), (g53, 64)), 4: ((g34, 256),), 5: ((g53, 0), (g5, 0)), 2: ((g2, 0),)}
-    for level, where in places.items():
+    for level, dst, row in ((5, g5, 0), (3, g34, 0), (4, g34, 256), (2, g2, 0)):
         n = CHIP >> level
         for j in range(2):
             rows = used(offs[level, pos[1] + j], level)
             for i in range(2):
-                part = buf[2 * i + j, rows, :].astype(BF16)
-                for dst, row in where:
-                    dst[row + j * n : row + (j + 1) * n, i * HD : (i + 1) * HD] = part
+                at = slice(row + j * n, row + (j + 1) * n)
+                dst[at, i * HD : (i + 1) * HD] = buf[2 * i + j, rows, :].astype(BF16)
 
 
 def raw_scores(q, k):
@@ -132,23 +129,32 @@
             peak[j, rows, :] = m
 
 
-def own_tile_kernel(pos, q, kv, after, *state):
-    del after
+def other_tile_kernel(pos, q, kv, after, *state):
+    del after
+    tile(TOK - pos[0] * TOK, q, kv, state)
+
+
+def own_tile_kernel(pos, acc0, peak0, total0, q, kv, after, *state):
+    del acc0, peak0, total0, after
     tile(pos[0] * TOK, q, kv, state)
 
 
-def other_tile_kernel(pos, acc0, peak0, total0, q, kv, after, *state):
-    del acc0, peak0, total0, after
-    tile(TOK - pos[0] * TOK, q, kv, state)
-
-
-def gather_kernel(g5, a0, a1, a2, after, out):
-    del after
-    for i, part in enumerate((g5, a0, a1, a2)):
-        out[64 * i : 64 * (i + 1), :] = part[:64, :]
-
-
-def pair_kernel(g34, zb, p1, p2):
+def mix_kernel(g5, y5, g34, after, u0, u1):
+    del after
+    for dst in (u0, u1):
+        dst[:64, :] = g5[...]
+        dst[64:128, :] = y5[...]
+    u0[128:, :] = g34[:256, :]
+
+
+def gather_kernel(u1, a0, a1, a2, after, out):
+    del after
+    for i, part in enumerate((u1, a0, a1, a2)):
+        out[128 * i : 128 * (i + 1), :] = part[:128, :]
+
+
+def pair_kernel(g34, zb, after, p1, p2):
+    del after
     for dst in (p1, p2):
         dst[:128, :] = g34[256:, :]
         dst[128:256, :] = zb[256:, :]
@@ -160,7 +166,7 @@
     span = lax.rem(pos[2], 1 << (level - 1))
     code = lax.broadcasted_iota(jnp.int32, (1, TOK), 1) // n
     if level == 5:
-        code = ((code & 3) << 1) | ((code >> 2) & 1) | (code & 8)
+        code = (code & 6) | ((code & 1) << 3) | (code >> 3)
     bias = jnp.where((code == 0) | ((span ^ code) < span), 0.0, -jnp.inf)
     s = raw_scores(q, jnp.concatenate([x[:, :HD] for x in blocks], axis=0)) + bias
     row = lax.broadcasted_iota(jnp.int32, s.shape, 0)
@@ -198,38 +204,55 @@
         merge(state, j, rows[j], parts[j])
 
 
-def finish(acc, total, rows, dst):
-    for j in range(2):
-        dst[:, j * HD : (j + 1) * HD] = (acc[j, rows, :] * (1.0 / total[j, rows, :])).astype(BF16)
+def far_parts(pos, offs, bq, qrow, level, j, blocks):
+    n = CHIP >> level
+    rows = used(offs[level, pos[1] + j], level)
+    scores = far_scores(pos, bq[qrow + j * n : qrow + (j + 1) * n, :], blocks, level)
+    return j, rows, scores, far_values(blocks)
+
+
+def merge_all(work, state):
+    parts = softmax_parts([x[2] for x in work], [x[3] for x in work])
+    for (j, rows, _, _), part in zip(work, parts):
+        merge(state, j, rows, part)
+
+
+def third_kernel(pos, offs, acc0, peak0, total0, bq, g34, a0, zb, h1, *state):
+    del acc0, peak0, total0
+    work = []
+    for j in range(2):
+        at = slice(j * 128, (j + 1) * 128)
+        blocks = [g34[at], zb[at], a0[128 + j * 128 : 256 + j * 128], h1[256 + j * 128 : 384 + j * 128]]
+        work.append(far_parts(pos, offs, bq, 192, 3, j, blocks))
+    merge_all(work, state)
 
 
 def far_kernel(
-    pos, offs, acc0, peak0, total0, bq, g34, g5, a0, a1, a2, zb, h1, h2, h3, e, f, g, acc, peak, total, other
+    pos, offs, acc0, peak0, total0, bq, g34, u1, a0, a1, a2, zb, h1, h2, h3, e, acc, peak, total, other
 ):
     del acc0, peak0, total0
     work = []
-    for level, qrow in ((3, 192), (4, 64), (5, 0)):
+    for level, qrow in ((4, 64), (5, 0)):
         n = CHIP >> level
         for j in range(2):
 
             def cut(ref, row):
                 return ref[row + j * n : row + (j + 1) * n]
 
-            if level == 3:
-                blocks = [cut(g34, 0), cut(zb, 0), cut(a0, 64), cut(h1, 256)]
-            elif level == 4:
+            if level == 4:
                 blocks = [cut(g34, 256), cut(zb, 256)]
                 blocks += [cut(x, row) for x in (h1, h2, h3) for row in (0, 128)]
             else:
-                blocks = [cut(x, 0) for x in (g5, a0, a1, a2)]
-                blocks += [cut(x, 64 * i) for x in (e, f, g) for i in range(4)]
-            rows = used(offs[level, pos[1] + j], level)
-            scores = far_scores(pos, cut(bq, qrow), blocks, level)
-            work.append((j, rows, scores, far_values(blocks)))
-    parts = softmax_parts([x[2] for x in work], [x[3] for x in work])
-    for (j, rows, _, _), part in zip(work, parts):
-        merge((acc, peak, total), j, rows, part)
+                blocks = [cut(x, row) for x in (u1, a0, a1, a2) for row in (0, 64)]
+                blocks += [cut(e, 64 * i) for i in range(8)]
+            work.append(far_parts(pos, offs, bq, qrow, level, j, blocks))
+    merge_all(work, (acc, peak, total))
     finish(acc, total, halves(pos)[1], other)
+
+
+def finish(acc, total, rows, dst):
+    for j in range(2):
+        dst[:, j * HD : (j + 1) * HD] = (acc[j, rows, :] * (1.0 / total[j, rows, :])).astype(BF16)
 
 
 def dots(pos, far, rows, w, dest):
@@ -330,25 +353,24 @@
     )
     rq = swap(oq, CORE)
     states = [((2, CHIP, HD), F32)] * 3
-    state = call(own_tile_kernel, (pos,), (mq, mkv), states, flops=2 * unit, unread=(oq,))
-    g34, g2, g53, g5 = call(
+    g34, g2, g5 = call(
         pick_kernel,
         (pos, offsets),
         (mkv, rkv),
-        [rows(384), rows(512), rows(320), rows(64)],
+        [rows(384), rows(512), rows(64)],
         [pltpu.VMEM((4, CHIP, HD), F32)],
-        unread=(state[0],),
-    )
-    zb = swap(g34, Z)
-    a0, a1, a2 = swap(g53, X1), swap(g5, X2), swap(g5, X1 | X2)
-    z2 = swap(g2, Z)
+    )
+    y5, zb, z2 = swap(g5, Y1), swap(g34, Z), swap(g2, Z)
+    state = call(other_tile_kernel, (pos,), (rq, rkv), states, flops=2 * unit, unread=(g34,))
+    u0, u1 = call(mix_kernel, (), (g5, y5, g34), [rows(384), rows(128)], unread=(state[0],))
+    a0, a1, a2 = swap(u0, X1), swap(u1, X2), swap(u1, X1 | X2)
+    p1, p2 = call(pair_kernel, (), (g34, zb), [rows(512), rows(256)], unread=(u1,))
+    h1, h2, h3 = swap(p1, X1), swap(p2, X2), swap(p2, X1 | X2)
     state = call(
-        other_tile_kernel, (pos,), (*state, rq, rkv), states, flops=2 * unit, unread=(g34,), inplace=3
-    )
-    p1, p2 = call(pair_kernel, (), (g34, zb), [rows(512), rows(256)])
-    h1, h2, h3 = swap(p1, X1), swap(p2, X2), swap(p2, X1 | X2)
-    x5 = call(gather_kernel, (), (g5, a0, a1, a2), [rows(256)], unread=(state[0],))[0]
-    e, f, g = swap(x5, Z), swap(x5, Y1), swap(x5, Y1 | Z)
+        own_tile_kernel, (pos,), (*state, mq, mkv), states, flops=2 * unit, unread=(p1,), inplace=3
+    )
+    x5 = call(gather_kernel, (), (u1, a0, a1, a2), [rows(512)], unread=(state[0],))[0]
+    e = swap(x5, Z)
     *state, bq = call(
         near_kernel,
         (pos, offsets),
@@ -359,10 +381,13 @@
         unread=(x5,),
         inplace=3,
     )
+    state = call(
+        third_kernel, (pos, offsets), (*state, bq, g34, a0, zb, h1), states, flops=unit // 2, inplace=3
+    )
     acc, _, total, other = call(
         far_kernel,
         (pos, offsets),
-        (*state, bq, g34, g5, a0, a1, a2, zb, h1, h2, h3, e, f, g),
+        (*state, bq, g34, u1, a0, a1, a2, zb, h1, h2, h3, e),
         states + [rows(TOK)],
         flops=unit,
         inplace=3,

time: 78.3 us -> 77.2 us (0.986)
  starting transfers between devices: 28.6 us -> 26.4 us
  Pallas kernels: 14.6 us -> 15.5 us
    ppermute x14 -> x13, starting transfers between devices: 16.9 us -> 14.6 us  [swap(): return lax.ppermute(block, 'ctx', [(i, i ^ bits) for i in range(64)])]
    pallas_call x15 -> x17, Pallas kernels: 14.6 us -> 15.5 us  [call(): pl.pallas_call(kernel, in_specs=[SMEM] * len(scalars) + [inside] * len(ar...]
    ppermute x6, waiting for transfers between devices: 27.8 us -> 28.6 us  [cross(): return lax.ppermute(block, 'head', [(i, i ^ bits) for i in range(4)])]
    ppermute x14 -> x13, waiting for transfers between devices: 6.85 us -> 6.22 us  [swap(): return lax.ppermute(block, 'ctx', [(i, i ^ bits) for i in range(64)])]
  transfers between devices with their start and end apart: 20 -> 19, of which waited for: 11 -> 8; matrix products, arithmetic and copies ran while one was open for 0% -> 0% of each run, Pallas kernels for 13% -> 15%
where the time goes in v4:
time: 77.2 us; the launch traced here: 77.1 us
  waiting for transfers between devices  34.8 us (45%)
  starting transfers between devices  26.4 us (34%)
  Pallas kernels  15.5 us (20%)
    ppermute x6, waiting for transfers between devices, cross(): return lax.ppermute(block, 'head', [(i, i ^ bits) for i in range(4)])  28.6 us
    pallas_call x17, Pallas kernels, call(): pl.pallas_call(kernel, in_specs=[SMEM] * len(scalars) + [inside] * len(ar...  15.5 us
    ppermute x13, starting transfers between devices, swap(): return lax.ppermute(block, 'ctx', [(i, i ^ bits) for i in range(64)])  14.6 us
    ppermute x6, starting transfers between devices, cross(): return lax.ppermute(block, 'head', [(i, i ^ bits) for i in range(4)])  11.8 us
    ppermute x13, waiting for transfers between devices, swap(): return lax.ppermute(block, 'ctx', [(i, i ^ bits) for i in range(64)])  6.22 us
  transfers between devices with their start and end apart: 19, of which 8 were waited for; matrix products, arithmetic and copies ran while one was open for 0% of the time, Pallas kernels for 15%

profile of v4, /device:TPU:1, one launch (start us, length us, event | category | flops | bytes accessed | tf_op | source)
XLA Modules:
  0.0 77.1 jit_solution(12394566161548539072)
XLA Ops:
  0.0 0.0 copy-start.1
  0.0 1.1 %shard_map.55.after = bf16[2,512,256]{2,1,0:T(8,128)(2,1)S(1)} custom-call(bf16[512,512]{1,0:T(8,128)(2,1)} %k.3, bf16[512,512]{1,0:T(8,128)(2,1)} %v.3), custom_call_target="tpu_custom_call" | custom-call | bytes 1048576 | tf_op jit(solution)/shard_map/pallas_call | solution.py:318
  1.1 3.3 %collective-permute-start.1 = (bf16[2,512,256]{2,1,0:T(8,128)(2,1)S(1)}, bf16[2,512,256]{2,1,0:T(8,128)(2,1)S(1)}, u32[]{:S(2)}, u32[]{:S(2)}) collective-permute-start(bf16[2,512,256]{2,1,0:T(8,128)(2,1)S(1)} %shard_map.55.after), channel_id=1, source_target_pairs={{0,4},{4,0},{8,12},{12,8},{16,20},{20,16},{24,28},{28,24},{32,36},... | collective-permute-start | bytes 1572872 | tf_op jit(solution)/shard_map/ppermute | solution.py:21
  4.4 1.2 %shard_map.56 = (bf16[512,256]{1,0:T(8,128)(2,1)S(1)}, bf16[2,512,256]{2,1,0:T(8,128)(2,1)S(1)}, bf16[512,256]{1,0:T(8,128)(2,1)S(1)}) custom-call(bf16[512,512]{1,0:T(8,128)(2,1)} %q.1, bf16[512,512]{1,0:T(8,128)(2,1)} %k.3, bf16[512,512]{1,0:T(8,128)(2,1)} %v.3, bf16[2,512,256]{2,1,0:T(8,128)(2,1)S(1)} %shard_map.55.after), custom_call_target="tpu_custom_call" | custom-call | bytes 1572864 | tf_op jit(solution)/shard_map/pallas_call | solution.py:318
  5.6 0.1 collective-permute-start
  5.7 0.1 pad_add_fusion.pos
  5.8 0.1 collective-permute-done.1.rkv.kv
  5.9 0.0 copy-done.1
  5.9 1.0 %shard_map.57 = (bf16[384,256]{1,0:T(8,128)(2,1)S(1)}, bf16[512,256]{1,0:T(8,128)(2,1)S(1)}, bf16[64,256]{1,0:T(8,128)(2,1)S(1)}) custom-call(s32[4]{0:T(128)S(1)} %pad_add_fusion.pos, s32[6,16]{1,0:T(8,128)S(1)} %copy-done.1, bf16[2,512,256]{2,1,0:T(8,128)(2,1)S(1)} %get-tuple-element.41.mkv.kv, bf16[2,512,256]{2,1,0:T(8,128)(2,1)S(1)} %collective-permute-done.1.rkv.kv), custom_call_target="tpu_custom_call" | custom-call | bytes 1048576 | tf_op jit(solution)/shard_map/pallas_call | solution.py:318
  7.0 0.1 collective-permute-start.3
  7.1 1.2 %collective-permute-start.2 = (bf16[384,256]{1,0:T(8,128)(2,1)S(1)}, bf16[384,256]{1,0:T(8,128)(2,1)S(1)}, u32[]{:S(2)}, u32[]{:S(2)}) collective-permute-start(bf16[384,256]{1,0:T(8,128)(2,1)S(1)} %get-tuple-element.42.after.g34), channel_id=1, source_target_pairs={{0,8},{4,12},{8,0},{12,4},{16,24},{20,28},{24,16},{28,20},{32,40},... | collective-permute-start | bytes 589832 | tf_op jit(solution)/shard_map/ppermute | solution.py:21
  8.2 0.0 collective-permute-done.q.rq
  8.2 1.5 %shard_map.58 = (f32[2,1024,128]{2,1,0:T(8,128)S(1)}, f32[2,1024,128]{2,1,0:T(8,128)S(1)}, f32[2,1024,128]{2,1,0:T(8,128)S(1)}) custom-call(s32[4]{0:T(128)S(1)} %pad_add_fusion.pos, bf16[512,256]{1,0:T(8,128)(2,1)S(1)} %collective-permute-done.q.rq, bf16[2,512,256]{2,1,0:T(8,128)(2,1)S(1)} %collective-permute-done.1.rkv.kv, ...), custom_call_target="tpu_custom_call" | custom-call | flops 268435456 | bytes 786432 | tf_op jit(solution)/shard_map/pallas_call | solution.py:318
  9.8 0.0 collective-permute-done.3.y5
  9.8 1.3 %collective-permute-start.5 = (bf16[384,256]{1,0:T(8,128)(2,1)S(1)}, bf16[384,256]{1,0:T(8,128)(2,1)S(1)}, u32[]{:S(2)}, u32[]{:S(2)}) collective-permute-start(bf16[384,256]{1,0:T(8,128)(2,1)S(1)} %get-tuple-element.54), channel_id=1, source_target_pairs={{0,16},{4,20},{8,24},{12,28},{16,0},{20,4},{24,8},{28,12},{32,48},... | collective-permute-start | bytes 589832 | tf_op jit(solution)/shard_map/ppermute | solution.py:21
  11.1 2.5 %collective-permute-start.6 = (bf16[128,256]{1,0:T(8,128)(2,1)S(1)}, bf16[128,256]{1,0:T(8,128)(2,1)S(1)}, u32[]{:S(2)}, u32[]{:S(2)}) collective-permute-start(bf16[128,256]{1,0:T(8,128)(2,1)S(1)} %get-tuple-element.48.after.u1), channel_id=1, source_target_pairs={{0,32},{4,36},{8,40},{12,44},{16,48},{20,52},{24,56},{28,60},{32,0... | collective-permute-start | bytes 196616 | tf_op jit(solution)/shard_map/ppermute | solution.py:21
  13.6 0.2 collective-permute-start.7
  13.8 0.4 collective-permute-start.4
  14.1 0.0 collective-permute-done.2.zb
  14.2 0.1 collective-permute-start.8
  14.3 1.5 %shard_map.61 = (f32[2,1024,128]{2,1,0:T(8,128)S(1)}, f32[2,1024,128]{2,1,0:T(8,128)S(1)}, f32[2,1024,128]{2,1,0:T(8,128)S(1)}) custom-call(s32[4]{0:T(128)S(1)} %pad_add_fusion.pos, f32[2,1024,128]{2,1,0:T(8,128)S(1)} %get-tuple-element.43.after.acc0, ...), custom_call_target="tpu_custom_call", output_to_operand_aliasing={{0}: (1, {}), {1}: (2, {}), {2}: (3, {})} | custom-call | flops 268435456 | bytes 3932160 | tf_op jit(solution)/shard_map/pallas_call | solution.py:318
  15.8 2.9 %collective-permute-done.6.a1 = bf16[128,256]{1,0:T(8,128)(2,1)S(1)} collective-permute-done((bf16[128,256]{1,0:T(8,128)(2,1)S(1)}, bf16[128,256]{1,0:T(8,128)(2,1)S(1)}, u32[]{:S(2)}, u32[]{:S(2)}) %collective-permute-start.6) | collective-permute-done | bytes 65568 | tf_op jit(solution)/shard_map/ppermute | solution.py:21
  18.7 0.0 collective-permute-done.7.a2
  18.7 0.0 collective-permute-done.5.a0
  18.7 0.1 collective-permute-start.11
  18.8 0.7 collective-permute-start.10
  19.5 1.2 %collective-permute-start.9 = (bf16[256,256]{1,0:T(8,128)(2,1)S(1)}, bf16[256,256]{1,0:T(8,128)(2,1)S(1)}, u32[]{:S(2)}, u32[]{:S(2)}) collective-permute-start(bf16[256,256]{1,0:T(8,128)(2,1)S(1)} %get-tuple-element.62), channel_id=1, source_target_pairs={{0,32},{4,36},{8,40},{12,44},{16,48},{20,52},{24,56},{28,60},{32,0... | collective-permute-start | bytes 393224 | tf_op jit(solution)/shard_map/ppermute | solution.py:21
  20.7 0.0 collective-permute-done.4.z2
  20.7 2.4 %shard_map.63 = (f32[2,1024,128]{2,1,0:T(8,128)S(1)}, f32[2,1024,128]{2,1,0:T(8,128)S(1)}, f32[2,1024,128]{2,1,0:T(8,128)S(1)}, bf16[448,128]{1,0:T(8,128)(2,1)S(1)}) custom-call(s32[4]{0:T(128)S(1)} %pad_add_fusion.pos, s32[6,16]{1,0:T(8,128)S(1)} %copy-done.1, ...), custom_call_target="tpu_custom_call", output_to_operand_aliasing={{0}: (2, {}), {1}: (3, {}), {2}: (4, {})} | custom-call | flops 402653184 | bytes 5242880 | tf_op jit(solution)/shard_map/pallas_call | solution.py:318
  23.1 0.0 collective-permute-done.8.h1
  23.1 1.2 %shard_map.64 = (f32[2,1024,128]{2,1,0:T(8,128)S(1)}, f32[2,1024,128]{2,1,0:T(8,128)S(1)}, f32[2,1024,128]{2,1,0:T(8,128)S(1)}) custom-call(s32[4]{0:T(128)S(1)} %pad_add_fusion.pos, s32[6,16]{1,0:T(8,128)S(1)} %copy-done.1, f32[2,1024,128]{2,1,0:T(8,128)S(1)} %get-tuple-element.55.acc0, ...), custom_call_target="tpu_custom_call", output_to_operand_aliasing={{0}: (2, {}), {1}: (3, {}), {2}: (4, {})} | custom-call | flops 67108864 | bytes 4112384 | tf_op jit(solution)/shard_map/pallas_call | solution.py:318
  24.3 0.0 collective-permute-done.10.h3
  24.3 2.8 %collective-permute-done.9.h2 = bf16[256,256]{1,0:T(8,128)(2,1)S(1)} collective-permute-done((bf16[256,256]{1,0:T(8,128)(2,1)S(1)}, bf16[256,256]{1,0:T(8,128)(2,1)S(1)}, u32[]{:S(2)}, u32[]{:S(2)}) %collective-permute-start.9) | collective-permute-done | bytes 131104 | tf_op jit(solution)/shard_map/ppermute | solution.py:21
  27.1 0.0 collective-permute-done.11.e
  27.1 0.0 copy-start
  27.1 1.4 %shard_map.65 = (f32[2,1024,128]{2,1,0:T(8,128)S(1)}, f32[2,1024,128]{2,1,0:T(8,128)S(1)}, f32[2,1024,128]{2,1,0:T(8,128)S(1)}, bf16[512,256]{1,0:T(8,128)(2,1)S(1)}) custom-call(s32[4]{0:T(128)S(1)} %pad_add_fusion.pos, s32[6,16]{1,0:T(8,128)S(1)} %copy-done.1, ...), custom_call_target="tpu_custom_call", output_to_operand_aliasing={{0}: (2, {}), {1}: (3, {}), {2}: (4, {})} | custom-call | flops 134217728 | bytes 4833280 | tf_op jit(solution)/shard_map/pallas_call | solution.py:318
  28.5 3.5 %collective-permute-start.12 = (bf16[512,256]{1,0:T(8,128)(2,1)S(1)}, bf16[512,256]{1,0:T(8,128)(2,1)S(1)}, u32[]{:S(2)}, u32[]{:S(2)}) collective-permute-start(bf16[512,256]{1,0:T(8,128)(2,1)S(1)} %get-tuple-element.65.after), channel_id=1, source_target_pairs={{0,4},{4,0},{8,12},{12,8},{16,20},{20,16},{24,28},{28,24},{32,36},... | collective-permute-start | bytes 786440 | tf_op jit(solution)/shard_map/ppermute | solution.py:21
  32.0 0.0 copy-done
  32.0 0.9 %shard_map.66 = (bf16[512,256]{1,0:T(8,128)(2,1)S(1)}, f32[512,512]{1,0:T(8,128)S(1)}) custom-call(s32[4]{0:T(128)S(1)} %pad_add_fusion.pos, f32[2,1024,128]{2,1,0:T(8,128)S(1)} %get-tuple-element.63.acc, f32[2,1024,128]{2,1,0:T(8,128)S(1)} %get-tuple-element.64.total, bf16[512,2048]{1,0:T(8,128)(2,1)S(1)} %copy-done, ...), custom_call_target="tpu_custom_call" | custom-call | flops 134217728 | bytes 4194304 | tf_op jit(solution)/shard_map/pallas_call | solution.py:318
  32.9 0.3 collective-permute-done.12.back
  33.2 0.8 %shard_map.67 = (bf16[256,512]{1,0:T(8,128)(2,1)S(1)}, bf16[256,512]{1,0:T(8,128)(2,1)S(1)}) custom-call(s32[4]{0:T(128)S(1)} %pad_add_fusion.pos, f32[512,512]{1,0:T(8,128)S(1)} %get-tuple-element.67.part, bf16[512,256]{1,0:T(8,128)(2,1)S(1)} %collective-permute-done.12.back, bf16[512,2048]{1,0:T(8,128)(2,1)S(1)} %copy-done), custom_call_target="tpu_custom_call" | custom-call | flops 134217728 | bytes 3407872 | tf_op jit(solution)/shard_map/pallas_call | solution.py:318
  34.0 5.2 %collective-permute-start.17 = (bf16[256,512]{1,0:T(8,128)(2,1)S(1)}, bf16[256,512]{1,0:T(8,128)(2,1)S(1)}, u32[]{:S(2)}, u32[]{:S(2)}) collective-permute-start(bf16[256,512]{1,0:T(8,128)(2,1)S(1)} %get-tuple-element.74), channel_id=1, source_target_pairs={{0,3},{1,2},{2,1},{3,0},{4,7},{5,6},{6,5},{7,4},{8,11},{9,10},{10,... | collective-permute-start | bytes 786440 | tf_op jit(solution)/shard_map/ppermute | solution.py:25
  39.3 1.2 %collective-permute-start.14 = (bf16[256,512]{1,0:T(8,128)(2,1)S(1)}, bf16[256,512]{1,0:T(8,128)(2,1)S(1)}, u32[]{:S(2)}, u32[]{:S(2)}) collective-permute-start(bf16[256,512]{1,0:T(8,128)(2,1)S(1)} %get-tuple-element.68.after), channel_id=1, source_target_pairs={{0,1},{1,0},{2,3},{3,2},{4,5},{5,4},{6,7},{7,6},{8,9},{9,8},{10,11... | collective-permute-start | bytes 786440 | tf_op jit(solution)/shard_map/ppermute | solution.py:25
  40.4 1.5 %shard_map.68 = (bf16[256,512]{1,0:T(8,128)(2,1)S(1)}, bf16[256,512]{1,0:T(8,128)(2,1)S(1)}, f32[256,512]{1,0:T(8,128)S(1)}, f32[256,512]{1,0:T(8,128)S(1)}, f32[512,512]{1,0:T(8,128)S(1)}) custom-call(s32[4]{0:T(128)S(1)} %pad_add_fusion.pos, bf16[512,256]{1,0:T(8,128)(2,1)S(1)} %get-tuple-element.66.mine, ...), custom_call_target="tpu_custom_call" | custom-call | flops 805306368 | bytes 2621440 | tf_op jit(solution)/shard_map/pallas_call | solution.py:318
  42.0 1.3 %collective-permute-start.13 = (bf16[256,512]{1,0:T(8,128)(2,1)S(1)}, bf16[256,512]{1,0:T(8,128)(2,1)S(1)}, u32[]{:S(2)}, u32[]{:S(2)}) collective-permute-start(bf16[256,512]{1,0:T(8,128)(2,1)S(1)} %get-tuple-element.70), channel_id=1, source_target_pairs={{0,1},{1,0},{2,3},{3,2},{4,5},{5,4},{6,7},{7,6},{8,9},{9,8},{10,11... | collective-permute-start | bytes 786440 | tf_op jit(solution)/shard_map/ppermute | solution.py:25
  43.3 0.1 collective-permute-start.16
  43.4 9.0 %collective-permute-done.17.came = bf16[256,512]{1,0:T(8,128)(2,1)S(1)} collective-permute-done((bf16[256,512]{1,0:T(8,128)(2,1)S(1)}, bf16[256,512]{1,0:T(8,128)(2,1)S(1)}, u32[]{:S(2)}, u32[]{:S(2)}) %collective-permute-start.17) | collective-permute-done | bytes 262176 | tf_op jit(solution)/shard_map/ppermute | solution.py:25
  52.4 1.0 %collective-permute-start.18 = (bf16[256,512]{1,0:T(8,128)(2,1)S(1)}, bf16[256,512]{1,0:T(8,128)(2,1)S(1)}, u32[]{:S(2)}, u32[]{:S(2)}) collective-permute-start(bf16[256,512]{1,0:T(8,128)(2,1)S(1)} %shard_map.70), channel_id=1, source_target_pairs={{0,1},{1,0},{2,3},{3,2},{4,5},{5,4},{6,7},{7,6},{8,9},{9,8},{10,11... | collective-permute-start | bytes 786440 | tf_op jit(solution)/shard_map/ppermute | solution.py:25
  53.4 1.1 %collective-permute-done.14.came = bf16[256,512]{1,0:T(8,128)(2,1)S(1)} collective-permute-done((bf16[256,512]{1,0:T(8,128)(2,1)S(1)}, bf16[256,512]{1,0:T(8,128)(2,1)S(1)}, u32[]{:S(2)}, u32[]{:S(2)}) %collective-permute-start.14) | collective-permute-done | bytes 262176 | tf_op jit(solution)/shard_map/ppermute | solution.py:25
  54.5 3.1 %collective-permute-start.15 = (bf16[256,512]{1,0:T(8,128)(2,1)S(1)}, bf16[256,512]{1,0:T(8,128)(2,1)S(1)}, u32[]{:S(2)}, u32[]{:S(2)}) collective-permute-start(bf16[256,512]{1,0:T(8,128)(2,1)S(1)} %shard_map.69), channel_id=1, source_target_pairs={{0,3},{1,2},{2,1},{3,0},{4,7},{5,6},{6,5},{7,4},{8,11},{9,10},{10,... | collective-permute-start | bytes 786440 | tf_op jit(solution)/shard_map/ppermute | solution.py:25
  57.6 10.2 %collective-permute-done.13.up2 = bf16[256,512]{1,0:T(8,128)(2,1)S(1)} collective-permute-done((bf16[256,512]{1,0:T(8,128)(2,1)S(1)}, bf16[256,512]{1,0:T(8,128)(2,1)S(1)}, u32[]{:S(2)}, u32[]{:S(2)}) %collective-permute-start.13) | collective-permute-done | bytes 262176 | tf_op jit(solution)/shard_map/ppermute | solution.py:25
  67.8 0.0 collective-permute-done.16.down2
  67.8 8.3 %collective-permute-done.18.down3 = bf16[256,512]{1,0:T(8,128)(2,1)S(1)} collective-permute-done((bf16[256,512]{1,0:T(8,128)(2,1)S(1)}, bf16[256,512]{1,0:T(8,128)(2,1)S(1)}, u32[]{:S(2)}, u32[]{:S(2)}) %collective-permute-start.18) | collective-permute-done | bytes 262176 | tf_op jit(solution)/shard_map/ppermute | solution.py:25
  76.1 0.0 collective-permute-done.15.up3
  76.1 0.9 %shard_map.71 = bf16[512,512]{1,0:T(8,128)(2,1)} custom-call(f32[512,512]{1,0:T(8,128)S(1)} %get-tuple-element.69.own, bf16[256,512]{1,0:T(8,128)(2,1)S(1)} %collective-permute-done.13.up2, bf16[256,512]{1,0:T(8,128)(2,1)S(1)} %collective-permute-done.15.up3, bf16[256,512]{1,0:T(8,128)(2,1)S(1)} %collective-permute-done.16.down2, ...), custom_call_target="tpu_custom_call" | custom-call | bytes 2097152 | tf_op jit(solution)/shard_map/pallas_call | solution.py:318
  (5 shorter events, 0.2 us)
Async XLA Ops:
  0.0 5.9 %copy-start.1 = (s32[6,16]{1,0:T(8,128)S(1)}, s32[6,16]{1,0:T(8,128)}, u32[]{:S(2)}) copy-start(s32[6,16]{1,0:T(8,128)} %offs.7) | copy-start | bytes 1156
  1.1 4.9 %collective-permute-start.1 = (bf16[2,512,256]{2,1,0:T(8,128)(2,1)S(1)}, bf16[2,512,256]{2,1,0:T(8,128)(2,1)S(1)}, u32[]{:S(2)}, u32[]{:S(2)}) collective-permute-start(bf16[2,512,256]{2,1,0:T(8,128)(2,1)S(1)} %shard_map.55.after), channel_id=1, source_target_pairs={{0,4},{4,0},{8,12},{12,8},{16,20},{20,16},{24,28},{28,24},{32,36},... | collective-permute-start | bytes 1572872 | tf_op jit(solution)/shard_map/ppermute | solution.py:21
  5.6 2.6 %collective-permute-start = (bf16[512,256]{1,0:T(8,128)(2,1)S(1)}, bf16[512,256]{1,0:T(8,128)(2,1)S(1)}, u32[]{:S(2)}, u32[]{:S(2)}) collective-permute-start(bf16[512,256]{1,0:T(8,128)(2,1)S(1)} %get-tuple-element.40), channel_id=1, source_target_pairs={{0,4},{4,0},{8,12},{12,8},{16,20},{20,16},{24,28},{28,24},{32,36},... | collective-permute-start | bytes 786440 | tf_op jit(solution)/shard_map/ppermute | solution.py:21
  7.0 2.9 %collective-permute-start.3 = (bf16[64,256]{1,0:T(8,128)(2,1)S(1)}, bf16[64,256]{1,0:T(8,128)(2,1)S(1)}, u32[]{:S(2)}, u32[]{:S(2)}) collective-permute-start(bf16[64,256]{1,0:T(8,128)(2,1)S(1)} %get-tuple-element.47.g5), channel_id=1, source_target_pairs={{0,64},{4,68},{8,72},{12,76},{16,80},{20,84},{24,88},{28,92},{32,9... | collective-permute-start | bytes 98312 | tf_op jit(solution)/shard_map/ppermute | solution.py:21
  7.1 7.1 %collective-permute-start.2 = (bf16[384,256]{1,0:T(8,128)(2,1)S(1)}, bf16[384,256]{1,0:T(8,128)(2,1)S(1)}, u32[]{:S(2)}, u32[]{:S(2)}) collective-permute-start(bf16[384,256]{1,0:T(8,128)(2,1)S(1)} %get-tuple-element.42.after.g34), channel_id=1, source_target_pairs={{0,8},{4,12},{8,0},{12,4},{16,24},{20,28},{24,16},{28,20},{32,40},... | collective-permute-start | bytes 589832 | tf_op jit(solution)/shard_map/ppermute | solution.py:21
  9.8 8.9 %collective-permute-start.5 = (bf16[384,256]{1,0:T(8,128)(2,1)S(1)}, bf16[384,256]{1,0:T(8,128)(2,1)S(1)}, u32[]{:S(2)}, u32[]{:S(2)}) collective-permute-start(bf16[384,256]{1,0:T(8,128)(2,1)S(1)} %get-tuple-element.54), channel_id=1, source_target_pairs={{0,16},{4,20},{8,24},{12,28},{16,0},{20,4},{24,8},{28,12},{32,48},... | collective-permute-start | bytes 589832 | tf_op jit(solution)/shard_map/ppermute | solution.py:21
  11.1 7.6 %collective-permute-start.6 = (bf16[128,256]{1,0:T(8,128)(2,1)S(1)}, bf16[128,256]{1,0:T(8,128)(2,1)S(1)}, u32[]{:S(2)}, u32[]{:S(2)}) collective-permute-start(bf16[128,256]{1,0:T(8,128)(2,1)S(1)} %get-tuple-element.48.after.u1), channel_id=1, source_target_pairs={{0,32},{4,36},{8,40},{12,44},{16,48},{20,52},{24,56},{28,60},{32,0... | collective-permute-start | bytes 196616 | tf_op jit(solution)/shard_map/ppermute | solution.py:21
  13.6 5.1 %collective-permute-start.7 = (bf16[128,256]{1,0:T(8,128)(2,1)S(1)}, bf16[128,256]{1,0:T(8,128)(2,1)S(1)}, u32[]{:S(2)}, u32[]{:S(2)}) collective-permute-start(bf16[128,256]{1,0:T(8,128)(2,1)S(1)} %get-tuple-element.48.after.u1), channel_id=1, source_target_pairs={{0,48},{4,52},{8,56},{12,60},{16,32},{20,36},{24,40},{28,44},{32,1... | collective-permute-start | bytes 196616 | tf_op jit(solution)/shard_map/ppermute | solution.py:21
  13.8 6.9 %collective-permute-start.4 = (bf16[512,256]{1,0:T(8,128)(2,1)S(1)}, bf16[512,256]{1,0:T(8,128)(2,1)S(1)}, u32[]{:S(2)}, u32[]{:S(2)}) collective-permute-start(bf16[512,256]{1,0:T(8,128)(2,1)S(1)} %get-tuple-element.53.g2), channel_id=1, source_target_pairs={{0,8},{4,12},{8,0},{12,4},{16,24},{20,28},{24,16},{28,20},{32,40},... | collective-permute-start | bytes 786440 | tf_op jit(solution)/shard_map/ppermute | solution.py:21
  14.2 8.9 %collective-permute-start.8 = (bf16[512,256]{1,0:T(8,128)(2,1)S(1)}, bf16[512,256]{1,0:T(8,128)(2,1)S(1)}, u32[]{:S(2)}, u32[]{:S(2)}) collective-permute-start(bf16[512,256]{1,0:T(8,128)(2,1)S(1)} %get-tuple-element.49.after), channel_id=1, source_target_pairs={{0,16},{4,20},{8,24},{12,28},{16,0},{20,4},{24,8},{28,12},{32,48},... | collective-permute-start | bytes 786440 | tf_op jit(solution)/shard_map/ppermute | solution.py:21
  18.7 8.4 %collective-permute-start.11 = (bf16[512,256]{1,0:T(8,128)(2,1)S(1)}, bf16[512,256]{1,0:T(8,128)(2,1)S(1)}, u32[]{:S(2)}, u32[]{:S(2)}) collective-permute-start(bf16[512,256]{1,0:T(8,128)(2,1)S(1)} %shard_map.62.after), channel_id=1, source_target_pairs={{0,8},{4,12},{8,0},{12,4},{16,24},{20,28},{24,16},{28,20},{32,40},... | collective-permute-start | bytes 786440 | tf_op jit(solution)/shard_map/ppermute | solution.py:21
  18.8 5.4 %collective-permute-start.10 = (bf16[256,256]{1,0:T(8,128)(2,1)S(1)}, bf16[256,256]{1,0:T(8,128)(2,1)S(1)}, u32[]{:S(2)}, u32[]{:S(2)}) collective-permute-start(bf16[256,256]{1,0:T(8,128)(2,1)S(1)} %get-tuple-element.62), channel_id=1, source_target_pairs={{0,48},{4,52},{8,56},{12,60},{16,32},{20,36},{24,40},{28,44},{32,1... | collective-permute-start | bytes 393224 | tf_op jit(solution)/shard_map/ppermute | solution.py:21
  19.5 7.6 %collective-permute-start.9 = (bf16[256,256]{1,0:T(8,128)(2,1)S(1)}, bf16[256,256]{1,0:T(8,128)(2,1)S(1)}, u32[]{:S(2)}, u32[]{:S(2)}) collective-permute-start(bf16[256,256]{1,0:T(8,128)(2,1)S(1)} %get-tuple-element.62), channel_id=1, source_target_pairs={{0,32},{4,36},{8,40},{12,44},{16,48},{20,52},{24,56},{28,60},{32,0... | collective-permute-start | bytes 393224 | tf_op jit(solution)/shard_map/ppermute | solution.py:21
  27.1 4.9 %copy-start = (bf16[512,2048]{1,0:T(8,128)(2,1)S(1)}, bf16[512,2048]{1,0:T(8,128)(2,1)}, u32[]{:S(2)}) copy-start(bf16[512,2048]{1,0:T(8,128)(2,1)} %w.5) | copy-start | bytes 6291460
  28.5 4.7 %collective-permute-start.12 = (bf16[512,256]{1,0:T(8,128)(2,1)S(1)}, bf16[512,256]{1,0:T(8,128)(2,1)S(1)}, u32[]{:S(2)}, u32[]{:S(2)}) collective-permute-start(bf16[512,256]{1,0:T(8,128)(2,1)S(1)} %get-tuple-element.65.after), channel_id=1, source_target_pairs={{0,4},{4,0},{8,12},{12,8},{16,20},{20,16},{24,28},{28,24},{32,36},... | collective-permute-start | bytes 786440 | tf_op jit(solution)/shard_map/ppermute | solution.py:21
  34.0 18.4 %collective-permute-start.17 = (bf16[256,512]{1,0:T(8,128)(2,1)S(1)}, bf16[256,512]{1,0:T(8,128)(2,1)S(1)}, u32[]{:S(2)}, u32[]{:S(2)}) collective-permute-start(bf16[256,512]{1,0:T(8,128)(2,1)S(1)} %get-tuple-element.74), channel_id=1, source_target_pairs={{0,3},{1,2},{2,1},{3,0},{4,7},{5,6},{6,5},{7,4},{8,11},{9,10},{10,... | collective-permute-start | bytes 786440 | tf_op jit(solution)/shard_map/ppermute | solution.py:25
  39.3 15.2 %collective-permute-start.14 = (bf16[256,512]{1,0:T(8,128)(2,1)S(1)}, bf16[256,512]{1,0:T(8,128)(2,1)S(1)}, u32[]{:S(2)}, u32[]{:S(2)}) collective-permute-start(bf16[256,512]{1,0:T(8,128)(2,1)S(1)} %get-tuple-element.68.after), channel_id=1, source_target_pairs={{0,1},{1,0},{2,3},{3,2},{4,5},{5,4},{6,7},{7,6},{8,9},{9,8},{10,11... | collective-permute-start | bytes 786440 | tf_op jit(solution)/shard_map/ppermute | solution.py:25
  42.0 25.8 %collective-permute-start.13 = (bf16[256,512]{1,0:T(8,128)(2,1)S(1)}, bf16[256,512]{1,0:T(8,128)(2,1)S(1)}, u32[]{:S(2)}, u32[]{:S(2)}) collective-permute-start(bf16[256,512]{1,0:T(8,128)(2,1)S(1)} %get-tuple-element.70), channel_id=1, source_target_pairs={{0,1},{1,0},{2,3},{3,2},{4,5},{5,4},{6,7},{7,6},{8,9},{9,8},{10,11... | collective-permute-start | bytes 786440 | tf_op jit(solution)/shard_map/ppermute | solution.py:25
  43.3 24.5 %collective-permute-start.16 = (bf16[256,512]{1,0:T(8,128)(2,1)S(1)}, bf16[256,512]{1,0:T(8,128)(2,1)S(1)}, u32[]{:S(2)}, u32[]{:S(2)}) collective-permute-start(bf16[256,512]{1,0:T(8,128)(2,1)S(1)} %get-tuple-element.72), channel_id=1, source_target_pairs={{0,3},{1,2},{2,1},{3,0},{4,7},{5,6},{6,5},{7,4},{8,11},{9,10},{10,... | collective-permute-start | bytes 786440 | tf_op jit(solution)/shard_map/ppermute | solution.py:25
  52.4 23.6 %collective-permute-start.18 = (bf16[256,512]{1,0:T(8,128)(2,1)S(1)}, bf16[256,512]{1,0:T(8,128)(2,1)S(1)}, u32[]{:S(2)}, u32[]{:S(2)}) collective-permute-start(bf16[256,512]{1,0:T(8,128)(2,1)S(1)} %shard_map.70), channel_id=1, source_target_pairs={{0,1},{1,0},{2,3},{3,2},{4,5},{5,4},{6,7},{7,6},{8,9},{9,8},{10,11... | collective-permute-start | bytes 786440 | tf_op jit(solution)/shard_map/ppermute | solution.py:25
  54.5 21.6 %collective-permute-start.15 = (bf16[256,512]{1,0:T(8,128)(2,1)S(1)}, bf16[256,512]{1,0:T(8,128)(2,1)S(1)}, u32[]{:S(2)}, u32[]{:S(2)}) collective-permute-start(bf16[256,512]{1,0:T(8,128)(2,1)S(1)} %shard_map.69), channel_id=1, source_target_pairs={{0,3},{1,2},{2,1},{3,0},{4,7},{5,6},{6,5},{7,4},{8,11},{9,10},{10,... | collective-permute-start | bytes 786440 | tf_op jit(solution)/shard_map/ppermute | solution.py:25

commit v5 on v4

--- a/solution.py
+++ b/solution.py
@@ -69,10 +69,18 @@
         buf[base + j, there, :] = theirs[:, cols].astype(F32)
 
 
-def pick_kernel(pos, offs, mkv, rkv, g34, g2, g5, buf):
+def pick_kernel(pos, offs, mkv, rkv, g34, g5, buf):
     for i in range(2):
         fill(buf, 2 * i, pos, mkv.at[i], rkv.at[i])
-    for level, dst, row in ((5, g5, 0), (3, g34, 0), (4, g34, 256), (2, g2, 0)):
+    pick(pos, offs, buf, ((5, g5, 0), (3, g34, 0), (4, g34, 256)))
+
+
+def second_kernel(pos, offs, buf, g2):
+    pick(pos, offs, buf, ((2, g2, 0),))
+
+
+def pick(pos, offs, buf, places):
+    for level, dst, row in places:
         n = CHIP >> level
         for j in range(2):
             rows = used(offs[level, pos[1] + j], level)
@@ -178,12 +186,10 @@
     return jnp.concatenate([x[:, HD:] for x in blocks], axis=0)
 
 
-def near_kernel(pos, offs, acc0, peak0, total0, mq, mkv, rq, rkv, g2, z2, after, acc, peak, total, bq, buf):
+def near_kernel(pos, offs, acc0, peak0, total0, mq, rq, kv, g2, z2, after, acc, peak, total, bq, buf):
     del acc0, peak0, total0, after
     state = (acc, peak, total)
     fill(buf, 0, pos, mq, rq)
-    for i in range(2):
-        fill(buf, 2 + 2 * i, pos, mkv.at[i], rkv.at[i])
     row = 0
     for level in (5, 4, 3):
         n = CHIP >> level
@@ -192,7 +198,8 @@
             row += n
     for j in range(2):
         off = offs[1, pos[1] + j]
-        qs, ks, vs = (buf[2 * i + j, used(off, 1), :].astype(BF16) for i in range(3))
+        refs = (buf.at[j], kv.at[j], kv.at[2 + j])
+        qs, ks, vs = (x[used(off, 1), :].astype(BF16) for x in refs)
         parts = softmax_parts(causal_scores(qs, ks), [vs[:256], vs])
         for half, part in enumerate(parts):
             merge(state, j, used(off, 1, half * 256, 256), part)
@@ -353,13 +360,13 @@
     )
     rq = swap(oq, CORE)
     states = [((2, CHIP, HD), F32)] * 3
-    g34, g2, g5 = call(
+    g34, g5, kv = call(
         pick_kernel,
         (pos, offsets),
         (mkv, rkv),
-        [rows(384), rows(512), rows(64)],
-        [pltpu.VMEM((4, CHIP, HD), F32)],
-    )
+        [rows(384), rows(64), ((4, CHIP, HD), F32)],
+    )
+    g2 = call(second_kernel, (pos, offsets), (kv,), [rows(512)])[0]
     y5, zb, z2 = swap(g5, Y1), swap(g34, Z), swap(g2, Z)
     state = call(other_tile_kernel, (pos,), (rq, rkv), states, flops=2 * unit, unread=(g34,))
     u0, u1 = call(mix_kernel, (), (g5, y5, g34), [rows(384), rows(128)], unread=(state[0],))
@@ -374,9 +381,9 @@
     *state, bq = call(
         near_kernel,
         (pos, offsets),
-        (*state, mq, mkv, rq, rkv, g2, z2),
+        (*state, mq, rq, kv, g2, z2),
         states + [((448, HD), BF16)],
-        [pltpu.VMEM((6, CHIP, HD), F32)],
+        [pltpu.VMEM((2, CHIP, HD), F32)],
         flops=3 * unit,
         unread=(x5,),
         inplace=3,

time: 77.2 us -> 76.8 us (level)
  waiting for transfers between devices: 34.8 us -> 33.8 us
    ppermute x13, waiting for transfers between devices: 6.22 us -> 4.73 us  [swap(): return lax.ppermute(block, 'ctx', [(i, i ^ bits) for i in range(64)])]
    pallas_call x17 -> x18, Pallas kernels: 15.5 us -> 16 us  [call(): pl.pallas_call(kernel, in_specs=[SMEM] * len(scalars) + [inside] * len(ar...]
  transfers between devices with their start and end apart: 19 -> 19, of which waited for: 8 -> 9; matrix products, arithmetic and copies ran while one was open for 0% -> 0% of each run, Pallas kernels for 15% -> 15%
where the time goes in v5:
time: 76.8 us; the launch traced here: 76.7 us
  waiting for transfers between devices  33.8 us (44%)
  starting transfers between devices  26.4 us (34%)
  Pallas kernels  16 us (21%)
    ppermute x6, waiting for transfers between devices, cross(): return lax.ppermute(block, 'head', [(i, i ^ bits) for i in range(4)])  29.1 us
    pallas_call x18, Pallas kernels, call(): pl.pallas_call(kernel, in_specs=[SMEM] * len(scalars) + [inside] * len(ar...  16 us
    ppermute x13, starting transfers between devices, swap(): return lax.ppermute(block, 'ctx', [(i, i ^ bits) for i in range(64)])  15.2 us
    ppermute x6, starting transfers between devices, cross(): return lax.ppermute(block, 'head', [(i, i ^ bits) for i in range(4)])  11.2 us
    ppermute x13, waiting for transfers between devices, swap(): return lax.ppermute(block, 'ctx', [(i, i ^ bits) for i in range(64)])  4.73 us
  transfers between devices with their start and end apart: 19, of which 9 were waited for; matrix products, arithmetic and copies ran while one was open for 0% of the time, Pallas kernels for 15%

profile of v5, /device:TPU:1, one launch (start us, length us, event | category | flops | bytes accessed | tf_op | source)
XLA Modules:
  0.0 76.7 jit_solution(3341085784899720125)
XLA Ops:
  0.0 0.0 copy-start.1
  0.0 1.1 %shard_map.55.after = bf16[2,512,256]{2,1,0:T(8,128)(2,1)S(1)} custom-call(bf16[512,512]{1,0:T(8,128)(2,1)} %k.3, bf16[512,512]{1,0:T(8,128)(2,1)} %v.3), custom_call_target="tpu_custom_call" | custom-call | bytes 1048576 | tf_op jit(solution)/shard_map/pallas_call | solution.py:325
  1.1 3.3 %collective-permute-start.1 = (bf16[2,512,256]{2,1,0:T(8,128)(2,1)S(1)}, bf16[2,512,256]{2,1,0:T(8,128)(2,1)S(1)}, u32[]{:S(2)}, u32[]{:S(2)}) collective-permute-start(bf16[2,512,256]{2,1,0:T(8,128)(2,1)S(1)} %shard_map.55.after), channel_id=1, source_target_pairs={{0,4},{4,0},{8,12},{12,8},{16,20},{20,16},{24,28},{28,24},{32,36},... | collective-permute-start | bytes 1572872 | tf_op jit(solution)/shard_map/ppermute | solution.py:21
  4.4 1.2 %shard_map.56 = (bf16[512,256]{1,0:T(8,128)(2,1)S(1)}, bf16[2,512,256]{2,1,0:T(8,128)(2,1)S(1)}, bf16[512,256]{1,0:T(8,128)(2,1)S(1)}) custom-call(bf16[512,512]{1,0:T(8,128)(2,1)} %q.1, bf16[512,512]{1,0:T(8,128)(2,1)} %k.3, bf16[512,512]{1,0:T(8,128)(2,1)} %v.3, bf16[2,512,256]{2,1,0:T(8,128)(2,1)S(1)} %shard_map.55.after), custom_call_target="tpu_custom_call" | custom-call | bytes 1572864 | tf_op jit(solution)/shard_map/pallas_call | solution.py:325
  5.6 0.1 collective-permute-start
  5.7 0.1 pad_add_fusion.pos
  5.8 0.1 collective-permute-done.1.rkv.kv
  5.9 0.0 copy-done.1
  5.9 0.9 %shard_map.57 = (bf16[384,256]{1,0:T(8,128)(2,1)S(1)}, bf16[64,256]{1,0:T(8,128)(2,1)S(1)}, f32[4,1024,128]{2,1,0:T(8,128)S(1)}) custom-call(s32[4]{0:T(128)S(1)} %pad_add_fusion.pos, s32[6,16]{1,0:T(8,128)S(1)} %copy-done.1, bf16[2,512,256]{2,1,0:T(8,128)(2,1)S(1)} %get-tuple-element.41.mkv.kv, bf16[2,512,256]{2,1,0:T(8,128)(2,1)S(1)} %collective-permute-done.1.rkv.kv), custom_call_target="tpu_custom_call" | custom-call | bytes 1048576 | tf_op jit(solution)/shard_map/pallas_call | solution.py:325
  6.9 0.1 collective-permute-start.3
  7.0 1.2 %collective-permute-start.2 = (bf16[384,256]{1,0:T(8,128)(2,1)S(1)}, bf16[384,256]{1,0:T(8,128)(2,1)S(1)}, u32[]{:S(2)}, u32[]{:S(2)}) collective-permute-start(bf16[384,256]{1,0:T(8,128)(2,1)S(1)} %get-tuple-element.42.after.g34), channel_id=1, source_target_pairs={{0,8},{4,12},{8,0},{12,4},{16,24},{20,28},{24,16},{28,20},{32,40},... | collective-permute-start | bytes 589832 | tf_op jit(solution)/shard_map/ppermute | solution.py:21
  8.2 0.0 collective-permute-done.q.rq
  8.2 1.5 %shard_map.58 = (f32[2,1024,128]{2,1,0:T(8,128)S(1)}, f32[2,1024,128]{2,1,0:T(8,128)S(1)}, f32[2,1024,128]{2,1,0:T(8,128)S(1)}) custom-call(s32[4]{0:T(128)S(1)} %pad_add_fusion.pos, bf16[512,256]{1,0:T(8,128)(2,1)S(1)} %collective-permute-done.q.rq, bf16[2,512,256]{2,1,0:T(8,128)(2,1)S(1)} %collective-permute-done.1.rkv.kv, ...), custom_call_target="tpu_custom_call" | custom-call | flops 268435456 | bytes 786432 | tf_op jit(solution)/shard_map/pallas_call | solution.py:325
  9.7 0.0 collective-permute-done.3.y5
  9.8 1.3 %collective-permute-start.5 = (bf16[384,256]{1,0:T(8,128)(2,1)S(1)}, bf16[384,256]{1,0:T(8,128)(2,1)S(1)}, u32[]{:S(2)}, u32[]{:S(2)}) collective-permute-start(bf16[384,256]{1,0:T(8,128)(2,1)S(1)} %get-tuple-element.54), channel_id=1, source_target_pairs={{0,16},{4,20},{8,24},{12,28},{16,0},{20,4},{24,8},{28,12},{32,48},... | collective-permute-start | bytes 589832 | tf_op jit(solution)/shard_map/ppermute | solution.py:21
  11.0 2.5 %collective-permute-start.6 = (bf16[128,256]{1,0:T(8,128)(2,1)S(1)}, bf16[128,256]{1,0:T(8,128)(2,1)S(1)}, u32[]{:S(2)}, u32[]{:S(2)}) collective-permute-start(bf16[128,256]{1,0:T(8,128)(2,1)S(1)} %get-tuple-element.48.after.u1), channel_id=1, source_target_pairs={{0,32},{4,36},{8,40},{12,44},{16,48},{20,52},{24,56},{28,60},{32,0... | collective-permute-start | bytes 196616 | tf_op jit(solution)/shard_map/ppermute | solution.py:21
  13.5 0.2 collective-permute-start.7
  13.7 0.7 shard_map.62.g2
  14.4 0.4 collective-permute-start.4
  14.8 0.0 collective-permute-done.2.zb
  14.9 0.1 collective-permute-start.8
  15.0 1.5 %shard_map.61 = (f32[2,1024,128]{2,1,0:T(8,128)S(1)}, f32[2,1024,128]{2,1,0:T(8,128)S(1)}, f32[2,1024,128]{2,1,0:T(8,128)S(1)}) custom-call(s32[4]{0:T(128)S(1)} %pad_add_fusion.pos, f32[2,1024,128]{2,1,0:T(8,128)S(1)} %get-tuple-element.43.after.acc0, ...), custom_call_target="tpu_custom_call", output_to_operand_aliasing={{0}: (1, {}), {1}: (2, {}), {2}: (3, {})} | custom-call | flops 268435456 | bytes 3932160 | tf_op jit(solution)/shard_map/pallas_call | solution.py:325
  16.5 2.1 %collective-permute-done.6.a1 = bf16[128,256]{1,0:T(8,128)(2,1)S(1)} collective-permute-done((bf16[128,256]{1,0:T(8,128)(2,1)S(1)}, bf16[128,256]{1,0:T(8,128)(2,1)S(1)}, u32[]{:S(2)}, u32[]{:S(2)}) %collective-permute-start.6) | collective-permute-done | bytes 65568 | tf_op jit(solution)/shard_map/ppermute | solution.py:21
  18.6 0.0 collective-permute-done.7.a2
  18.6 0.0 collective-permute-done.5.a0
  18.6 0.1 collective-permute-start.11
  18.7 1.5 %collective-permute-start.10 = (bf16[256,256]{1,0:T(8,128)(2,1)S(1)}, bf16[256,256]{1,0:T(8,128)(2,1)S(1)}, u32[]{:S(2)}, u32[]{:S(2)}) collective-permute-start(bf16[256,256]{1,0:T(8,128)(2,1)S(1)} %get-tuple-element.62), channel_id=1, source_target_pairs={{0,48},{4,52},{8,56},{12,60},{16,32},{20,36},{24,40},{28,44},{32,1... | collective-permute-start | bytes 393224 | tf_op jit(solution)/shard_map/ppermute | solution.py:21
  20.2 1.2 %collective-permute-start.9 = (bf16[256,256]{1,0:T(8,128)(2,1)S(1)}, bf16[256,256]{1,0:T(8,128)(2,1)S(1)}, u32[]{:S(2)}, u32[]{:S(2)}) collective-permute-start(bf16[256,256]{1,0:T(8,128)(2,1)S(1)} %get-tuple-element.62), channel_id=1, source_target_pairs={{0,32},{4,36},{8,40},{12,44},{16,48},{20,52},{24,56},{28,60},{32,0... | collective-permute-start | bytes 393224 | tf_op jit(solution)/shard_map/ppermute | solution.py:21
  21.4 0.0 collective-permute-done.4.z2
  21.4 2.3 %shard_map.64 = (f32[2,1024,128]{2,1,0:T(8,128)S(1)}, f32[2,1024,128]{2,1,0:T(8,128)S(1)}, f32[2,1024,128]{2,1,0:T(8,128)S(1)}, bf16[448,128]{1,0:T(8,128)(2,1)S(1)}) custom-call(s32[4]{0:T(128)S(1)} %pad_add_fusion.pos, s32[6,16]{1,0:T(8,128)S(1)} %copy-done.1, ...), custom_call_target="tpu_custom_call", output_to_operand_aliasing={{0}: (2, {}), {1}: (3, {}), {2}: (4, {})} | custom-call | flops 402653184 | bytes 6291456 | tf_op jit(solution)/shard_map/pallas_call | solution.py:325
  23.7 0.0 collective-permute-done.8.h1
  23.7 1.2 %shard_map.65 = (f32[2,1024,128]{2,1,0:T(8,128)S(1)}, f32[2,1024,128]{2,1,0:T(8,128)S(1)}, f32[2,1024,128]{2,1,0:T(8,128)S(1)}) custom-call(s32[4]{0:T(128)S(1)} %pad_add_fusion.pos, s32[6,16]{1,0:T(8,128)S(1)} %copy-done.1, f32[2,1024,128]{2,1,0:T(8,128)S(1)} %get-tuple-element.55.acc0, ...), custom_call_target="tpu_custom_call", output_to_operand_aliasing={{0}: (2, {}), {1}: (3, {}), {2}: (4, {})} | custom-call | flops 67108864 | bytes 4112384 | tf_op jit(solution)/shard_map/pallas_call | solution.py:325
  24.8 0.0 collective-permute-done.10.h3
  24.9 2.1 %collective-permute-done.9.h2 = bf16[256,256]{1,0:T(8,128)(2,1)S(1)} collective-permute-done((bf16[256,256]{1,0:T(8,128)(2,1)S(1)}, bf16[256,256]{1,0:T(8,128)(2,1)S(1)}, u32[]{:S(2)}, u32[]{:S(2)}) %collective-permute-start.9) | collective-permute-done | bytes 131104 | tf_op jit(solution)/shard_map/ppermute | solution.py:21
  27.0 0.0 collective-permute-done.11.e
  27.0 0.0 copy-start
  27.0 1.4 %shard_map.66 = (f32[2,1024,128]{2,1,0:T(8,128)S(1)}, f32[2,1024,128]{2,1,0:T(8,128)S(1)}, f32[2,1024,128]{2,1,0:T(8,128)S(1)}, bf16[512,256]{1,0:T(8,128)(2,1)S(1)}) custom-call(s32[4]{0:T(128)S(1)} %pad_add_fusion.pos, s32[6,16]{1,0:T(8,128)S(1)} %copy-done.1, ...), custom_call_target="tpu_custom_call", output_to_operand_aliasing={{0}: (2, {}), {1}: (3, {}), {2}: (4, {})} | custom-call | flops 134217728 | bytes 4833280 | tf_op jit(solution)/shard_map/pallas_call | solution.py:325
  28.4 3.3 %collective-permute-start.12 = (bf16[512,256]{1,0:T(8,128)(2,1)S(1)}, bf16[512,256]{1,0:T(8,128)(2,1)S(1)}, u32[]{:S(2)}, u32[]{:S(2)}) collective-permute-start(bf16[512,256]{1,0:T(8,128)(2,1)S(1)} %get-tuple-element.65.after), channel_id=1, source_target_pairs={{0,4},{4,0},{8,12},{12,8},{16,20},{20,16},{24,28},{28,24},{32,36},... | collective-permute-start | bytes 786440 | tf_op jit(solution)/shard_map/ppermute | solution.py:21
  31.6 0.0 copy-done
  31.6 0.8 %shard_map.67 = (bf16[512,256]{1,0:T(8,128)(2,1)S(1)}, f32[512,512]{1,0:T(8,128)S(1)}) custom-call(s32[4]{0:T(128)S(1)} %pad_add_fusion.pos, f32[2,1024,128]{2,1,0:T(8,128)S(1)} %get-tuple-element.63.acc, f32[2,1024,128]{2,1,0:T(8,128)S(1)} %get-tuple-element.64.total, bf16[512,2048]{1,0:T(8,128)(2,1)S(1)} %copy-done, ...), custom_call_target="tpu_custom_call" | custom-call | flops 134217728 | bytes 4194304 | tf_op jit(solution)/shard_map/pallas_call | solution.py:325
  32.5 0.3 collective-permute-done.12.back
  32.8 0.8 %shard_map.68 = (bf16[256,512]{1,0:T(8,128)(2,1)S(1)}, bf16[256,512]{1,0:T(8,128)(2,1)S(1)}) custom-call(s32[4]{0:T(128)S(1)} %pad_add_fusion.pos, f32[512,512]{1,0:T(8,128)S(1)} %get-tuple-element.67.part, bf16[512,256]{1,0:T(8,128)(2,1)S(1)} %collective-permute-done.12.back, bf16[512,2048]{1,0:T(8,128)(2,1)S(1)} %copy-done), custom_call_target="tpu_custom_call" | custom-call | flops 134217728 | bytes 3407872 | tf_op jit(solution)/shard_map/pallas_call | solution.py:325
  33.7 5.4 %collective-permute-start.17 = (bf16[256,512]{1,0:T(8,128)(2,1)S(1)}, bf16[256,512]{1,0:T(8,128)(2,1)S(1)}, u32[]{:S(2)}, u32[]{:S(2)}) collective-permute-start(bf16[256,512]{1,0:T(8,128)(2,1)S(1)} %get-tuple-element.74), channel_id=1, source_target_pairs={{0,3},{1,2},{2,1},{3,0},{4,7},{5,6},{6,5},{7,4},{8,11},{9,10},{10,... | collective-permute-start | bytes 786440 | tf_op jit(solution)/shard_map/ppermute | solution.py:25
  39.1 1.2 %collective-permute-start.14 = (bf16[256,512]{1,0:T(8,128)(2,1)S(1)}, bf16[256,512]{1,0:T(8,128)(2,1)S(1)}, u32[]{:S(2)}, u32[]{:S(2)}) collective-permute-start(bf16[256,512]{1,0:T(8,128)(2,1)S(1)} %get-tuple-element.68.after), channel_id=1, source_target_pairs={{0,1},{1,0},{2,3},{3,2},{4,5},{5,4},{6,7},{7,6},{8,9},{9,8},{10,11... | collective-permute-start | bytes 786440 | tf_op jit(solution)/shard_map/ppermute | solution.py:25
  40.3 1.5 %shard_map.69 = (bf16[256,512]{1,0:T(8,128)(2,1)S(1)}, bf16[256,512]{1,0:T(8,128)(2,1)S(1)}, f32[256,512]{1,0:T(8,128)S(1)}, f32[256,512]{1,0:T(8,128)S(1)}, f32[512,512]{1,0:T(8,128)S(1)}) custom-call(s32[4]{0:T(128)S(1)} %pad_add_fusion.pos, bf16[512,256]{1,0:T(8,128)(2,1)S(1)} %get-tuple-element.66.mine, ...), custom_call_target="tpu_custom_call" | custom-call | flops 805306368 | bytes 2621440 | tf_op jit(solution)/shard_map/pallas_call | solution.py:325
  41.8 1.3 %collective-permute-start.13 = (bf16[256,512]{1,0:T(8,128)(2,1)S(1)}, bf16[256,512]{1,0:T(8,128)(2,1)S(1)}, u32[]{:S(2)}, u32[]{:S(2)}) collective-permute-start(bf16[256,512]{1,0:T(8,128)(2,1)S(1)} %get-tuple-element.70), channel_id=1, source_target_pairs={{0,1},{1,0},{2,3},{3,2},{4,5},{5,4},{6,7},{7,6},{8,9},{9,8},{10,11... | collective-permute-start | bytes 786440 | tf_op jit(solution)/shard_map/ppermute | solution.py:25
  43.1 0.1 collective-permute-start.16
  43.2 9.6 %collective-permute-done.17.came = bf16[256,512]{1,0:T(8,128)(2,1)S(1)} collective-permute-done((bf16[256,512]{1,0:T(8,128)(2,1)S(1)}, bf16[256,512]{1,0:T(8,128)(2,1)S(1)}, u32[]{:S(2)}, u32[]{:S(2)}) %collective-permute-start.17) | collective-permute-done | bytes 262176 | tf_op jit(solution)/shard_map/ppermute | solution.py:25
  52.8 0.1 shard_map.71
  52.8 1.5 %collective-permute-start.18 = (bf16[256,512]{1,0:T(8,128)(2,1)S(1)}, bf16[256,512]{1,0:T(8,128)(2,1)S(1)}, u32[]{:S(2)}, u32[]{:S(2)}) collective-permute-start(bf16[256,512]{1,0:T(8,128)(2,1)S(1)} %shard_map.71), channel_id=1, source_target_pairs={{0,1},{1,0},{2,3},{3,2},{4,5},{5,4},{6,7},{7,6},{8,9},{9,8},{10,11... | collective-permute-start | bytes 786440 | tf_op jit(solution)/shard_map/ppermute | solution.py:25
  54.3 1.4 %collective-permute-done.14.came = bf16[256,512]{1,0:T(8,128)(2,1)S(1)} collective-permute-done((bf16[256,512]{1,0:T(8,128)(2,1)S(1)}, bf16[256,512]{1,0:T(8,128)(2,1)S(1)}, u32[]{:S(2)}, u32[]{:S(2)}) %collective-permute-start.14) | collective-permute-done | bytes 262176 | tf_op jit(solution)/shard_map/ppermute | solution.py:25
  55.7 1.8 %collective-permute-start.15 = (bf16[256,512]{1,0:T(8,128)(2,1)S(1)}, bf16[256,512]{1,0:T(8,128)(2,1)S(1)}, u32[]{:S(2)}, u32[]{:S(2)}) collective-permute-start(bf16[256,512]{1,0:T(8,128)(2,1)S(1)} %shard_map.70), channel_id=1, source_target_pairs={{0,3},{1,2},{2,1},{3,0},{4,7},{5,6},{6,5},{7,4},{8,11},{9,10},{10,... | collective-permute-start | bytes 786440 | tf_op jit(solution)/shard_map/ppermute | solution.py:25
  57.5 10.1 %collective-permute-done.13.up2 = bf16[256,512]{1,0:T(8,128)(2,1)S(1)} collective-permute-done((bf16[256,512]{1,0:T(8,128)(2,1)S(1)}, bf16[256,512]{1,0:T(8,128)(2,1)S(1)}, u32[]{:S(2)}, u32[]{:S(2)}) %collective-permute-start.13) | collective-permute-done | bytes 262176 | tf_op jit(solution)/shard_map/ppermute | solution.py:25
  67.6 0.0 collective-permute-done.16.down2
  67.6 5.8 %collective-permute-done.18.down3 = bf16[256,512]{1,0:T(8,128)(2,1)S(1)} collective-permute-done((bf16[256,512]{1,0:T(8,128)(2,1)S(1)}, bf16[256,512]{1,0:T(8,128)(2,1)S(1)}, u32[]{:S(2)}, u32[]{:S(2)}) %collective-permute-start.18) | collective-permute-done | bytes 262176 | tf_op jit(solution)/shard_map/ppermute | solution.py:25
  73.4 2.3 %collective-permute-done.15.up3 = bf16[256,512]{1,0:T(8,128)(2,1)S(1)} collective-permute-done((bf16[256,512]{1,0:T(8,128)(2,1)S(1)}, bf16[256,512]{1,0:T(8,128)(2,1)S(1)}, u32[]{:S(2)}, u32[]{:S(2)}) %collective-permute-start.15) | collective-permute-done | bytes 262176 | tf_op jit(solution)/shard_map/ppermute | solution.py:25
  75.6 0.9 %shard_map.72 = bf16[512,512]{1,0:T(8,128)(2,1)} custom-call(f32[512,512]{1,0:T(8,128)S(1)} %get-tuple-element.69.own, bf16[256,512]{1,0:T(8,128)(2,1)S(1)} %collective-permute-done.13.up2, bf16[256,512]{1,0:T(8,128)(2,1)S(1)} %collective-permute-done.15.up3, bf16[256,512]{1,0:T(8,128)(2,1)S(1)} %collective-permute-done.16.down2, ...), custom_call_target="tpu_custom_call" | custom-call | bytes 2097152 | tf_op jit(solution)/shard_map/pallas_call | solution.py:325
  (4 shorter events, 0.1 us)
Async XLA Ops:
  0.0 5.9 %copy-start.1 = (s32[6,16]{1,0:T(8,128)S(1)}, s32[6,16]{1,0:T(8,128)}, u32[]{:S(2)}) copy-start(s32[6,16]{1,0:T(8,128)} %offs.9) | copy-start | bytes 1156
  1.1 4.9 %collective-permute-start.1 = (bf16[2,512,256]{2,1,0:T(8,128)(2,1)S(1)}, bf16[2,512,256]{2,1,0:T(8,128)(2,1)S(1)}, u32[]{:S(2)}, u32[]{:S(2)}) collective-permute-start(bf16[2,512,256]{2,1,0:T(8,128)(2,1)S(1)} %shard_map.55.after), channel_id=1, source_target_pairs={{0,4},{4,0},{8,12},{12,8},{16,20},{20,16},{24,28},{28,24},{32,36},... | collective-permute-start | bytes 1572872 | tf_op jit(solution)/shard_map/ppermute | solution.py:21
  5.6 2.6 %collective-permute-start = (bf16[512,256]{1,0:T(8,128)(2,1)S(1)}, bf16[512,256]{1,0:T(8,128)(2,1)S(1)}, u32[]{:S(2)}, u32[]{:S(2)}) collective-permute-start(bf16[512,256]{1,0:T(8,128)(2,1)S(1)} %get-tuple-element.40), channel_id=1, source_target_pairs={{0,4},{4,0},{8,12},{12,8},{16,20},{20,16},{24,28},{28,24},{32,36},... | collective-permute-start | bytes 786440 | tf_op jit(solution)/shard_map/ppermute | solution.py:21
  6.9 2.9 %collective-permute-start.3 = (bf16[64,256]{1,0:T(8,128)(2,1)S(1)}, bf16[64,256]{1,0:T(8,128)(2,1)S(1)}, u32[]{:S(2)}, u32[]{:S(2)}) collective-permute-start(bf16[64,256]{1,0:T(8,128)(2,1)S(1)} %get-tuple-element.47.g5), channel_id=1, source_target_pairs={{0,64},{4,68},{8,72},{12,76},{16,80},{20,84},{24,88},{28,92},{32,9... | collective-permute-start | bytes 98312 | tf_op jit(solution)/shard_map/ppermute | solution.py:21
  7.0 7.9 %collective-permute-start.2 = (bf16[384,256]{1,0:T(8,128)(2,1)S(1)}, bf16[384,256]{1,0:T(8,128)(2,1)S(1)}, u32[]{:S(2)}, u32[]{:S(2)}) collective-permute-start(bf16[384,256]{1,0:T(8,128)(2,1)S(1)} %get-tuple-element.42.after.g34), channel_id=1, source_target_pairs={{0,8},{4,12},{8,0},{12,4},{16,24},{20,28},{24,16},{28,20},{32,40},... | collective-permute-start | bytes 589832 | tf_op jit(solution)/shard_map/ppermute | solution.py:21
  9.8 8.9 %collective-permute-start.5 = (bf16[384,256]{1,0:T(8,128)(2,1)S(1)}, bf16[384,256]{1,0:T(8,128)(2,1)S(1)}, u32[]{:S(2)}, u32[]{:S(2)}) collective-permute-start(bf16[384,256]{1,0:T(8,128)(2,1)S(1)} %get-tuple-element.54), channel_id=1, source_target_pairs={{0,16},{4,20},{8,24},{12,28},{16,0},{20,4},{24,8},{28,12},{32,48},... | collective-permute-start | bytes 589832 | tf_op jit(solution)/shard_map/ppermute | solution.py:21
  11.0 7.6 %collective-permute-start.6 = (bf16[128,256]{1,0:T(8,128)(2,1)S(1)}, bf16[128,256]{1,0:T(8,128)(2,1)S(1)}, u32[]{:S(2)}, u32[]{:S(2)}) collective-permute-start(bf16[128,256]{1,0:T(8,128)(2,1)S(1)} %get-tuple-element.48.after.u1), channel_id=1, source_target_pairs={{0,32},{4,36},{8,40},{12,44},{16,48},{20,52},{24,56},{28,60},{32,0... | collective-permute-start | bytes 196616 | tf_op jit(solution)/shard_map/ppermute | solution.py:21
  13.5 5.1 %collective-permute-start.7 = (bf16[128,256]{1,0:T(8,128)(2,1)S(1)}, bf16[128,256]{1,0:T(8,128)(2,1)S(1)}, u32[]{:S(2)}, u32[]{:S(2)}) collective-permute-start(bf16[128,256]{1,0:T(8,128)(2,1)S(1)} %get-tuple-element.48.after.u1), channel_id=1, source_target_pairs={{0,48},{4,52},{8,56},{12,60},{16,32},{20,36},{24,40},{28,44},{32,1... | collective-permute-start | bytes 196616 | tf_op jit(solution)/shard_map/ppermute | solution.py:21
  14.4 7.0 %collective-permute-start.4 = (bf16[512,256]{1,0:T(8,128)(2,1)S(1)}, bf16[512,256]{1,0:T(8,128)(2,1)S(1)}, u32[]{:S(2)}, u32[]{:S(2)}) collective-permute-start(bf16[512,256]{1,0:T(8,128)(2,1)S(1)} %shard_map.62.g2), channel_id=1, source_target_pairs={{0,8},{4,12},{8,0},{12,4},{16,24},{20,28},{24,16},{28,20},{32,40},... | collective-permute-start | bytes 786440 | tf_op jit(solution)/shard_map/ppermute | solution.py:21
  14.9 8.8 %collective-permute-start.8 = (bf16[512,256]{1,0:T(8,128)(2,1)S(1)}, bf16[512,256]{1,0:T(8,128)(2,1)S(1)}, u32[]{:S(2)}, u32[]{:S(2)}) collective-permute-start(bf16[512,256]{1,0:T(8,128)(2,1)S(1)} %get-tuple-element.49.after), channel_id=1, source_target_pairs={{0,16},{4,20},{8,24},{12,28},{16,0},{20,4},{24,8},{28,12},{32,48},... | collective-permute-start | bytes 786440 | tf_op jit(solution)/shard_map/ppermute | solution.py:21
  18.6 8.3 %collective-permute-start.11 = (bf16[512,256]{1,0:T(8,128)(2,1)S(1)}, bf16[512,256]{1,0:T(8,128)(2,1)S(1)}, u32[]{:S(2)}, u32[]{:S(2)}) collective-permute-start(bf16[512,256]{1,0:T(8,128)(2,1)S(1)} %shard_map.63.after), channel_id=1, source_target_pairs={{0,8},{4,12},{8,0},{12,4},{16,24},{20,28},{24,16},{28,20},{32,40},... | collective-permute-start | bytes 786440 | tf_op jit(solution)/shard_map/ppermute | solution.py:21
  18.7 6.1 %collective-permute-start.10 = (bf16[256,256]{1,0:T(8,128)(2,1)S(1)}, bf16[256,256]{1,0:T(8,128)(2,1)S(1)}, u32[]{:S(2)}, u32[]{:S(2)}) collective-permute-start(bf16[256,256]{1,0:T(8,128)(2,1)S(1)} %get-tuple-element.62), channel_id=1, source_target_pairs={{0,48},{4,52},{8,56},{12,60},{16,32},{20,36},{24,40},{28,44},{32,1... | collective-permute-start | bytes 393224 | tf_op jit(solution)/shard_map/ppermute | solution.py:21
  20.2 6.8 %collective-permute-start.9 = (bf16[256,256]{1,0:T(8,128)(2,1)S(1)}, bf16[256,256]{1,0:T(8,128)(2,1)S(1)}, u32[]{:S(2)}, u32[]{:S(2)}) collective-permute-start(bf16[256,256]{1,0:T(8,128)(2,1)S(1)} %get-tuple-element.62), channel_id=1, source_target_pairs={{0,32},{4,36},{8,40},{12,44},{16,48},{20,52},{24,56},{28,60},{32,0... | collective-permute-start | bytes 393224 | tf_op jit(solution)/shard_map/ppermute | solution.py:21
  27.0 4.7 %copy-start = (bf16[512,2048]{1,0:T(8,128)(2,1)S(1)}, bf16[512,2048]{1,0:T(8,128)(2,1)}, u32[]{:S(2)}) copy-start(bf16[512,2048]{1,0:T(8,128)(2,1)} %w.5) | copy-start | bytes 6291460
  28.4 4.4 %collective-permute-start.12 = (bf16[512,256]{1,0:T(8,128)(2,1)S(1)}, bf16[512,256]{1,0:T(8,128)(2,1)S(1)}, u32[]{:S(2)}, u32[]{:S(2)}) collective-permute-start(bf16[512,256]{1,0:T(8,128)(2,1)S(1)} %get-tuple-element.65.after), channel_id=1, source_target_pairs={{0,4},{4,0},{8,12},{12,8},{16,20},{20,16},{24,28},{28,24},{32,36},... | collective-permute-start | bytes 786440 | tf_op jit(solution)/shard_map/ppermute | solution.py:21
  33.7 19.1 %collective-permute-start.17 = (bf16[256,512]{1,0:T(8,128)(2,1)S(1)}, bf16[256,512]{1,0:T(8,128)(2,1)S(1)}, u32[]{:S(2)}, u32[]{:S(2)}) collective-permute-start(bf16[256,512]{1,0:T(8,128)(2,1)S(1)} %get-tuple-element.74), channel_id=1, source_target_pairs={{0,3},{1,2},{2,1},{3,0},{4,7},{5,6},{6,5},{7,4},{8,11},{9,10},{10,... | collective-permute-start | bytes 786440 | tf_op jit(solution)/shard_map/ppermute | solution.py:25
  39.1 16.6 %collective-permute-start.14 = (bf16[256,512]{1,0:T(8,128)(2,1)S(1)}, bf16[256,512]{1,0:T(8,128)(2,1)S(1)}, u32[]{:S(2)}, u32[]{:S(2)}) collective-permute-start(bf16[256,512]{1,0:T(8,128)(2,1)S(1)} %get-tuple-element.68.after), channel_id=1, source_target_pairs={{0,1},{1,0},{2,3},{3,2},{4,5},{5,4},{6,7},{7,6},{8,9},{9,8},{10,11... | collective-permute-start | bytes 786440 | tf_op jit(solution)/shard_map/ppermute | solution.py:25
  41.8 25.8 %collective-permute-start.13 = (bf16[256,512]{1,0:T(8,128)(2,1)S(1)}, bf16[256,512]{1,0:T(8,128)(2,1)S(1)}, u32[]{:S(2)}, u32[]{:S(2)}) collective-permute-start(bf16[256,512]{1,0:T(8,128)(2,1)S(1)} %get-tuple-element.70), channel_id=1, source_target_pairs={{0,1},{1,0},{2,3},{3,2},{4,5},{5,4},{6,7},{7,6},{8,9},{9,8},{10,11... | collective-permute-start | bytes 786440 | tf_op jit(solution)/shard_map/ppermute | solution.py:25
  43.1 24.5 %collective-permute-start.16 = (bf16[256,512]{1,0:T(8,128)(2,1)S(1)}, bf16[256,512]{1,0:T(8,128)(2,1)S(1)}, u32[]{:S(2)}, u32[]{:S(2)}) collective-permute-start(bf16[256,512]{1,0:T(8,128)(2,1)S(1)} %get-tuple-element.72), channel_id=1, source_target_pairs={{0,3},{1,2},{2,1},{3,0},{4,7},{5,6},{6,5},{7,4},{8,11},{9,10},{10,... | collective-permute-start | bytes 786440 | tf_op jit(solution)/shard_map/ppermute | solution.py:25
  52.8 20.6 %collective-permute-start.18 = (bf16[256,512]{1,0:T(8,128)(2,1)S(1)}, bf16[256,512]{1,0:T(8,128)(2,1)S(1)}, u32[]{:S(2)}, u32[]{:S(2)}) collective-permute-start(bf16[256,512]{1,0:T(8,128)(2,1)S(1)} %shard_map.71), channel_id=1, source_target_pairs={{0,1},{1,0},{2,3},{3,2},{4,5},{5,4},{6,7},{7,6},{8,9},{9,8},{10,11... | collective-permute-start | bytes 786440 | tf_op jit(solution)/shard_map/ppermute | solution.py:25
  55.7 19.9 %collective-permute-start.15 = (bf16[256,512]{1,0:T(8,128)(2,1)S(1)}, bf16[256,512]{1,0:T(8,128)(2,1)S(1)}, u32[]{:S(2)}, u32[]{:S(2)}) collective-permute-start(bf16[256,512]{1,0:T(8,128)(2,1)S(1)} %shard_map.70), channel_id=1, source_target_pairs={{0,3},{1,2},{2,1},{3,0},{4,7},{5,6},{6,5},{7,4},{8,11},{9,10},{10,... | collective-permute-start | bytes 786440 | tf_op jit(solution)/shard_map/ppermute | solution.py:25

commit v6 on v5

--- a/solution.py
+++ b/solution.py
@@ -147,8 +147,8 @@
     tile(pos[0] * TOK, q, kv, state)
 
 
-def mix_kernel(g5, y5, g34, after, u0, u1):
-    del after
+def mix_kernel(g5, y5, g34, after, g2, u0, u1):
+    del after, g2
     for dst in (u0, u1):
         dst[:64, :] = g5[...]
         dst[64:128, :] = y5[...]
@@ -369,7 +369,7 @@
     g2 = call(second_kernel, (pos, offsets), (kv,), [rows(512)])[0]
     y5, zb, z2 = swap(g5, Y1), swap(g34, Z), swap(g2, Z)
     state = call(other_tile_kernel, (pos,), (rq, rkv), states, flops=2 * unit, unread=(g34,))
-    u0, u1 = call(mix_kernel, (), (g5, y5, g34), [rows(384), rows(128)], unread=(state[0],))
+    u0, u1 = call(mix_kernel, (), (g5, y5, g34), [rows(384), rows(128)], unread=(state[0], g2))
     a0, a1, a2 = swap(u0, X1), swap(u1, X2), swap(u1, X1 | X2)
     p1, p2 = call(pair_kernel, (), (g34, zb), [rows(512), rows(256)], unread=(u1,))
     h1, h2, h3 = swap(p1, X1), swap(p2, X2), swap(p2, X1 | X2)

time: 76.8 us -> 77.9 us (1.014)
  waiting for transfers between devices: 33.8 us -> 34.9 us
    ppermute x13, waiting for transfers between devices: 4.73 us -> 6.28 us  [swap(): return lax.ppermute(block, 'ctx', [(i, i ^ bits) for i in range(64)])]
  transfers between devices with their start and end apart: 19 -> 19, of which waited for: 9 -> 8; matrix products, arithmetic and copies ran while one was open for 0% -> 0% of each run, Pallas kernels for 15% -> 15%
where the time goes in v6:
time: 77.9 us; the launch traced here: 77.7 us
  waiting for transfers between devices  34.9 us (45%)
  starting transfers between devices  26.5 us (34%)
  Pallas kernels  16 us (21%)
    ppermute x6, waiting for transfers between devices, cross(): return lax.ppermute(block, 'head', [(i, i ^ bits) for i in range(4)])  28.6 us
    pallas_call x18, Pallas kernels, call(): pl.pallas_call(kernel, in_specs=[SMEM] * len(scalars) + [inside] * len(ar...  16 us
    ppermute x13, starting transfers between devices, swap(): return lax.ppermute(block, 'ctx', [(i, i ^ bits) for i in range(64)])  14.6 us
    ppermute x6, starting transfers between devices, cross(): return lax.ppermute(block, 'head', [(i, i ^ bits) for i in range(4)])  11.8 us
    ppermute x13, waiting for transfers between devices, swap(): return lax.ppermute(block, 'ctx', [(i, i ^ bits) for i in range(64)])  6.28 us
  transfers between devices with their start and end apart: 19, of which 8 were waited for; matrix products, arithmetic and copies ran while one was open for 0% of the time, Pallas kernels for 15%

profile of v6, /device:TPU:1, one launch (start us, length us, event | category | flops | bytes accessed | tf_op | source)
XLA Modules:
  0.0 77.7 jit_solution(13964135097864433582)
XLA Ops:
  0.0 0.0 copy-start.1
  0.0 1.1 %shard_map.55.after = bf16[2,512,256]{2,1,0:T(8,128)(2,1)S(1)} custom-call(bf16[512,512]{1,0:T(8,128)(2,1)} %k.3, bf16[512,512]{1,0:T(8,128)(2,1)} %v.3), custom_call_target="tpu_custom_call" | custom-call | bytes 1048576 | tf_op jit(solution)/shard_map/pallas_call | solution.py:325
  1.1 3.3 %collective-permute-start.1 = (bf16[2,512,256]{2,1,0:T(8,128)(2,1)S(1)}, bf16[2,512,256]{2,1,0:T(8,128)(2,1)S(1)}, u32[]{:S(2)}, u32[]{:S(2)}) collective-permute-start(bf16[2,512,256]{2,1,0:T(8,128)(2,1)S(1)} %shard_map.55.after), channel_id=1, source_target_pairs={{0,4},{4,0},{8,12},{12,8},{16,20},{20,16},{24,28},{28,24},{32,36},... | collective-permute-start | bytes 1572872 | tf_op jit(solution)/shard_map/ppermute | solution.py:21
  4.4 1.2 %shard_map.56 = (bf16[512,256]{1,0:T(8,128)(2,1)S(1)}, bf16[2,512,256]{2,1,0:T(8,128)(2,1)S(1)}, bf16[512,256]{1,0:T(8,128)(2,1)S(1)}) custom-call(bf16[512,512]{1,0:T(8,128)(2,1)} %q.1, bf16[512,512]{1,0:T(8,128)(2,1)} %k.3, bf16[512,512]{1,0:T(8,128)(2,1)} %v.3, bf16[2,512,256]{2,1,0:T(8,128)(2,1)S(1)} %shard_map.55.after), custom_call_target="tpu_custom_call" | custom-call | bytes 1572864 | tf_op jit(solution)/shard_map/pallas_call | solution.py:325
  5.6 0.1 collective-permute-start
  5.7 0.1 pad_add_fusion.pos
  5.8 0.1 collective-permute-done.1.rkv.kv
  5.9 0.0 copy-done.1
  5.9 0.9 %shard_map.57 = (bf16[384,256]{1,0:T(8,128)(2,1)S(1)}, bf16[64,256]{1,0:T(8,128)(2,1)S(1)}, f32[4,1024,128]{2,1,0:T(8,128)S(1)}) custom-call(s32[4]{0:T(128)S(1)} %pad_add_fusion.pos, s32[6,16]{1,0:T(8,128)S(1)} %copy-done.1, bf16[2,512,256]{2,1,0:T(8,128)(2,1)S(1)} %get-tuple-element.41.mkv.kv, bf16[2,512,256]{2,1,0:T(8,128)(2,1)S(1)} %collective-permute-done.1.rkv.kv), custom_call_target="tpu_custom_call" | custom-call | bytes 1048576 | tf_op jit(solution)/shard_map/pallas_call | solution.py:325
  6.9 0.1 collective-permute-start.3
  7.0 1.2 %collective-permute-start.2 = (bf16[384,256]{1,0:T(8,128)(2,1)S(1)}, bf16[384,256]{1,0:T(8,128)(2,1)S(1)}, u32[]{:S(2)}, u32[]{:S(2)}) collective-permute-start(bf16[384,256]{1,0:T(8,128)(2,1)S(1)} %get-tuple-element.42.after.g34), channel_id=1, source_target_pairs={{0,8},{4,12},{8,0},{12,4},{16,24},{20,28},{24,16},{28,20},{32,40},... | collective-permute-start | bytes 589832 | tf_op jit(solution)/shard_map/ppermute | solution.py:21
  8.2 0.7 shard_map.59.g2
  8.9 0.0 collective-permute-done.q.rq
  8.9 1.5 %shard_map.58 = (f32[2,1024,128]{2,1,0:T(8,128)S(1)}, f32[2,1024,128]{2,1,0:T(8,128)S(1)}, f32[2,1024,128]{2,1,0:T(8,128)S(1)}) custom-call(s32[4]{0:T(128)S(1)} %pad_add_fusion.pos, bf16[512,256]{1,0:T(8,128)(2,1)S(1)} %collective-permute-done.q.rq, bf16[2,512,256]{2,1,0:T(8,128)(2,1)S(1)} %collective-permute-done.1.rkv.kv, ...), custom_call_target="tpu_custom_call" | custom-call | flops 268435456 | bytes 786432 | tf_op jit(solution)/shard_map/pallas_call | solution.py:325
  10.4 0.0 collective-permute-done.3.y5
  10.5 1.3 %collective-permute-start.5 = (bf16[384,256]{1,0:T(8,128)(2,1)S(1)}, bf16[384,256]{1,0:T(8,128)(2,1)S(1)}, u32[]{:S(2)}, u32[]{:S(2)}) collective-permute-start(bf16[384,256]{1,0:T(8,128)(2,1)S(1)} %get-tuple-element.54), channel_id=1, source_target_pairs={{0,16},{4,20},{8,24},{12,28},{16,0},{20,4},{24,8},{28,12},{32,48},... | collective-permute-start | bytes 589832 | tf_op jit(solution)/shard_map/ppermute | solution.py:21
  11.7 2.5 %collective-permute-start.6 = (bf16[128,256]{1,0:T(8,128)(2,1)S(1)}, bf16[128,256]{1,0:T(8,128)(2,1)S(1)}, u32[]{:S(2)}, u32[]{:S(2)}) collective-permute-start(bf16[128,256]{1,0:T(8,128)(2,1)S(1)} %get-tuple-element.49.after.u1), channel_id=1, source_target_pairs={{0,32},{4,36},{8,40},{12,44},{16,48},{20,52},{24,56},{28,60},{32,0... | collective-permute-start | bytes 196616 | tf_op jit(solution)/shard_map/ppermute | solution.py:21
  14.2 0.2 collective-permute-start.7
  14.4 0.4 collective-permute-start.4
  14.8 0.0 collective-permute-done.2.zb
  14.8 0.1 collective-permute-start.8
  14.9 1.5 %shard_map.62 = (f32[2,1024,128]{2,1,0:T(8,128)S(1)}, f32[2,1024,128]{2,1,0:T(8,128)S(1)}, f32[2,1024,128]{2,1,0:T(8,128)S(1)}) custom-call(s32[4]{0:T(128)S(1)} %pad_add_fusion.pos, f32[2,1024,128]{2,1,0:T(8,128)S(1)} %get-tuple-element.43.after.acc0, ...), custom_call_target="tpu_custom_call", output_to_operand_aliasing={{0}: (1, {}), {1}: (2, {}), {2}: (3, {})} | custom-call | flops 268435456 | bytes 3932160 | tf_op jit(solution)/shard_map/pallas_call | solution.py:325
  16.4 2.9 %collective-permute-done.6.a1 = bf16[128,256]{1,0:T(8,128)(2,1)S(1)} collective-permute-done((bf16[128,256]{1,0:T(8,128)(2,1)S(1)}, bf16[128,256]{1,0:T(8,128)(2,1)S(1)}, u32[]{:S(2)}, u32[]{:S(2)}) %collective-permute-start.6) | collective-permute-done | bytes 65568 | tf_op jit(solution)/shard_map/ppermute | solution.py:21
  19.3 0.0 collective-permute-done.7.a2
  19.3 0.0 collective-permute-done.5.a0
  19.4 0.3 collective-permute-start.11
  19.6 0.7 collective-permute-start.10
  20.3 1.1 %collective-permute-start.9 = (bf16[256,256]{1,0:T(8,128)(2,1)S(1)}, bf16[256,256]{1,0:T(8,128)(2,1)S(1)}, u32[]{:S(2)}, u32[]{:S(2)}) collective-permute-start(bf16[256,256]{1,0:T(8,128)(2,1)S(1)} %get-tuple-element.62), channel_id=1, source_target_pairs={{0,32},{4,36},{8,40},{12,44},{16,48},{20,52},{24,56},{28,60},{32,0... | collective-permute-start | bytes 393224 | tf_op jit(solution)/shard_map/ppermute | solution.py:21
  21.4 0.0 collective-permute-done.4.z2
  21.4 2.3 %shard_map.64 = (f32[2,1024,128]{2,1,0:T(8,128)S(1)}, f32[2,1024,128]{2,1,0:T(8,128)S(1)}, f32[2,1024,128]{2,1,0:T(8,128)S(1)}, bf16[448,128]{1,0:T(8,128)(2,1)S(1)}) custom-call(s32[4]{0:T(128)S(1)} %pad_add_fusion.pos, s32[6,16]{1,0:T(8,128)S(1)} %copy-done.1, ...), custom_call_target="tpu_custom_call", output_to_operand_aliasing={{0}: (2, {}), {1}: (3, {}), {2}: (4, {})} | custom-call | flops 402653184 | bytes 6291456 | tf_op jit(solution)/shard_map/pallas_call | solution.py:325
  23.7 0.0 collective-permute-done.8.h1
  23.7 1.2 %shard_map.65 = (f32[2,1024,128]{2,1,0:T(8,128)S(1)}, f32[2,1024,128]{2,1,0:T(8,128)S(1)}, f32[2,1024,128]{2,1,0:T(8,128)S(1)}) custom-call(s32[4]{0:T(128)S(1)} %pad_add_fusion.pos, s32[6,16]{1,0:T(8,128)S(1)} %copy-done.1, f32[2,1024,128]{2,1,0:T(8,128)S(1)} %get-tuple-element.55.acc0, ...), custom_call_target="tpu_custom_call", output_to_operand_aliasing={{0}: (2, {}), {1}: (3, {}), {2}: (4, {})} | custom-call | flops 67108864 | bytes 4112384 | tf_op jit(solution)/shard_map/pallas_call | solution.py:325
  24.8 0.0 collective-permute-done.10.h3
  24.8 2.9 %collective-permute-done.9.h2 = bf16[256,256]{1,0:T(8,128)(2,1)S(1)} collective-permute-done((bf16[256,256]{1,0:T(8,128)(2,1)S(1)}, bf16[256,256]{1,0:T(8,128)(2,1)S(1)}, u32[]{:S(2)}, u32[]{:S(2)}) %collective-permute-start.9) | collective-permute-done | bytes 131104 | tf_op jit(solution)/shard_map/ppermute | solution.py:21
  27.8 0.0 collective-permute-done.11.e
  27.8 0.0 copy-start
  27.8 1.4 %shard_map.66 = (f32[2,1024,128]{2,1,0:T(8,128)S(1)}, f32[2,1024,128]{2,1,0:T(8,128)S(1)}, f32[2,1024,128]{2,1,0:T(8,128)S(1)}, bf16[512,256]{1,0:T(8,128)(2,1)S(1)}) custom-call(s32[4]{0:T(128)S(1)} %pad_add_fusion.pos, s32[6,16]{1,0:T(8,128)S(1)} %copy-done.1, ...), custom_call_target="tpu_custom_call", output_to_operand_aliasing={{0}: (2, {}), {1}: (3, {}), {2}: (4, {})} | custom-call | flops 134217728 | bytes 4833280 | tf_op jit(solution)/shard_map/pallas_call | solution.py:325
  29.1 3.5 %collective-permute-start.12 = (bf16[512,256]{1,0:T(8,128)(2,1)S(1)}, bf16[512,256]{1,0:T(8,128)(2,1)S(1)}, u32[]{:S(2)}, u32[]{:S(2)}) collective-permute-start(bf16[512,256]{1,0:T(8,128)(2,1)S(1)} %get-tuple-element.65.after), channel_id=1, source_target_pairs={{0,4},{4,0},{8,12},{12,8},{16,20},{20,16},{24,28},{28,24},{32,36},... | collective-permute-start | bytes 786440 | tf_op jit(solution)/shard_map/ppermute | solution.py:21
  32.6 0.0 copy-done
  32.6 0.9 %shard_map.67 = (bf16[512,256]{1,0:T(8,128)(2,1)S(1)}, f32[512,512]{1,0:T(8,128)S(1)}) custom-call(s32[4]{0:T(128)S(1)} %pad_add_fusion.pos, f32[2,1024,128]{2,1,0:T(8,128)S(1)} %get-tuple-element.63.acc, f32[2,1024,128]{2,1,0:T(8,128)S(1)} %get-tuple-element.64.total, bf16[512,2048]{1,0:T(8,128)(2,1)S(1)} %copy-done, ...), custom_call_target="tpu_custom_call" | custom-call | flops 134217728 | bytes 4194304 | tf_op jit(solution)/shard_map/pallas_call | solution.py:325
  33.5 0.3 collective-permute-done.12.back
  33.8 0.8 %shard_map.68 = (bf16[256,512]{1,0:T(8,128)(2,1)S(1)}, bf16[256,512]{1,0:T(8,128)(2,1)S(1)}) custom-call(s32[4]{0:T(128)S(1)} %pad_add_fusion.pos, f32[512,512]{1,0:T(8,128)S(1)} %get-tuple-element.67.part, bf16[512,256]{1,0:T(8,128)(2,1)S(1)} %collective-permute-done.12.back, bf16[512,2048]{1,0:T(8,128)(2,1)S(1)} %copy-done), custom_call_target="tpu_custom_call" | custom-call | flops 134217728 | bytes 3407872 | tf_op jit(solution)/shard_map/pallas_call | solution.py:325
  34.7 5.2 %collective-permute-start.17 = (bf16[256,512]{1,0:T(8,128)(2,1)S(1)}, bf16[256,512]{1,0:T(8,128)(2,1)S(1)}, u32[]{:S(2)}, u32[]{:S(2)}) collective-permute-start(bf16[256,512]{1,0:T(8,128)(2,1)S(1)} %get-tuple-element.74), channel_id=1, source_target_pairs={{0,3},{1,2},{2,1},{3,0},{4,7},{5,6},{6,5},{7,4},{8,11},{9,10},{10,... | collective-permute-start | bytes 786440 | tf_op jit(solution)/shard_map/ppermute | solution.py:25
  39.9 1.2 %collective-permute-start.14 = (bf16[256,512]{1,0:T(8,128)(2,1)S(1)}, bf16[256,512]{1,0:T(8,128)(2,1)S(1)}, u32[]{:S(2)}, u32[]{:S(2)}) collective-permute-start(bf16[256,512]{1,0:T(8,128)(2,1)S(1)} %get-tuple-element.68.after), channel_id=1, source_target_pairs={{0,1},{1,0},{2,3},{3,2},{4,5},{5,4},{6,7},{7,6},{8,9},{9,8},{10,11... | collective-permute-start | bytes 786440 | tf_op jit(solution)/shard_map/ppermute | solution.py:25
  41.1 1.5 %shard_map.69 = (bf16[256,512]{1,0:T(8,128)(2,1)S(1)}, bf16[256,512]{1,0:T(8,128)(2,1)S(1)}, f32[256,512]{1,0:T(8,128)S(1)}, f32[256,512]{1,0:T(8,128)S(1)}, f32[512,512]{1,0:T(8,128)S(1)}) custom-call(s32[4]{0:T(128)S(1)} %pad_add_fusion.pos, bf16[512,256]{1,0:T(8,128)(2,1)S(1)} %get-tuple-element.66.mine, ...), custom_call_target="tpu_custom_call" | custom-call | flops 805306368 | bytes 2621440 | tf_op jit(solution)/shard_map/pallas_call | solution.py:325
  42.6 1.3 %collective-permute-start.13 = (bf16[256,512]{1,0:T(8,128)(2,1)S(1)}, bf16[256,512]{1,0:T(8,128)(2,1)S(1)}, u32[]{:S(2)}, u32[]{:S(2)}) collective-permute-start(bf16[256,512]{1,0:T(8,128)(2,1)S(1)} %get-tuple-element.70), channel_id=1, source_target_pairs={{0,1},{1,0},{2,3},{3,2},{4,5},{5,4},{6,7},{7,6},{8,9},{9,8},{10,11... | collective-permute-start | bytes 786440 | tf_op jit(solution)/shard_map/ppermute | solution.py:25
  43.9 0.1 collective-permute-start.16
  44.0 9.1 %collective-permute-done.17.came = bf16[256,512]{1,0:T(8,128)(2,1)S(1)} collective-permute-done((bf16[256,512]{1,0:T(8,128)(2,1)S(1)}, bf16[256,512]{1,0:T(8,128)(2,1)S(1)}, u32[]{:S(2)}, u32[]{:S(2)}) %collective-permute-start.17) | collective-permute-done | bytes 262176 | tf_op jit(solution)/shard_map/ppermute | solution.py:25
  53.1 0.1 shard_map.71
  53.1 0.9 %collective-permute-start.18 = (bf16[256,512]{1,0:T(8,128)(2,1)S(1)}, bf16[256,512]{1,0:T(8,128)(2,1)S(1)}, u32[]{:S(2)}, u32[]{:S(2)}) collective-permute-start(bf16[256,512]{1,0:T(8,128)(2,1)S(1)} %shard_map.71), channel_id=1, source_target_pairs={{0,1},{1,0},{2,3},{3,2},{4,5},{5,4},{6,7},{7,6},{8,9},{9,8},{10,11... | collective-permute-start | bytes 786440 | tf_op jit(solution)/shard_map/ppermute | solution.py:25
  54.0 1.1 %collective-permute-done.14.came = bf16[256,512]{1,0:T(8,128)(2,1)S(1)} collective-permute-done((bf16[256,512]{1,0:T(8,128)(2,1)S(1)}, bf16[256,512]{1,0:T(8,128)(2,1)S(1)}, u32[]{:S(2)}, u32[]{:S(2)}) %collective-permute-start.14) | collective-permute-done | bytes 262176 | tf_op jit(solution)/shard_map/ppermute | solution.py:25
  55.2 3.1 %collective-permute-start.15 = (bf16[256,512]{1,0:T(8,128)(2,1)S(1)}, bf16[256,512]{1,0:T(8,128)(2,1)S(1)}, u32[]{:S(2)}, u32[]{:S(2)}) collective-permute-start(bf16[256,512]{1,0:T(8,128)(2,1)S(1)} %shard_map.70), channel_id=1, source_target_pairs={{0,3},{1,2},{2,1},{3,0},{4,7},{5,6},{6,5},{7,4},{8,11},{9,10},{10,... | collective-permute-start | bytes 786440 | tf_op jit(solution)/shard_map/ppermute | solution.py:25
  58.3 10.1 %collective-permute-done.13.up2 = bf16[256,512]{1,0:T(8,128)(2,1)S(1)} collective-permute-done((bf16[256,512]{1,0:T(8,128)(2,1)S(1)}, bf16[256,512]{1,0:T(8,128)(2,1)S(1)}, u32[]{:S(2)}, u32[]{:S(2)}) %collective-permute-start.13) | collective-permute-done | bytes 262176 | tf_op jit(solution)/shard_map/ppermute | solution.py:25
  68.4 0.0 collective-permute-done.16.down2
  68.4 8.3 %collective-permute-done.18.down3 = bf16[256,512]{1,0:T(8,128)(2,1)S(1)} collective-permute-done((bf16[256,512]{1,0:T(8,128)(2,1)S(1)}, bf16[256,512]{1,0:T(8,128)(2,1)S(1)}, u32[]{:S(2)}, u32[]{:S(2)}) %collective-permute-start.18) | collective-permute-done | bytes 262176 | tf_op jit(solution)/shard_map/ppermute | solution.py:25
  76.7 0.0 collective-permute-done.15.up3
  76.7 0.9 %shard_map.72 = bf16[512,512]{1,0:T(8,128)(2,1)} custom-call(f32[512,512]{1,0:T(8,128)S(1)} %get-tuple-element.69.own, bf16[256,512]{1,0:T(8,128)(2,1)S(1)} %collective-permute-done.13.up2, bf16[256,512]{1,0:T(8,128)(2,1)S(1)} %collective-permute-done.15.up3, bf16[256,512]{1,0:T(8,128)(2,1)S(1)} %collective-permute-done.16.down2, ...), custom_call_target="tpu_custom_call" | custom-call | bytes 2097152 | tf_op jit(solution)/shard_map/pallas_call | solution.py:325
  (4 shorter events, 0.1 us)
Async XLA Ops:
  0.0 5.9 %copy-start.1 = (s32[6,16]{1,0:T(8,128)S(1)}, s32[6,16]{1,0:T(8,128)}, u32[]{:S(2)}) copy-start(s32[6,16]{1,0:T(8,128)} %offs.9) | copy-start | bytes 1156
  1.1 4.9 %collective-permute-start.1 = (bf16[2,512,256]{2,1,0:T(8,128)(2,1)S(1)}, bf16[2,512,256]{2,1,0:T(8,128)(2,1)S(1)}, u32[]{:S(2)}, u32[]{:S(2)}) collective-permute-start(bf16[2,512,256]{2,1,0:T(8,128)(2,1)S(1)} %shard_map.55.after), channel_id=1, source_target_pairs={{0,4},{4,0},{8,12},{12,8},{16,20},{20,16},{24,28},{28,24},{32,36},... | collective-permute-start | bytes 1572872 | tf_op jit(solution)/shard_map/ppermute | solution.py:21
  5.6 3.2 %collective-permute-start = (bf16[512,256]{1,0:T(8,128)(2,1)S(1)}, bf16[512,256]{1,0:T(8,128)(2,1)S(1)}, u32[]{:S(2)}, u32[]{:S(2)}) collective-permute-start(bf16[512,256]{1,0:T(8,128)(2,1)S(1)} %get-tuple-element.40), channel_id=1, source_target_pairs={{0,4},{4,0},{8,12},{12,8},{16,20},{20,16},{24,28},{28,24},{32,36},... | collective-permute-start | bytes 786440 | tf_op jit(solution)/shard_map/ppermute | solution.py:21
  6.9 3.5 %collective-permute-start.3 = (bf16[64,256]{1,0:T(8,128)(2,1)S(1)}, bf16[64,256]{1,0:T(8,128)(2,1)S(1)}, u32[]{:S(2)}, u32[]{:S(2)}) collective-permute-start(bf16[64,256]{1,0:T(8,128)(2,1)S(1)} %get-tuple-element.47.g5), channel_id=1, source_target_pairs={{0,64},{4,68},{8,72},{12,76},{16,80},{20,84},{24,88},{28,92},{32,9... | collective-permute-start | bytes 98312 | tf_op jit(solution)/shard_map/ppermute | solution.py:21
  7.0 7.8 %collective-permute-start.2 = (bf16[384,256]{1,0:T(8,128)(2,1)S(1)}, bf16[384,256]{1,0:T(8,128)(2,1)S(1)}, u32[]{:S(2)}, u32[]{:S(2)}) collective-permute-start(bf16[384,256]{1,0:T(8,128)(2,1)S(1)} %get-tuple-element.42.after.g34), channel_id=1, source_target_pairs={{0,8},{4,12},{8,0},{12,4},{16,24},{20,28},{24,16},{28,20},{32,40},... | collective-permute-start | bytes 589832 | tf_op jit(solution)/shard_map/ppermute | solution.py:21
  10.5 8.9 %collective-permute-start.5 = (bf16[384,256]{1,0:T(8,128)(2,1)S(1)}, bf16[384,256]{1,0:T(8,128)(2,1)S(1)}, u32[]{:S(2)}, u32[]{:S(2)}) collective-permute-start(bf16[384,256]{1,0:T(8,128)(2,1)S(1)} %get-tuple-element.54), channel_id=1, source_target_pairs={{0,16},{4,20},{8,24},{12,28},{16,0},{20,4},{24,8},{28,12},{32,48},... | collective-permute-start | bytes 589832 | tf_op jit(solution)/shard_map/ppermute | solution.py:21
  11.7 7.6 %collective-permute-start.6 = (bf16[128,256]{1,0:T(8,128)(2,1)S(1)}, bf16[128,256]{1,0:T(8,128)(2,1)S(1)}, u32[]{:S(2)}, u32[]{:S(2)}) collective-permute-start(bf16[128,256]{1,0:T(8,128)(2,1)S(1)} %get-tuple-element.49.after.u1), channel_id=1, source_target_pairs={{0,32},{4,36},{8,40},{12,44},{16,48},{20,52},{24,56},{28,60},{32,0... | collective-permute-start | bytes 196616 | tf_op jit(solution)/shard_map/ppermute | solution.py:21
  14.2 5.1 %collective-permute-start.7 = (bf16[128,256]{1,0:T(8,128)(2,1)S(1)}, bf16[128,256]{1,0:T(8,128)(2,1)S(1)}, u32[]{:S(2)}, u32[]{:S(2)}) collective-permute-start(bf16[128,256]{1,0:T(8,128)(2,1)S(1)} %get-tuple-element.49.after.u1), channel_id=1, source_target_pairs={{0,48},{4,52},{8,56},{12,60},{16,32},{20,36},{24,40},{28,44},{32,1... | collective-permute-start | bytes 196616 | tf_op jit(solution)/shard_map/ppermute | solution.py:21
  14.4 7.0 %collective-permute-start.4 = (bf16[512,256]{1,0:T(8,128)(2,1)S(1)}, bf16[512,256]{1,0:T(8,128)(2,1)S(1)}, u32[]{:S(2)}, u32[]{:S(2)}) collective-permute-start(bf16[512,256]{1,0:T(8,128)(2,1)S(1)} %shard_map.59.g2), channel_id=1, source_target_pairs={{0,8},{4,12},{8,0},{12,4},{16,24},{20,28},{24,16},{28,20},{32,40},... | collective-permute-start | bytes 786440 | tf_op jit(solution)/shard_map/ppermute | solution.py:21
  14.8 8.9 %collective-permute-start.8 = (bf16[512,256]{1,0:T(8,128)(2,1)S(1)}, bf16[512,256]{1,0:T(8,128)(2,1)S(1)}, u32[]{:S(2)}, u32[]{:S(2)}) collective-permute-start(bf16[512,256]{1,0:T(8,128)(2,1)S(1)} %get-tuple-element.50.after), channel_id=1, source_target_pairs={{0,16},{4,20},{8,24},{12,28},{16,0},{20,4},{24,8},{28,12},{32,48},... | collective-permute-start | bytes 786440 | tf_op jit(solution)/shard_map/ppermute | solution.py:21
  19.4 8.4 %collective-permute-start.11 = (bf16[512,256]{1,0:T(8,128)(2,1)S(1)}, bf16[512,256]{1,0:T(8,128)(2,1)S(1)}, u32[]{:S(2)}, u32[]{:S(2)}) collective-permute-start(bf16[512,256]{1,0:T(8,128)(2,1)S(1)} %shard_map.63.after), channel_id=1, source_target_pairs={{0,8},{4,12},{8,0},{12,4},{16,24},{20,28},{24,16},{28,20},{32,40},... | collective-permute-start | bytes 786440 | tf_op jit(solution)/shard_map/ppermute | solution.py:21
  19.6 5.2 %collective-permute-start.10 = (bf16[256,256]{1,0:T(8,128)(2,1)S(1)}, bf16[256,256]{1,0:T(8,128)(2,1)S(1)}, u32[]{:S(2)}, u32[]{:S(2)}) collective-permute-start(bf16[256,256]{1,0:T(8,128)(2,1)S(1)} %get-tuple-element.62), channel_id=1, source_target_pairs={{0,48},{4,52},{8,56},{12,60},{16,32},{20,36},{24,40},{28,44},{32,1... | collective-permute-start | bytes 393224 | tf_op jit(solution)/shard_map/ppermute | solution.py:21
  20.3 7.4 %collective-permute-start.9 = (bf16[256,256]{1,0:T(8,128)(2,1)S(1)}, bf16[256,256]{1,0:T(8,128)(2,1)S(1)}, u32[]{:S(2)}, u32[]{:S(2)}) collective-permute-start(bf16[256,256]{1,0:T(8,128)(2,1)S(1)} %get-tuple-element.62), channel_id=1, source_target_pairs={{0,32},{4,36},{8,40},{12,44},{16,48},{20,52},{24,56},{28,60},{32,0... | collective-permute-start | bytes 393224 | tf_op jit(solution)/shard_map/ppermute | solution.py:21
  27.8 4.9 %copy-start = (bf16[512,2048]{1,0:T(8,128)(2,1)S(1)}, bf16[512,2048]{1,0:T(8,128)(2,1)}, u32[]{:S(2)}) copy-start(bf16[512,2048]{1,0:T(8,128)(2,1)} %w.5) | copy-start | bytes 6291460
  29.1 4.7 %collective-permute-start.12 = (bf16[512,256]{1,0:T(8,128)(2,1)S(1)}, bf16[512,256]{1,0:T(8,128)(2,1)S(1)}, u32[]{:S(2)}, u32[]{:S(2)}) collective-permute-start(bf16[512,256]{1,0:T(8,128)(2,1)S(1)} %get-tuple-element.65.after), channel_id=1, source_target_pairs={{0,4},{4,0},{8,12},{12,8},{16,20},{20,16},{24,28},{28,24},{32,36},... | collective-permute-start | bytes 786440 | tf_op jit(solution)/shard_map/ppermute | solution.py:21
  34.7 18.4 %collective-permute-start.17 = (bf16[256,512]{1,0:T(8,128)(2,1)S(1)}, bf16[256,512]{1,0:T(8,128)(2,1)S(1)}, u32[]{:S(2)}, u32[]{:S(2)}) collective-permute-start(bf16[256,512]{1,0:T(8,128)(2,1)S(1)} %get-tuple-element.74), channel_id=1, source_target_pairs={{0,3},{1,2},{2,1},{3,0},{4,7},{5,6},{6,5},{7,4},{8,11},{9,10},{10,... | collective-permute-start | bytes 786440 | tf_op jit(solution)/shard_map/ppermute | solution.py:25
  39.9 15.3 %collective-permute-start.14 = (bf16[256,512]{1,0:T(8,128)(2,1)S(1)}, bf16[256,512]{1,0:T(8,128)(2,1)S(1)}, u32[]{:S(2)}, u32[]{:S(2)}) collective-permute-start(bf16[256,512]{1,0:T(8,128)(2,1)S(1)} %get-tuple-element.68.after), channel_id=1, source_target_pairs={{0,1},{1,0},{2,3},{3,2},{4,5},{5,4},{6,7},{7,6},{8,9},{9,8},{10,11... | collective-permute-start | bytes 786440 | tf_op jit(solution)/shard_map/ppermute | solution.py:25
  42.6 25.8 %collective-permute-start.13 = (bf16[256,512]{1,0:T(8,128)(2,1)S(1)}, bf16[256,512]{1,0:T(8,128)(2,1)S(1)}, u32[]{:S(2)}, u32[]{:S(2)}) collective-permute-start(bf16[256,512]{1,0:T(8,128)(2,1)S(1)} %get-tuple-element.70), channel_id=1, source_target_pairs={{0,1},{1,0},{2,3},{3,2},{4,5},{5,4},{6,7},{7,6},{8,9},{9,8},{10,11... | collective-permute-start | bytes 786440 | tf_op jit(solution)/shard_map/ppermute | solution.py:25
  43.9 24.5 %collective-permute-start.16 = (bf16[256,512]{1,0:T(8,128)(2,1)S(1)}, bf16[256,512]{1,0:T(8,128)(2,1)S(1)}, u32[]{:S(2)}, u32[]{:S(2)}) collective-permute-start(bf16[256,512]{1,0:T(8,128)(2,1)S(1)} %get-tuple-element.72), channel_id=1, source_target_pairs={{0,3},{1,2},{2,1},{3,0},{4,7},{5,6},{6,5},{7,4},{8,11},{9,10},{10,... | collective-permute-start | bytes 786440 | tf_op jit(solution)/shard_map/ppermute | solution.py:25
  53.1 23.6 %collective-permute-start.18 = (bf16[256,512]{1,0:T(8,128)(2,1)S(1)}, bf16[256,512]{1,0:T(8,128)(2,1)S(1)}, u32[]{:S(2)}, u32[]{:S(2)}) collective-permute-start(bf16[256,512]{1,0:T(8,128)(2,1)S(1)} %shard_map.71), channel_id=1, source_target_pairs={{0,1},{1,0},{2,3},{3,2},{4,5},{5,4},{6,7},{7,6},{8,9},{9,8},{10,11... | collective-permute-start | bytes 786440 | tf_op jit(solution)/shard_map/ppermute | solution.py:25
  55.2 21.5 %collective-permute-start.15 = (bf16[256,512]{1,0:T(8,128)(2,1)S(1)}, bf16[256,512]{1,0:T(8,128)(2,1)S(1)}, u32[]{:S(2)}, u32[]{:S(2)}) collective-permute-start(bf16[256,512]{1,0:T(8,128)(2,1)S(1)} %shard_map.70), channel_id=1, source_target_pairs={{0,3},{1,2},{2,1},{3,0},{4,7},{5,6},{6,5},{7,4},{8,11},{9,10},{10,... | collective-permute-start | bytes 786440 | tf_op jit(solution)/shard_map/ppermute | solution.py:25
